TPU v7x, 32 devices: a whole 2x2x4 slice. The times are simulated.
32 devices in a mesh: dp: 2 (over core), row: 4 (over z), col: 4 (over y, x).
Axes of the slice: x: 2, y: 2, z: 4, core: 2. Of those that a mesh axis runs over, the one named last changes fastest.
Arguments:
- inputs: bfloat16 [1024, 8192], P(('dp', 'row'), 'col'), may hold values from -6 to 6
- w_up: bfloat16 [8192, 16384], P('col', 'row'), may hold values from -0.1875 to 0.1875
- mask_up: int32 [32, 64], replicated, may hold values 0 or 1
- w_down: bfloat16 [16384, 8192], P('row', 'col'), may hold values from -0.125 to 0.125
- mask_down: int32 [64, 32], replicated, may hold values 0 or 1
- threshold: float32 [16384], P('row'), may hold values from 0.4 to 1.6
- cotangent: bfloat16 [1024, 8192], P(('dp', 'row'), 'col'), may hold values from -6 to 6
Outputs:
- output: bfloat16 [1024, 8192], P(('dp', 'row'), 'col')
- input_grad: bfloat16 [1024, 8192], P(('dp', 'row'), 'col')
- up_grad: bfloat16 [8192, 16384], P('col', 'row')
- down_grad: bfloat16 [16384, 8192], P('row', 'col')
Inputs may be any that keep to these rules, and one draw needn't show every extreme that they name: `mask_up`: 1 keeps a block, 0 zeroes it. `mask_down`: 1 keeps a block, 0 zeroes it.
All inputs are finite; a program needn't handle non-finite values.
Results may differ from a plain program's by a relative error of at most 0.0049.
Values may be sent and summed in bfloat16 or wider, within the bound.
No kernel may reach another device: no remote copies, remote signals or barrier semaphores. Data moves between devices by JAX's collectives and lax.ppermute only.
A program may use at most 256 MiB of HBM per device.

v0:
```python
import jax
import jax.numpy as jnp
from jax import lax
from jax.sharding import PartitionSpec as P

BLOCK = 256
STEPS = 4


spike_width = 1.0


def masked(weight, mask, first_place, second_place):
    rows_b = weight.shape[0] // BLOCK
    cols_b = weight.shape[1] // BLOCK
    window = lax.dynamic_slice(
        mask, (first_place * rows_b, second_place * cols_b), (rows_b, cols_b)
    )
    shaped = (
        weight.reshape(rows_b, BLOCK, cols_b, BLOCK) * window.astype(weight.dtype)[:, None, :, None]
    )
    return shaped.reshape(weight.shape)


def spiking(current, theta):
    membrane = jnp.zeros((current.shape[0], current.shape[2]), jnp.float32)
    volts = []
    spikes = []
    for step in range(STEPS):
        volt = membrane + current[:, step]
        spike = jnp.clip((volt - theta) / spike_width + 0.5, 0.0, 1.0)
        membrane = volt - theta * spike
        volts.append(volt)
        spikes.append(spike)
    return (jnp.stack(volts, 1), jnp.stack(spikes, 1))


def surrogate_back(grad_hidden, current, volts, spikes, theta):
    carry = jnp.zeros((current.shape[0], current.shape[2]), jnp.float32)
    grads = [None] * STEPS
    for step in range(STEPS - 1, -1, -1):
        offset = 2.0 * (volts[:, step] - theta) / spike_width
        gamma = 1.0 / (spike_width * (1.0 + offset * offset))
        dvolt = carry * (1.0 - theta * gamma) + grad_hidden[:, step] * current[:, step] * gamma
        grads[step] = dvolt + grad_hidden[:, step] * spikes[:, step]
        carry = dvolt
    return jnp.stack(grads, 1)


def contract_rows(left, right):
    return lax.dot_general(
        left, right, (((0,), (0,)), ((), ())), preferred_element_type=jnp.float32
    )


def contract_cols(left, right):
    return lax.dot_general(
        left, right, (((1,), (1,)), ((), ())), preferred_element_type=jnp.float32
    )


def per_device(inputs, w_up, mask_up, w_down, mask_down, threshold, cotangent):
    row_place = lax.axis_index("row")
    col_place = lax.axis_index("col")
    up_masked = masked(w_up, mask_up, col_place, row_place)
    down_masked = masked(w_down, mask_down, row_place, col_place)
    x_all = lax.all_gather(inputs, "row", axis=0, tiled=True)
    local_rows = x_all.shape[0] // lax.axis_size("col")
    current = lax.psum_scatter(
        jnp.dot(x_all, up_masked, preferred_element_type=jnp.float32),
        "col",
        scatter_dimension=0,
        tiled=True,
    )
    cur3 = current.reshape(local_rows // STEPS, STEPS, current.shape[1])
    volts, spikes = spiking(cur3, threshold)
    hidden = (spikes * cur3).astype(jnp.bfloat16).reshape(current.shape)
    hidden_all = lax.all_gather(hidden, "col", axis=0, tiled=True)
    out_terms = jnp.dot(hidden_all, down_masked, preferred_element_type=jnp.float32)
    output = lax.psum_scatter(out_terms, "row", scatter_dimension=0, tiled=True).astype(
        jnp.bfloat16
    )
    grad_all = lax.all_gather(cotangent, "row", axis=0, tiled=True)
    down_full = contract_rows(hidden_all, grad_all)
    down_local = masked(down_full, mask_down, row_place, col_place)
    down_total = lax.psum(down_local, "dp")
    hidden_grad = lax.psum_scatter(
        contract_cols(grad_all, down_masked), "col", scatter_dimension=0, tiled=True
    )
    current_grad = surrogate_back(hidden_grad.reshape(cur3.shape), cur3, volts, spikes, threshold)
    current_grad = current_grad.astype(jnp.bfloat16).reshape(current.shape)
    current_all = lax.all_gather(current_grad, "col", axis=0, tiled=True)
    up_local = masked(contract_rows(x_all, current_all), mask_up, col_place, row_place)
    up_total = lax.psum(up_local, "dp")
    input_terms = contract_cols(current_all, up_masked)
    input_grad = lax.psum_scatter(input_terms, "row", scatter_dimension=0, tiled=True).astype(
        jnp.bfloat16
    )
    return (output, input_grad, up_total.astype(jnp.bfloat16), down_total.astype(jnp.bfloat16))


def solution(mesh):
    in_specs = (
        P(("dp", "row"), "col"),
        P("col", "row"),
        P(),
        P("row", "col"),
        P(),
        P("row"),
        P(("dp", "row"), "col"),
    )
    out_specs = (P(("dp", "row"), "col"), P(("dp", "row"), "col"), P("col", "row"), P("row", "col"))
    return jax.shard_map(
        per_device, mesh=mesh, in_specs=in_specs, out_specs=out_specs, check_vma=False
    )
```

profile of v0, /device:TPU:0, one launch (start us, length us, event | category | flops | bytes accessed | tf_op | source)
XLA Modules:
  0.0 709.4 jit_solution(5849177476364023548)
XLA Ops:
  7.2 0.0 all-gather.9.cloned.1.call-start
  7.2 0.7 all-gather.9.cloned.1.call-update
  7.9 0.0 all-gather.5.cloned.1.call-start
  7.9 0.7 all-gather.5.cloned.1.call-update
  8.7 0.0 reduce-scatter.9.cloned.1.call-start
  8.7 0.8 dynamic-slice_convert_fusion
  9.5 0.1 copy.29
  9.6 1.7 mul.258
  11.3 9.6 %copy.48 = bf16[512,8,8,256]{3,1,2,0:T(8,128)(2,1)} copy(bf16[512,8,8,256]{3,2,1,0:T(8,128)(2,1)S(1)} %bitcast.35) | data formatting | bytes 33554432
  20.9 37.3 %all-gather.9.cloned.1.call-done = bf16[512,2048]{1,0:T(8,128)(2,1)} async-done(((bf16[128,2048]{1,0:T(8,128)(2,1)}), bf16[512,2048]{1,0:T(8,128)(2,1)}) %all-gather.9.cloned.1.call-update) | async-done | bytes 2097168 | tf_op jit(solution)/shard_map/all_gather | solution.py:83
  58.2 18.2 %convolution_bitcast_fusion = f32[512,4096]{0,1:T(8,128)} fusion(bf16[512,2048]{1,0:T(8,128)(2,1)} %all-gather.9.cloned.1.call-done, bf16[4096,2048]{1,0:T(8,128)(2,1)} %param.10, bf16[4096,2048]{1,0:T(8,128)(2,1)} %bitcast.37), kind=kOutput, calls=%fused_computation.2 | convolution fusion | flops 8598323200 | bytes 44040192 | tf_op jit(solution)/shard_map/dot_general | solution.py:57
  76.4 0.0 reduce-scatter.9.cloned.1.call-update
  76.4 0.0 reduce-scatter.5.cloned.1.call-start
  76.5 0.8 dynamic-slice_convert_fusion.2
  77.3 1.7 mul.251
  79.0 6.4 copy.47
  85.4 16.2 %mul.253 = bf16[2048,4096]{1,0:T(8,128)(2,1)} multiply(bf16[2048,4096]{1,0:T(8,128)(2,1)} %param.8, bf16[2048,4096]{1,0:T(8,128)(2,1)S(1)} %bitcast.34) | non-fusion elementwise | flops 8388608 | bytes 50331648 | tf_op jit(solution)/shard_map/mul | solution.py:20
  101.6 2.9 all-gather.5.cloned.1.call-done
  104.5 15.2 %convolution_bitcast_fusion.1 = f32[512,4096]{0,1:T(8,128)} fusion(bf16[2048,4096]{1,0:T(8,128)(2,1)} %mul.253, bf16[512,2048]{1,0:T(8,128)(2,1)} %all-gather.5.cloned.1.call-done), kind=kOutput, calls=%fused_computation.3 | convolution fusion | flops 8589934592 | bytes 27262976 | tf_op jit(solution)/shard_map/dot_general | solution.py:70
  119.7 0.0 reduce-scatter.5.cloned.1.call-update
  119.7 0.3 all-gather.11.cloned.1.call-start
  120.0 72.7 %reduce-scatter.9.cloned.1.call-done = f32[128,4096]{0,1:T(8,128)} async-done(((f32[512,4096]{0,1:T(8,128)}), f32[128,4096]{0,1:T(8,128)}) %reduce-scatter.9.cloned.1.call-update) | async-done | bytes 2097168 | tf_op jit(solution)/shard_map/reduce_scatter | solution.py:87
  192.7 1.9 copy.30
  194.6 1.7 reshape.254
  196.3 86.0 %reduce-scatter.5.cloned.1.call-done = f32[128,4096]{0,1:T(8,128)} async-done(((f32[512,4096]{0,1:T(8,128)}), f32[128,4096]{0,1:T(8,128)}) %reduce-scatter.5.cloned.1.call-update) | async-done | bytes 2097168 | tf_op jit(solution)/shard_map/reduce_scatter | solution.py:69
  282.3 1.9 copy.22
  284.2 1.7 reshape.253
  285.9 0.0 copy-start.2
  285.9 11.0 %fusion.3 = (f32[32,1,4096]{2,1,0:T(1,128)S(1)}, f32[32,1,4096]{2,1,0:T(1,128)S(1)}, f32[32,1,4096]{2,1,0:T(1,128)S(1)}, f32[32,1,4096]{2,1,0:T(1,128)S(1)}, f32...) fusion(f32[32,4,4096]{2,1,0:T(4,128)} %reshape.254, ...), kind=kLoop, calls=%fused_computation.28 | loop fusion | bytes 8388608 | tf_op jit(solution)/shard_map/slice | solution.py:44
  296.9 0.0 copy-done.2
  297.0 4.1 add_convert_fusion.3
  301.1 3.1 add_convert_fusion.2
  304.1 0.1 pad_maximum_fusion.1
  304.3 0.8 copy.35
  305.1 1.1 convert_element_type.37
  306.2 0.0 all-gather.11.cloned.1.call-update
  306.2 0.0 all-gather.7.cloned.1.call-start
  306.3 0.1 pad_maximum_fusion
  306.4 2.7 copy.27
  309.2 3.1 stack.8
  312.3 3.1 copy.28
  315.4 0.0 copy-done
  315.4 2.9 multiply_convert_fusion
  318.3 0.0 all-gather.7.cloned.1.call-update
  318.3 0.0 reduce-scatter.11.cloned.1.call-start
  318.4 40.7 %all-gather.11.cloned.1.call-done = bf16[512,4096]{1,0:T(8,128)(2,1)} async-done(((bf16[128,4096]{1,0:T(8,128)(2,1)}), bf16[512,4096]{1,0:T(8,128)(2,1)}) %all-gather.11.cloned.1.call-update) | async-done | bytes 4194320 | tf_op jit(solution)/shard_map/all_gather | solution.py:92
  359.1 25.3 %fusion.5 = f32[512,2048]{1,0:T(8,128)} fusion(bf16[512,4096]{1,0:T(8,128)(2,1)} %all-gather.11.cloned.1.call-done, bf16[2048,4096]{1,0:T(8,128)(2,1)} %mul.253), kind=kOutput, calls=%fused_computation.30 | convolution fusion | flops 8589934592 | bytes 25165824 | tf_op jit(solution)/shard_map/dot_general | solution.py:57
  384.4 0.0 reduce-scatter.11.cloned.1.call-update
  384.4 0.0 reduce-scatter.7.cloned.1.call-start
  384.5 0.1 copy.36
  384.6 0.1 copy.37
  384.6 2.8 mul.291
  387.4 20.7 %copy.50 = f32[512,8,8,256]{3,1,2,0:T(8,128)} copy(f32[512,8,8,256]{3,2,1,0:T(8,128)S(1)} %bitcast.32) | data formatting | bytes 67108864
  408.1 2.8 mul.288
  410.9 20.7 %copy.49 = f32[512,8,8,256]{3,1,2,0:T(8,128)} copy(f32[512,8,8,256]{3,2,1,0:T(8,128)S(1)} %bitcast.33) | data formatting | bytes 67108864
  431.6 28.2 %convolution_multiply_fusion = f32[4096,2048]{1,0:T(8,128)} fusion(f32[4096,2048]{1,0:T(8,128)} %bitcast.30, bf16[512,4096]{0,1:T(8,128)(2,1)} %all-gather.7.cloned.1.call-done, bf16[512,2048]{1,0:T(8,128)(2,1)} %all-gather.9.cloned.1.call-done), kind=kOutput, calls=%fused_computation.1 | convolution fusion | flops 8598323200 | bytes 73400320 | tf_op jit(solution)/shard_map/dot_general | solution.py:51
  459.8 0.0 copy-done.1
  459.8 24.0 %bitcast_multiply_fusion = f32[2048,4096]{0,1:T(8,128)} fusion(f32[2048,4096]{0,1:T(8,128)} %bitcast.31, bf16[512,4096]{1,0:T(8,128)(2,1)S(1)} %copy-done.1, bf16[512,2048]{1,0:T(8,128)(2,1)} %all-gather.5.cloned.1.call-done), kind=kOutput, calls=%fused_computation | convolution fusion | flops 8598323200 | bytes 73400320 | tf_op jit(solution)/shard_map/dot_general | solution.py:51
  483.8 18.1 %fusion.1 = f32[512,2048]{1,0:T(8,128)} fusion(bf16[512,4096]{0,1:T(8,128)(2,1)} %all-gather.7.cloned.1.call-done, bf16[4096,2048]{1,0:T(8,128)(2,1)} %param.10, bf16[4096,2048]{1,0:T(8,128)(2,1)} %bitcast.38), kind=kOutput, calls=%fused_computation.5 | convolution fusion | flops 8598323200 | bytes 41943040 | tf_op jit(solution)/shard_map/dot_general | solution.py:79
  501.9 0.0 reduce-scatter.7.cloned.1.call-update
  501.9 175.0 %all-reduce.2 = (bf16[2048,4096]{0,1:T(8,128)(2,1)}, bf16[4096,2048]{1,0:T(8,128)(2,1)}) all-reduce(f32[2048,4096]{0,1:T(8,128)} %bitcast_multiply_fusion, f32[4096,2048]{1,0:T(8,128)} %convolution_multiply_fusion), channel_id=1, replica_groups=mesh['dp'=2,'row'=4,'col'=4] {'dp'}, use_global_device_ids=true, to_apply=%region_4.5 | all-reduce | flops 16777216 | bytes 100663296 | tf_op jit(solution)/shard_map/psum | solution.py:94
  676.9 21.2 %copy.38 = bf16[2048,4096]{1,0:T(8,128)(2,1)} copy(bf16[2048,4096]{0,1:T(8,128)(2,1)} %get-tuple-element.16) | data formatting | bytes 33554432
  698.1 2.1 convert_element_type.38
  700.2 2.1 convert_element_type.36
  (5 shorter events, 0.0 us)
Async XLA Ops:
  7.2 51.1 %all-gather.9.cloned.1.call-start = ((), (), s32[]{:S(2)}) async-start(), calls=%async_computation.8 | async-start | bytes 2621440 | tf_op jit(solution)/shard_map/all_gather | solution.py:83
  7.9 96.6 %all-gather.5.cloned.1.call-start = ((), (), s32[]{:S(2)}) async-start(), calls=%async_computation.4 | async-start | bytes 2621440 | tf_op jit(solution)/shard_map/all_gather | solution.py:67
  8.7 184.0 %reduce-scatter.9.cloned.1.call-start = ((), (), s32[]{:S(2)}) async-start(), calls=%async_computation.9 | async-start | bytes 10485760 | tf_op jit(solution)/shard_map/reduce_scatter | solution.py:87
  76.4 205.9 %reduce-scatter.5.cloned.1.call-start = ((), (), s32[]{:S(2)}) async-start(), calls=%async_computation.5 | async-start | bytes 10485760 | tf_op jit(solution)/shard_map/reduce_scatter | solution.py:69
  119.7 239.4 %all-gather.11.cloned.1.call-start = ((), (), s32[]{:S(2)}) async-start(), calls=%async_computation.10 | async-start | bytes 5242880 | tf_op jit(solution)/shard_map/all_gather | solution.py:92
  285.9 11.0 %copy-start.2 = (f32[4096]{0:T(1024)S(1)}, f32[4096]{0:T(1024)}, u32[]{:S(2)}) copy-start(f32[4096]{0:T(1024)} %param.12) | copy-start | bytes 49156
  306.2 125.4 %all-gather.7.cloned.1.call-start = ((), (), s32[]{:S(2)}) async-start(), calls=%async_computation.6 | async-start | bytes 5242880 | tf_op jit(solution)/shard_map/all_gather | solution.py:78
  309.2 6.3 copy-start
  318.3 379.8 %reduce-scatter.11.cloned.1.call-start = ((), (), s32[]{:S(2)}) async-start(), calls=%async_computation.11 | async-start | bytes 5242880 | tf_op jit(solution)/shard_map/reduce_scatter | solution.py:96
  384.4 315.8 %reduce-scatter.7.cloned.1.call-start = ((), (), s32[]{:S(2)}) async-start(), calls=%async_computation.7 | async-start | bytes 5242880 | tf_op jit(solution)/shard_map/reduce_scatter | solution.py:80
  431.6 28.2 %copy-start.1 = (bf16[512,4096]{1,0:T(8,128)(2,1)S(1)}, bf16[512,4096]{1,0:T(8,128)(2,1)}, u32[]{:S(2)}) copy-start(bf16[512,4096]{1,0:T(8,128)(2,1)} %all-gather.11.cloned.1.call-done) | copy-start | bytes 12582916
Sparse Core Ops, SparseCore 0:
  9.6 48.6 all-gather.8
  59.8 44.6 all-gather.4
  107.6 85.0 reduce-scatter.8
  195.9 86.3 reduce-scatter.4
  306.4 52.6 all-gather.10
  360.8 52.5 all-gather.6
  415.7 76.7 reduce-scatter.10
  502.1 77.1 reduce-scatter.6
where the time goes:
time: 713 us; the launch traced here: 709 us
  waiting for transfers between devices  241 us (34%)
  blocking collectives  175 us (25%)
  matrix products  129 us (18%)
  local copies, waits for them, and re-layouts  117 us (16%)
  other arithmetic  32.2 us (5%)
  between operations  14.5 us (2%)
    psum x1, blocking collectives, per_device(): up_total = lax.psum(up_local, 'dp')  175 us
    reduce_scatter x1, waiting for transfers between devices, per_device(): lax.psum_scatter(jnp.dot(x_all, up_masked, preferred_element_type=jnp.flo...  86 us
    unnamed x11, local copies, waits for them, and re-layouts  78.6 us
    reduce_scatter x1, waiting for transfers between devices, per_device(): lax.psum_scatter(contract_cols(grad_all, down_masked), 'col', scatter_dim...  72.7 us
    dot_general x2, matrix products, contract_rows(): lax.dot_general(left, right, (((0,), (0,)), ((), ())), preferred_element_...  52.2 us
    dot_general x2, matrix products, contract_cols(): lax.dot_general(left, right, (((1,), (1,)), ((), ())), preferred_element_...  43.5 us
    all_gather x1, waiting for transfers between devices, per_device(): current_all = lax.all_gather(current_grad, 'col', axis=0, tiled=True)  40.7 us
    all_gather x1, waiting for transfers between devices, per_device(): grad_all = lax.all_gather(cotangent, 'row', axis=0, tiled=True)  37.3 us
  transfers between devices with their start and end apart: 8, of which 5 were waited for; matrix products, arithmetic and copies ran while one was open for 36% of the time, Pallas kernels for 0%

commit v1 on v0

v1 whole, which is shorter than its diff:
```python
import functools
import math

import jax
import jax.numpy as jnp
from jax import lax
from jax.experimental import pallas as pl
from jax.experimental.pallas import tpu as pltpu
from jax.sharding import PartitionSpec as P

BLOCK = 256
STEPS = 4
QUARTERS = 4
LANES = 128
SLOTS = 32
STAGES = 4
PIECES = 8
CODE_UNIT = 2.0**-13
LARGEST_INPUT = 6.0
LARGEST_WEIGHT = 0.1875
VMEM_LIMIT = 56 * 1024 * 1024


spike_width = 1.0

VMEM = pl.BlockSpec(memory_space=pltpu.VMEM)
SMEM = pl.BlockSpec(memory_space=pltpu.SMEM)
ANY = pl.BlockSpec(memory_space=pl.ANY)


def params():
    return pltpu.CompilerParams(vmem_limit_bytes=VMEM_LIMIT)


def shape(dims, kind):
    return jax.ShapeDtypeStruct(dims, kind)


def product(left, right, left_dim, right_dim):
    return lax.dot_general(
        left, right, (((left_dim,), (right_dim,)), ((), ())), preferred_element_type=jnp.float32
    )


def split_units(units):
    quarter = units // QUARTERS
    width = min(BLOCK, quarter)
    return quarter, width, quarter // width


def code_rate(depth):
    largest = 2.02 * depth * LARGEST_INPUT * LARGEST_WEIGHT
    return 32760.0 / math.log1p(largest / CODE_UNIT)


def encode(value, rate):
    size = jnp.log(1.0 + jnp.abs(value) * (1.0 / CODE_UNIT)) * rate + 0.5
    code = size.astype(jnp.int32)
    return jnp.where(value < 0.0, -code, code).astype(jnp.int16)


def decode(code, rate):
    wide = code.astype(jnp.int32).astype(jnp.float32)
    size = (jnp.exp(jnp.abs(wide) * (1.0 / rate)) - 1.0) * CODE_UNIT
    return jnp.where(wide < 0.0, -size, size)


def lists_kernel(place, mask_up, mask_down, up_list, down_list, *, deep, parts, width):
    col, row = place[0], place[1]
    groups = QUARTERS * parts
    units = groups * width // BLOCK

    def walk(g, counts):
        up, down = counts
        piece = (col ^ (g // parts)) * parts + g % parts
        unit = row * units + piece * width // BLOCK
        for k in range(deep):
            entry = piece * 65536 + g * 256 + k
            feature = col * deep + k
            up_list[up] = entry
            down_list[down] = entry
            up = up + mask_up[feature, unit]
            down = down + mask_down[unit, feature]
        return up, down

    up, down = lax.fori_loop(0, groups, walk, (jnp.int32(0), jnp.int32(0)))
    up_list[groups * deep] = up
    down_list[groups * deep] = down


def kept_lists(place, mask_up, mask_down, features, units):
    _, width, parts = split_units(units)
    deep = features // BLOCK
    size = QUARTERS * parts * deep + 1
    return pl.pallas_call(
        functools.partial(lists_kernel, deep=deep, parts=parts, width=width),
        in_specs=[SMEM] * 3,
        out_specs=[SMEM] * 2,
        out_shape=[shape((size,), jnp.int32)] * 2,
        compiler_params=params(),
        name="kept_blocks",
    )(place, mask_up, mask_down)


def each_kept(lists, weights, held, sems, width, hidden_first, use, meanwhile):
    counts = [entries[entries.shape[0] - 1] for entries in lists]

    def copy(which, entry, slot):
        units = pl.ds(pl.multiple_of((entry >> 16) * width, width), width)
        features = pl.ds(pl.multiple_of((entry & 255) * BLOCK, BLOCK), BLOCK)
        weight = weights[which]
        source = weight.at[units, features] if hidden_first[which] else weight.at[features, units]
        return pltpu.make_async_copy(source, held[which].at[slot], sems.at[which, slot])

    def fetch(base):
        for which in range(2):

            def start(i, _, which=which):
                copy(which, lists[which][base + i], i).start()
                return 0

            lax.fori_loop(0, jnp.clip(counts[which] - base, 0, SLOTS), start, 0)

    fetch(0)
    for slots in held:
        slots[SLOTS] = jnp.zeros(slots.shape[1:], slots.dtype)
    meanwhile()

    def turn(index, _):
        base = index * SLOTS
        live = [jnp.clip(count - base, 0, SLOTS) for count in counts]

        @pl.when(index > 0)
        def _():
            fetch(base)

        for which in range(2):

            def finish(i, _, which=which):
                copy(which, lists[which][base + i], i).wait()
                return 0

            lax.fori_loop(0, live[which], finish, 0)

        def work(i, _):
            for t in range(2):
                spot = i * 2 + t
                for which in range(2):
                    real = spot < live[which]
                    entry = lists[which][jnp.where(real, base + spot, 0)]
                    slot = jnp.where(real, spot, SLOTS)
                    use(which, (entry >> 8) & 255, entry & 255, held[which].at[slot])
            return 0

        lax.fori_loop(0, (jnp.maximum(live[0], live[1]) + 1) // 2, work, 0)
        return 0

    turns = (jnp.maximum(counts[0], counts[1]) + SLOTS - 1) // SLOTS
    lax.fori_loop(0, turns, turn, 0)


def scatter_kernel(
    up_list,
    down_list,
    left,
    w_up,
    w_down,
    own,
    keep_a,
    keep_b,
    send_y,
    send_x,
    turned,
    held_up,
    held_down,
    acc,
    sems,
):
    _, groups, rows, width = acc.shape
    depth = left.shape[2]
    parts = groups // QUARTERS
    half = rows // 2
    rate = code_rate(depth)

    def meanwhile():
        acc[...] = jnp.zeros_like(acc)
        for which in range(2):
            for k in range(depth // BLOCK):
                columns = slice(k * BLOCK, (k + 1) * BLOCK)
                turned[which, columns, :] = left[which, :, columns].T

    def use(which, g, k, block):
        columns = pl.ds(pl.multiple_of(k * BLOCK, BLOCK), BLOCK)
        acc[which, g] += product(left[which, :, columns], block[...], 1, which)

    each_kept(
        (up_list, down_list),
        (w_up, w_down),
        (held_up, held_down),
        sems,
        width,
        (False, True),
        use,
        meanwhile,
    )
    for which in range(2):
        for part in range(parts):
            columns = slice(part * width, (part + 1) * width)
            near_x, near_y, far = (acc.at[which, r * parts + part] for r in (1, 2, 3))
            send_y[which, 0, :, columns] = encode(near_y[:half], rate)
            send_y[which, 1, :, columns] = encode(far[:half], rate)
            send_x[which, 0, :, columns] = encode(near_x[half:], rate)
            send_x[which, 1, :, columns] = encode(far[half:], rate)
            keep_a[which, :, columns] = near_x[:half]
            keep_b[which, :, columns] = near_y[half:]
            own[which, :, columns] = acc[which, part]


def scatter_terms(lists, left, w_up, w_down):
    _, rows, depth = left.shape
    units = w_up.shape[1]
    quarter, width, parts = split_units(units)
    half = rows // 2
    return pl.pallas_call(
        scatter_kernel,
        in_specs=[SMEM, SMEM, VMEM, ANY, ANY],
        out_specs=[VMEM] * 6,
        scratch_shapes=[
            pltpu.VMEM((SLOTS + 1, BLOCK, width), w_up.dtype),
            pltpu.VMEM((SLOTS + 1, width, BLOCK), w_down.dtype),
            pltpu.VMEM((2, QUARTERS * parts, rows, width), jnp.float32),
            pltpu.SemaphoreType.DMA((2, SLOTS)),
        ],
        out_shape=[
            shape((2, rows, quarter), jnp.float32),
            shape((2, half, quarter), jnp.float32),
            shape((2, half, quarter), jnp.float32),
            shape((2, 2, half, quarter), jnp.int16),
            shape((2, 2, half, quarter), jnp.int16),
            shape((2, depth, rows), left.dtype),
        ],
        compiler_params=params(),
        cost_estimate=pl.CostEstimate(
            flops=rows * depth * units // 2, bytes_accessed=16 * 2**20, transcendentals=0
        ),
        name="current_and_hidden_grad_terms",
    )(*lists, left, w_up, w_down)


def relay_kernel(keep_a, keep_b, near_y, near_x, late_a, late_b, *, rate):
    for which in range(2):
        late_a[which] = encode(keep_a[which] + decode(near_y[which, 1], rate), rate)
        late_b[which] = encode(keep_b[which] + decode(near_x[which, 1], rate), rate)


def relay(keep_a, keep_b, near_y, near_x, rate):
    return pl.pallas_call(
        functools.partial(relay_kernel, rate=rate),
        in_specs=[VMEM] * 4,
        out_specs=[VMEM] * 2,
        out_shape=[shape(keep_a.shape, jnp.int16)] * 2,
        compiler_params=params(),
        name="relayed_terms",
    )(keep_a, keep_b, near_y, near_x)


def neuron_kernel(
    own, near_y, near_x, late_a, late_b, theta, both, values, grads, hiddens, results, *, rate
):
    rows = own.shape[1]
    tokens = rows // STEPS
    half = rows // 2
    for i in range(own.shape[2] // LANES):
        columns = slice(i * LANES, (i + 1) * LANES)
        limit = theta[:, columns]
        for which, into in ((0, values), (1, grads)):
            for span, near, late in (
                (slice(0, half), near_y, late_a),
                (slice(half, rows), near_x, late_b),
            ):
                into[i, span] = own[which, span, columns] + (
                    decode(near[which, 0, :, columns], rate)
                    + decode(late[which, :, columns], rate)
                )
        membrane = jnp.zeros((tokens, LANES), jnp.float32)
        steps = []
        for step in range(STEPS):
            value = values[i, pl.ds(step, tokens, stride=STEPS), :]
            volt = membrane + value
            spike = jnp.clip((volt - limit) / spike_width + 0.5, 0.0, 1.0)
            membrane = volt - limit * spike
            hiddens[i, pl.ds(step, tokens, stride=STEPS), :] = spike * value
            steps.append((value, volt, spike))
        both[0, :, columns] = hiddens[i].astype(both.dtype)
        carry = jnp.zeros((tokens, LANES), jnp.float32)
        for step in range(STEPS - 1, -1, -1):
            value, volt, spike = steps[step]
            grad = grads[i, pl.ds(step, tokens, stride=STEPS), :]
            offset = 2.0 * (volt - limit) / spike_width
            gamma = 1.0 / (spike_width * (1.0 + offset * offset))
            dvolt = carry * (1.0 - limit * gamma) + grad * value * gamma
            results[i, pl.ds(step, tokens, stride=STEPS), :] = dvolt + grad * spike
            carry = dvolt
        both[1, :, columns] = results[i].astype(both.dtype)


def neurons(own, near_y, near_x, late_a, late_b, theta, rate):
    _, rows, quarter = own.shape
    return pl.pallas_call(
        functools.partial(neuron_kernel, rate=rate),
        in_specs=[VMEM] * 6,
        out_specs=VMEM,
        scratch_shapes=[pltpu.VMEM((quarter // LANES, rows, LANES), jnp.float32)] * 4,
        out_shape=shape((2, rows, quarter), jnp.bfloat16),
        compiler_params=params(),
        name="spiking_and_surrogate",
    )(own, near_y, near_x, late_a, late_b, theta)


def collect_kernel(*refs, carried):
    up_list, down_list, mine, over_x, over_y, far_a, far_b = refs[:7]
    at = 8 if carried else 7
    w_up, w_down, out, whole, held_up, held_down, acc, sems = refs[at:]
    _, rows, quarter = mine.shape
    wide = acc.shape[1]
    width = held_up.shape[2]
    parts = quarter // width
    half = rows // 2

    def meanwhile():
        whole[:, 0] = mine[...]
        whole[:, 1] = over_x[...]
        whole[:, 2] = over_y[...]
        whole[:, 3, :half] = far_a[...]
        whole[:, 3, half:] = far_b[...]
        if carried:
            came = refs[7]
            first = came.shape[1]
            for which in range(2):
                for j in range(wide):
                    columns = slice(j * BLOCK, (j + 1) * BLOCK)
                    acc[which, j, :first] = came[which, :, columns].astype(jnp.float32)
            if first < rows:
                acc[:, :, first:] = jnp.zeros((2, wide, rows - first, BLOCK), jnp.float32)
        else:
            acc[...] = jnp.zeros_like(acc)

    def use(which, g, k, block):
        r, part = g // parts, g % parts
        columns = pl.ds(pl.multiple_of(part * width, width), width)
        acc[which, k] += product(whole[which, r, :, columns], block[...], 1, which)

    each_kept(
        (down_list, up_list),
        (w_down, w_up),
        (held_down, held_up),
        sems,
        width,
        (True, False),
        use,
        meanwhile,
    )
    for which in range(2):
        for j in range(wide):
            out[which, :, j * BLOCK : (j + 1) * BLOCK] = acc[which, j].astype(out.dtype)


def collect_terms(lists, pieces, came, w_up, w_down, out_type):
    _, rows, quarter = pieces[0].shape
    features, units = w_up.shape
    _, width, _ = split_units(units)
    extra = [] if came is None else [came]
    return pl.pallas_call(
        functools.partial(collect_kernel, carried=came is not None),
        in_specs=[SMEM, SMEM] + [VMEM] * (5 + len(extra)) + [ANY, ANY],
        out_specs=[VMEM, VMEM],
        scratch_shapes=[
            pltpu.VMEM((SLOTS + 1, BLOCK, width), w_up.dtype),
            pltpu.VMEM((SLOTS + 1, width, BLOCK), w_down.dtype),
            pltpu.VMEM((2, features // BLOCK, rows, BLOCK), jnp.float32),
            pltpu.SemaphoreType.DMA((2, SLOTS)),
        ],
        out_shape=[
            shape((2, rows, features), out_type),
            shape((2, QUARTERS, rows, quarter), pieces[0].dtype),
        ],
        compiler_params=params(),
        cost_estimate=pl.CostEstimate(
            flops=rows * features * units // 2, bytes_accessed=16 * 2**20, transcendentals=0
        ),
        name="output_and_input_grad_terms",
    )(*lists, *pieces, *extra, w_up, w_down)


def clear_kernel(place, up, down, rows_up, rows_down, sems):
    rows_up[...] = jnp.zeros_like(rows_up)
    rows_down[...] = jnp.zeros_like(rows_down)
    copies = []
    for which, (whole, rows) in enumerate(((up, rows_up), (down, rows_down))):
        for i in range(PIECES):
            target = whole.at[pl.ds(i * rows.shape[0], rows.shape[0]), :]
            copies.append(pltpu.make_async_copy(rows, target, sems.at[which, i]))
    for copy in copies:
        copy.start()
    for copy in copies:
        copy.wait()


def cleared(place, features, units, kind):
    return pl.pallas_call(
        clear_kernel,
        in_specs=[SMEM],
        out_specs=[ANY, ANY],
        scratch_shapes=[
            pltpu.VMEM((features // PIECES, units), kind),
            pltpu.VMEM((units // PIECES, features), kind),
            pltpu.SemaphoreType.DMA((2, PIECES)),
        ],
        out_shape=[shape((features, units), kind), shape((units, features), kind)],
        compiler_params=params(),
        cost_estimate=pl.CostEstimate(
            flops=0, bytes_accessed=4 * features * units, transcendentals=0
        ),
        name="zero_weight_grads",
    )(place)


def weight_grads_kernel(*refs, count):
    lists = refs[:2]
    units = refs[2 : 2 + count]
    turned = refs[2 + count : 2 + 2 * count]
    outs = refs[4 + 2 * count : 6 + 2 * count]
    held_u, held_f, stage_up, stage_down, load_sems, out_sems = refs[6 + 2 * count :]
    width = stage_up.shape[2]
    parts = held_u.shape[3] // width
    stages = (stage_up, stage_down)

    def loads(which):
        copies = []
        first = 0
        for i in range(count):
            rows = units[i].shape[2]
            span = pl.ds(first, rows)
            first += rows
            copies.append(
                pltpu.make_async_copy(
                    units[i].at[1 - which],
                    held_u.at[1 - which, :, span, :],
                    load_sems.at[which, 0, i],
                )
            )
            copies.append(
                pltpu.make_async_copy(
                    turned[i].at[which], held_f.at[which, :, span], load_sems.at[which, 1, i]
                )
            )
        return copies

    def store(which, n):
        entry = lists[which][n]
        slot = n % STAGES
        piece = pl.ds(pl.multiple_of((entry >> 16) * width, width), width)
        features = pl.ds(pl.multiple_of((entry & 255) * BLOCK, BLOCK), BLOCK)
        out = outs[which]
        target = out.at[piece, features] if which else out.at[features, piece]
        return pltpu.make_async_copy(stages[which].at[slot], target, out_sems.at[which, slot])

    first, second = loads(1), loads(0)
    for copy in first + second:
        copy.start()
    totals = [entries[entries.shape[0] - 1] for entries in lists]
    for which, copies in ((1, first), (0, second)):
        for copy in copies:
            copy.wait()

        def block(n, _, which=which):
            entry = lists[which][n]
            g = (entry >> 8) & 255
            features = pl.ds(pl.multiple_of((entry & 255) * BLOCK, BLOCK), BLOCK)
            columns = pl.ds(pl.multiple_of(g % parts * width, width), width)

            @pl.when(n >= STAGES)
            def _():
                store(which, n - STAGES).wait()

            value = product(
                held_f[which, features, :], held_u[1 - which, g // parts, :, columns], 1, 0
            )
            stage = stages[which]
            stage[n % STAGES] = (value.T if which else value).astype(stage.dtype)
            store(which, n).start()
            return 0

        lax.fori_loop(0, totals[which], block, 0)

    for which in (1, 0):

        def drain(n, _, which=which):
            store(which, n).wait()
            return 0

        lax.fori_loop(jnp.maximum(totals[which] - STAGES, 0), totals[which], drain, 0)


def weight_grads(lists, units, turned, zeros):
    count = len(units)
    quarter = units[0].shape[3]
    rows = sum(piece.shape[2] for piece in units)
    features = turned[0].shape[1]
    width = min(BLOCK, quarter)
    kind = units[0].dtype
    return pl.pallas_call(
        functools.partial(weight_grads_kernel, count=count),
        in_specs=[SMEM] * 2 + [ANY] * (2 * count + 2),
        out_specs=[ANY, ANY],
        scratch_shapes=[
            pltpu.VMEM((2, QUARTERS, rows, quarter), kind),
            pltpu.VMEM((2, features, rows), kind),
            pltpu.VMEM((STAGES, BLOCK, width), kind),
            pltpu.VMEM((STAGES, width, BLOCK), kind),
            pltpu.SemaphoreType.DMA((2, 2, count)),
            pltpu.SemaphoreType.DMA((2, STAGES)),
        ],
        out_shape=[shape(zero.shape, kind) for zero in zeros],
        input_output_aliases={2 + 2 * count: 0, 3 + 2 * count: 1},
        compiler_params=params(),
        cost_estimate=pl.CostEstimate(
            flops=rows * QUARTERS * quarter * features // 2,
            bytes_accessed=32 * 2**20,
            transcendentals=0,
        ),
        name="weight_grads",
    )(*lists, *units, *turned, *zeros)


def after(value, *others):
    return lax.optimization_barrier((value, *others))[0]


def across(value, flip):
    size = lax.axis_size("col")
    return lax.ppermute(value, "col", [(i, i ^ flip) for i in range(size)])


def other_core(value):
    return lax.ppermute(value, "dp", [(0, 1), (1, 0)])


def around(value):
    size = lax.axis_size("row")
    ring = list(range(0, size, 2)) + list(range(size - 1 - size % 2, 0, -2))
    return lax.ppermute(value, "row", [(ring[i], ring[(i + 1) % size]) for i in range(size)])


def per_device(inputs, w_up, mask_up, w_down, mask_down, threshold, cotangent):
    col_place = lax.axis_index("col").astype(jnp.int32)
    row_place = lax.axis_index("row").astype(jnp.int32)
    place = jnp.stack([col_place, row_place])
    features, units = w_up.shape
    quarter = units // QUARTERS
    rate = code_rate(features)
    theta = lax.dynamic_slice(threshold, (col_place * quarter,), (quarter,)).reshape(1, quarter)
    lists = kept_lists(place, mask_up, mask_down, features, units)
    rows = inputs.shape[0]

    ringed = lax.axis_size("row") == 4
    both = jnp.stack([inputs, cotangent])
    if ringed:
        rings = [both, around(both)]
        groups = ((0,), (1,), (2,), (3,))
    else:
        rings = [lax.all_gather(both, "row", axis=1, tiled=True)]
        groups = ((0,),)

    count = len(groups)
    terms, relays, pairs, gathered, wholes = ([None] * count for _ in range(5))
    carry = {"mine": None, "came": None, "last": None, "zeros": None}

    def scatter(i):
        chunk = [rings[j] for j in groups[i]]
        chunk = chunk[0] if len(chunk) == 1 else jnp.concatenate(chunk, axis=1)
        if carry["last"] is not None:
            chunk = after(chunk, carry["last"])
        own, keep_a, keep_b, send_y, send_x, turned = scatter_terms(lists, chunk, w_up, w_down)
        terms[i] = (own, keep_a, keep_b, across(send_y, 2), across(send_x, 1), turned)
        carry["last"] = own

    def hop():
        rings.append(around(after(rings[-1], carry["last"])))

    def clear():
        zeros = cleared(after(place, carry["last"]), features, units, w_up.dtype)
        carry["zeros"] = zeros
        carry["last"] = zeros[0]

    def pass_on(i):
        _, keep_a, keep_b, near_y, near_x, _ = terms[i]
        late_a, late_b = relay(after(keep_a, carry["last"]), keep_b, near_y, near_x, rate)
        relays[i] = (across(late_a, 1), across(late_b, 2))
        carry["last"] = late_a

    def fire(i):
        own, _, _, near_y, near_x, _ = terms[i]
        pair = neurons(after(own, carry["last"]), near_y, near_x, *relays[i], theta, rate)
        half = pair.shape[1] // 2
        over_x = across(pair, 1)
        over_y = across(pair, 2)
        far_a = across(over_y[:, :half], 1)
        far_b = across(over_x[:, half:], 2)
        gathered[i] = (pair, over_x, over_y, far_a, far_b)
        carry["last"] = pair

    def collect(i):
        first = carry["mine"] is None
        kind = jnp.float32 if first else jnp.bfloat16
        pair, *others = gathered[i]
        part, whole = collect_terms(
            lists, (after(pair, carry["last"]), *others), carry["came"], w_up, w_down, kind
        )
        if first:
            carry["mine"] = part
        else:
            came = around(part[:, :rows])
            for j in range(1, len(groups[i])):
                came = around(part[:, j * rows : (j + 1) * rows] + came)
            carry["came"] = came
        wholes[i] = whole
        carry["last"] = whole

    if ringed:
        order = "S0 H R0 S1 H F0 R1 S2 F1 C0 R2 S3 F2 C1 R3 F3 C2 Z C3"
    else:
        order = "S0 R0 F0 Z C0"
    for word in order.split():
        if word == "Z":
            clear()
        elif word == "H":
            hop()
        else:
            {"S": scatter, "R": pass_on, "F": fire, "C": collect}[word[0]](int(word[1]))

    unit_parts = wholes + [other_core(whole) for whole in wholes]
    feature_parts = [term[5] for term in terms] + [other_core(term[5]) for term in terms]
    up_grad, down_grad = weight_grads(lists, unit_parts, feature_parts, carry["zeros"])
    mine, came = after(carry["mine"], up_grad), carry["came"]
    if ringed:
        ends = mine + came.astype(jnp.float32)
    else:
        ends = lax.psum_scatter(mine, "row", scatter_dimension=1, tiled=True)
    output, input_grad = ends[0].astype(jnp.bfloat16), ends[1].astype(jnp.bfloat16)
    return (output, input_grad, up_grad, down_grad)


def solution(mesh):
    in_specs = (
        P(("dp", "row"), "col"),
        P("col", "row"),
        P(),
        P("row", "col"),
        P(),
        P("row"),
        P(("dp", "row"), "col"),
    )
    out_specs = (P(("dp", "row"), "col"), P(("dp", "row"), "col"), P("col", "row"), P("row", "col"))
    return jax.shard_map(
        per_device, mesh=mesh, in_specs=in_specs, out_specs=out_specs, check_vma=False
    )
```

time: 713 us -> 259 us (0.36)
  waiting for transfers between devices: 241 us -> 50.4 us
  blocking collectives: 175 us -> 0 us
  matrix products: 129 us -> 0 us
  Pallas kernels: 0 us -> 127 us
  local copies, waits for them, and re-layouts: 117 us -> 16.6 us
  starting transfers between devices: 0.58 us -> 57.1 us
  other arithmetic: 32.2 us -> 2.14 us
  between operations: 14.5 us -> 1.16 us
    psum x1 -> x0, blocking collectives: 175 us -> none  [per_device(): up_total = lax.psum(up_local, 'dp')]
    reduce_scatter x4 -> x0, waiting for transfers between devices: 159 us -> none  [the longest x1 86 us: per_device(): lax.psum_scatter(jnp.dot(x_all, up_masked, preferred_element_type=jnp.flo...]
    dot_general x6 -> x0, matrix products: 129 us -> none  [the longest x2 52.2 us: contract_rows(): lax.dot_general(left, right, (((0,), (0,)), ((), ())), preferred_element_...]
    pallas_call x0 -> x19, Pallas kernels: none -> 127 us  [the longest x4 34.4 us: collect_terms(): pl.pallas_call(functools.partial(collect_kernel, carried=came is not None...]
    all_gather x4 -> x0, waiting for transfers between devices: 81 us -> none  [the longest x1 40.7 us: per_device(): current_all = lax.all_gather(current_grad, 'col', axis=0, tiled=True)]
    unnamed x11 -> x95, local copies, waits for them, and re-layouts: 78.6 us -> 14.1 us
    ppermute x0 -> x46, starting transfers between devices: none -> 57.1 us  [the longest x32 33.6 us: across(): return lax.ppermute(value, 'col', [(i, i ^ flip) for i in range(size)])]
    ppermute x0 -> x46, waiting for transfers between devices: none -> 50.4 us  [the longest x32 37.3 us: across(): return lax.ppermute(value, 'col', [(i, i ^ flip) for i in range(size)])]
  transfers between devices with their start and end apart: 8 -> 46, of which waited for: 5 -> 17; matrix products, arithmetic and copies ran while one was open for 36% -> 1% of each run, Pallas kernels for 0% -> 47%
where the time goes in v1:
time: 259 us; the launch traced here: 254 us
  Pallas kernels  127 us (49%)
  starting transfers between devices  57.1 us (22%)
  waiting for transfers between devices  50.4 us (19%)
  local copies, waits for them, and re-layouts  16.6 us (6%)
    ppermute x32, waiting for transfers between devices, across(): return lax.ppermute(value, 'col', [(i, i ^ flip) for i in range(size)])  37.3 us
    pallas_call x4, Pallas kernels, collect_terms(): pl.pallas_call(functools.partial(collect_kernel, carried=came is not None...  34.4 us
    pallas_call x4, Pallas kernels, scatter_terms(): pl.pallas_call(scatter_kernel, in_specs=[SMEM, SMEM, VMEM, ANY, ANY], out...  34.2 us
    ppermute x32, starting transfers between devices, across(): return lax.ppermute(value, 'col', [(i, i ^ flip) for i in range(size)])  33.6 us
    ppermute x6, starting transfers between devices, around(): lax.ppermute(value, 'row', [(ring[i], ring[(i + 1) % size]) for i in rang...  21.7 us
    pallas_call x1, Pallas kernels, weight_grads(): pl.pallas_call(functools.partial(weight_grads_kernel, count=count), in_sp...  16.3 us
    pallas_call x4, Pallas kernels, neurons(): pl.pallas_call(functools.partial(neuron_kernel, rate=rate), in_specs=[VME...  15 us
    unnamed x95, local copies, waits for them, and re-layouts  14.1 us
  transfers between devices with their start and end apart: 46, of which 17 were waited for; matrix products, arithmetic and copies ran while one was open for 1% of the time, Pallas kernels for 47%

profile of v1, /device:TPU:0, one launch (start us, length us, event | category | flops | bytes accessed | tf_op | source)
XLA Modules:
  0.0 254.3 jit_solution(13894989805885280016)
XLA Ops:
  0.6 1.3 pad_maximum_fusion.left
  2.0 4.1 %collective-permute-start = (bf16[2,128,2048]{2,1,0:T(8,128)(2,1)S(1)}, bf16[2,128,2048]{2,1,0:T(8,128)(2,1)S(1)}, u32[]{:S(2)}, u32[]{:S(2)}) collective-permute-start(bf16[2,128,2048]{2,1,0:T(8,128)(2,1)S(1)} %pad_maximum_fusion.left), channel_id=1, source_target_pairs={{0,8},{8,12},{12,4},{4,0},{1,9},{9,13},{13,5},{5,1},{2,10},{10,14}... | collective-permute-start | bytes 3145736 | tf_op jit(solution)/shard_map/ppermute | solution.py:552
  7.3 2.9 %kept_blocks.1 = (s32[129]{0:T(256)}, s32[129]{0:T(256)}) custom-call(s32[2]{0:T(128)} %pad_add_fusion.place, s32[32,64]{1,0:T(8,128)} %mask_up.1, s32[64,32]{1,0:T(8,128)} %copy.13.mask_down), custom_call_target="tpu_custom_call" | custom-call | tf_op jit(solution)/shard_map/kept_blocks/pallas_call | solution.py:95
  10.3 8.5 %current_and_hidden_grad_terms.4 = (f32[2,128,1024]{2,1,0:T(8,128)}, f32[2,64,1024]{2,1,0:T(8,128)}, f32[2,64,1024]{2,1,0:T(8,128)}, s16[2,2,64,1024]{3,2,1,0:T(...) custom-call(s32[129]{0:T(256)} %get-tuple-element.69.up_list.refs_0_, ...), custom_call_target="tpu_custom_call" | custom-call | flops 536870912 | bytes 16777216 | tf_op jit(solution)/shard_map/current_and_hidden_grad_terms/pallas_call | solution.py:224
  18.8 1.3 collective-permute-start.1
  20.1 1.9 collective-permute-start.2
  22.0 6.5 %collective-permute-done.left = bf16[2,128,2048]{2,1,0:T(8,128)(2,1)S(1)} collective-permute-done((bf16[2,128,2048]{2,1,0:T(8,128)(2,1)S(1)}, bf16[2,128,2048]{2,1,0:T(8,128)(2,1)S(1)}, u32[]{:S(2)}, u32[]{:S(2)}) %collective-permute-start) | collective-permute-done | bytes 1048608 | tf_op jit(solution)/shard_map/ppermute | solution.py:552
  28.5 3.4 %collective-permute-start.5 = (bf16[2,128,2048]{2,1,0:T(8,128)(2,1)S(1)}, bf16[2,128,2048]{2,1,0:T(8,128)(2,1)S(1)}, u32[]{:S(2)}, u32[]{:S(2)}) collective-permute-start(bf16[2,128,2048]{2,1,0:T(8,128)(2,1)S(1)} %collective-permute-done.left), channel_id=1, source_target_pairs={{0,8},{8,12},{12,4},{4,0},{1,9},{9,13},{13,5},{5,1},{2,10},{10,14}... | collective-permute-start | bytes 3145736 | tf_op jit(solution)/shard_map/ppermute | solution.py:552
  32.4 1.1 collective-permute-done.2.near_x
  34.4 3.1 %relayed_terms.4 = (s16[2,64,1024]{2,1,0:T(8,128)(2,1)}, s16[2,64,1024]{2,1,0:T(8,128)(2,1)}) custom-call(f32[2,64,1024]{2,1,0:T(8,128)} %get-tuple-element.73.keep_a, f32[2,64,1024]{2,1,0:T(8,128)} %get-tuple-element.74.keep_b, s16[2,2,64,1024]{3,2,1,0:T(8,128)(2,1)} %copy-done.12, s16[2,2,64,1024]{3,2,1,0:T(8,128)(2,1)} %copy-done.13), custom_call_target="tpu_custom_call" | custom-call | tf_op jit(solution)/shard_map/relayed_terms/pallas_call | solution.py:257
  38.1 1.6 collective-permute-start.3
  39.6 8.5 %current_and_hidden_grad_terms.5 = (f32[2,128,1024]{2,1,0:T(8,128)}, f32[2,64,1024]{2,1,0:T(8,128)}, f32[2,64,1024]{2,1,0:T(8,128)}, s16[2,2,64,1024]{3,2,1,0:T(...) custom-call(s32[129]{0:T(256)} %get-tuple-element.69.up_list.refs_0_, ...), custom_call_target="tpu_custom_call" | custom-call | flops 536870912 | bytes 16777216 | tf_op jit(solution)/shard_map/current_and_hidden_grad_terms/pallas_call | solution.py:224
  48.1 1.4 collective-permute-start.6
  50.2 1.3 dynamic_slice.3
  52.2 3.7 %spiking_and_surrogate.4.refs_2_ = bf16[2,128,1024]{2,1,0:T(8,128)(2,1)} custom-call(f32[2,128,1024]{2,1,0:T(8,128)} %get-tuple-element.80.own, s16[2,2,64,1024]{3,2,1,0:T(8,128)(2,1)} %copy-done.12, s16[2,2,64,1024]{3,2,1,0:T(8,128)(2,1)} %copy-done.13, s16[2,64,1024]{2,1,0:T(8,128)(2,1)} %collective-permute-done.3.late_a, s16[2,64,1024]{2,1,0:T(8,128)(2,1)} %copy-done.38, ...), custom_call_target="tpu_custom_call" | custom-call | tf_op jit(solution)/shard_map/spiking_and_surrogate/pallas_call | solution.py:309
  56.1 1.9 collective-permute-start.10
  58.0 2.9 %collective-permute-start.14 = (bf16[2,128,2048]{2,1,0:T(8,128)(2,1)S(1)}, bf16[2,128,2048]{2,1,0:T(8,128)(2,1)S(1)}, u32[]{:S(2)}, u32[]{:S(2)}) collective-permute-start(bf16[2,128,2048]{2,1,0:T(8,128)(2,1)S(1)} %collective-permute-done.5.left), channel_id=1, source_target_pairs={{0,8},{8,12},{12,4},{4,0},{1,9},{9,13},{13,5},{5,1},{2,10},{10,14}... | collective-permute-start | bytes 3145736 | tf_op jit(solution)/shard_map/ppermute | solution.py:552
  60.9 2.4 collective-permute-done.6.near_y
  63.3 1.3 collective-permute-done.7.near_x
  65.4 3.1 %relayed_terms.5 = (s16[2,64,1024]{2,1,0:T(8,128)(2,1)}, s16[2,64,1024]{2,1,0:T(8,128)(2,1)}) custom-call(f32[2,64,1024]{2,1,0:T(8,128)} %get-tuple-element.84.keep_a, f32[2,64,1024]{2,1,0:T(8,128)} %get-tuple-element.85.keep_b, s16[2,2,64,1024]{3,2,1,0:T(8,128)(2,1)} %copy-done.8, s16[2,2,64,1024]{3,2,1,0:T(8,128)(2,1)} %copy-done.9), custom_call_target="tpu_custom_call" | custom-call | tf_op jit(solution)/shard_map/relayed_terms/pallas_call | solution.py:257
  69.4 5.2 %collective-permute-done.11.refs_4_ = bf16[2,128,1024]{2,1,0:T(8,128)(2,1)S(1)} collective-permute-done((bf16[2,128,1024]{2,1,0:T(8,128)(2,1)}, bf16[2,128,1024]{2,1,0:T(8,128)(2,1)S(1)}, u32[]{:S(2)}, u32[]{:S(2)}) %collective-permute-start.11) | collective-permute-done | bytes 524320 | tf_op jit(solution)/shard_map/ppermute | solution.py:542
  74.8 1.1 collective-permute-done.10.refs_3_
  75.9 0.8 collective-permute-start.13
  76.7 8.7 %current_and_hidden_grad_terms.6 = (f32[2,128,1024]{2,1,0:T(8,128)}, f32[2,64,1024]{2,1,0:T(8,128)}, f32[2,64,1024]{2,1,0:T(8,128)}, s16[2,2,64,1024]{3,2,1,0:T(...) custom-call(s32[129]{0:T(256)} %get-tuple-element.69.up_list.refs_0_, ...), custom_call_target="tpu_custom_call" | custom-call | flops 536870912 | bytes 16777216 | tf_op jit(solution)/shard_map/current_and_hidden_grad_terms/pallas_call | solution.py:224
  85.4 1.0 collective-permute-start.15
  86.5 1.2 collective-permute-start.16
  87.7 3.8 %spiking_and_surrogate.5.refs_2_ = bf16[2,128,1024]{2,1,0:T(8,128)(2,1)} custom-call(f32[2,128,1024]{2,1,0:T(8,128)} %get-tuple-element.91.own, s16[2,2,64,1024]{3,2,1,0:T(8,128)(2,1)} %copy-done.8, s16[2,2,64,1024]{3,2,1,0:T(8,128)(2,1)} %copy-done.9, s16[2,64,1024]{2,1,0:T(8,128)(2,1)} %copy-done.40, s16[2,64,1024]{2,1,0:T(8,128)(2,1)} %copy-done.37, ...), custom_call_target="tpu_custom_call" | custom-call | tf_op jit(solution)/shard_map/spiking_and_surrogate/pallas_call | solution.py:309
  91.5 0.9 collective-permute-start.20
  92.3 1.0 collective-permute-start.19
  93.3 8.6 %output_and_input_grad_terms.4 = (f32[2,128,2048]{2,1,0:T(8,128)}, bf16[2,4,128,1024]{3,2,1,0:T(8,128)(2,1)}) custom-call(s32[129]{0:T(256)} %get-tuple-element.69.up_list.refs_0_, s32[129]{0:T(256)} %get-tuple-element.70.down_list.refs_1_, bf16[2,128,1024]{2,1,0:T(8,128)(2,1)} %spiking_and_surrogate.4.refs_2_, bf16[2,128,1024]{2,1,0:T(8,128)(2,1)} %copy-done.17, ...), custom_call_target="tpu_custom_call" | custom-call | flops 536870912 | bytes 16777216 | tf_op jit(solution)/shard_map/output_and_input_grad_terms/pallas_call | solution.py:373
  103.0 3.1 %relayed_terms.6 = (s16[2,64,1024]{2,1,0:T(8,128)(2,1)}, s16[2,64,1024]{2,1,0:T(8,128)(2,1)}) custom-call(f32[2,64,1024]{2,1,0:T(8,128)} %get-tuple-element.98.keep_a, f32[2,64,1024]{2,1,0:T(8,128)} %get-tuple-element.99.keep_b, s16[2,2,64,1024]{3,2,1,0:T(8,128)(2,1)} %copy-done.10, s16[2,2,64,1024]{3,2,1,0:T(8,128)(2,1)} %copy-done.11), custom_call_target="tpu_custom_call" | custom-call | tf_op jit(solution)/shard_map/relayed_terms/pallas_call | solution.py:257
  106.8 1.6 collective-permute-start.17
  108.4 1.0 collective-permute-done.20.refs_4_
  110.0 1.2 collective-permute-start.22
  111.2 1.0 copy-done.26
  112.2 8.5 %current_and_hidden_grad_terms.7 = (f32[2,128,1024]{2,1,0:T(8,128)}, f32[2,64,1024]{2,1,0:T(8,128)}, f32[2,64,1024]{2,1,0:T(8,128)}, s16[2,2,64,1024]{3,2,1,0:T(...) custom-call(s32[129]{0:T(256)} %get-tuple-element.69.up_list.refs_0_, ...), custom_call_target="tpu_custom_call" | custom-call | flops 536870912 | bytes 16777216 | tf_op jit(solution)/shard_map/current_and_hidden_grad_terms/pallas_call | solution.py:224
  122.2 3.8 %spiking_and_surrogate.6.refs_2_ = bf16[2,128,1024]{2,1,0:T(8,128)(2,1)} custom-call(f32[2,128,1024]{2,1,0:T(8,128)} %get-tuple-element.105.own, s16[2,2,64,1024]{3,2,1,0:T(8,128)(2,1)} %copy-done.10, s16[2,2,64,1024]{3,2,1,0:T(8,128)(2,1)} %copy-done.11, s16[2,64,1024]{2,1,0:T(8,128)(2,1)} %copy-done.41, s16[2,64,1024]{2,1,0:T(8,128)(2,1)} %copy-done.39, ...), custom_call_target="tpu_custom_call" | custom-call | tf_op jit(solution)/shard_map/spiking_and_surrogate/pallas_call | solution.py:309
  127.4 8.3 %output_and_input_grad_terms.5 = (bf16[2,128,2048]{2,1,0:T(8,128)(2,1)}, bf16[2,4,128,1024]{3,2,1,0:T(8,128)(2,1)}) custom-call(s32[129]{0:T(256)} %get-tuple-element.69.up_list.refs_0_, s32[129]{0:T(256)} %get-tuple-element.70.down_list.refs_1_, bf16[2,128,1024]{2,1,0:T(8,128)(2,1)} %spiking_and_surrogate.5.refs_2_, bf16[2,128,1024]{2,1,0:T(8,128)(2,1)} %copy-done.21, ...), custom_call_target="tpu_custom_call" | custom-call | flops 536870912 | bytes 16777216 | tf_op jit(solution)/shard_map/output_and_input_grad_terms/pallas_call | solution.py:373
  135.7 4.8 %collective-permute-start.31 = (bf16[2,128,2048]{2,1,0:T(8,128)(2,1)}, bf16[2,128,2048]{2,1,0:T(8,128)(2,1)S(1)}, u32[]{:S(2)}, u32[]{:S(2)}) collective-permute-start(bf16[2,128,2048]{2,1,0:T(8,128)(2,1)} %get-tuple-element.118), channel_id=1, source_target_pairs={{0,8},{8,12},{12,4},{4,0},{1,9},{9,13},{13,5},{5,1},{2,10},{10,14}... | collective-permute-start | bytes 3145736 | tf_op jit(solution)/shard_map/ppermute | solution.py:552
  140.8 2.9 %collective-permute-start.24 = (s16[2,2,64,1024]{3,2,1,0:T(8,128)(2,1)S(1)}, s16[2,2,64,1024]{3,2,1,0:T(8,128)(2,1)S(1)}, u32[]{:S(2)}, u32[]{:S(2)}) collective-permute-start(s16[2,2,64,1024]{3,2,1,0:T(8,128)(2,1)S(1)} %copy-done.45), channel_id=1, source_target_pairs={{0,1},{1,0},{2,3},{3,2},{4,5},{5,4},{6,7},{7,6},{8,9},{9,8},{10,11... | collective-permute-start | bytes 1572872 | tf_op jit(solution)/shard_map/ppermute | solution.py:542
  143.8 0.8 collective-permute-start.27
  144.6 9.7 %collective-permute-done.23.near_y = s16[2,2,64,1024]{3,2,1,0:T(8,128)(2,1)S(1)} collective-permute-done((s16[2,2,64,1024]{3,2,1,0:T(8,128)(2,1)S(1)}, s16[2,2,64,1024]{3,2,1,0:T(8,128)(2,1)S(1)}, u32[]{:S(2)}, u32[]{:S(2)}) %collective-permute-start.23) | collective-permute-done | bytes 524320 | tf_op jit(solution)/shard_map/ppermute | solution.py:542
  154.3 1.9 collective-permute-done.24.near_x
  157.0 3.1 %relayed_terms.7 = (s16[2,64,1024]{2,1,0:T(8,128)(2,1)}, s16[2,64,1024]{2,1,0:T(8,128)(2,1)}) custom-call(f32[2,64,1024]{2,1,0:T(8,128)} %get-tuple-element.110.keep_a, f32[2,64,1024]{2,1,0:T(8,128)} %get-tuple-element.111.keep_b, s16[2,2,64,1024]{3,2,1,0:T(8,128)(2,1)} %copy-done.14, s16[2,2,64,1024]{3,2,1,0:T(8,128)(2,1)} %copy-done.15), custom_call_target="tpu_custom_call" | custom-call | tf_op jit(solution)/shard_map/relayed_terms/pallas_call | solution.py:257
  160.1 2.4 collective-permute-start.25
  163.0 1.1 collective-permute-start.29
  164.4 2.2 collective-permute-start.30
  166.6 2.9 %collective-permute-done.26.late_b = s16[2,64,1024]{2,1,0:T(8,128)(2,1)S(1)} collective-permute-done((s16[2,64,1024]{2,1,0:T(8,128)(2,1)}, s16[2,64,1024]{2,1,0:T(8,128)(2,1)S(1)}, u32[]{:S(2)}, u32[]{:S(2)}) %collective-permute-start.26) | collective-permute-done | bytes 262176 | tf_op jit(solution)/shard_map/ppermute | solution.py:542
  171.0 3.7 %spiking_and_surrogate.7.refs_2_ = bf16[2,128,1024]{2,1,0:T(8,128)(2,1)} custom-call(f32[2,128,1024]{2,1,0:T(8,128)} %get-tuple-element.115.own, s16[2,2,64,1024]{3,2,1,0:T(8,128)(2,1)} %copy-done.14, s16[2,2,64,1024]{3,2,1,0:T(8,128)(2,1)} %copy-done.15, s16[2,64,1024]{2,1,0:T(8,128)(2,1)} %copy-done.43, s16[2,64,1024]{2,1,0:T(8,128)(2,1)} %copy-done.42, ...), custom_call_target="tpu_custom_call" | custom-call | tf_op jit(solution)/shard_map/spiking_and_surrogate/pallas_call | solution.py:309
  174.7 1.4 collective-permute-start.33
  176.1 1.9 collective-permute-start.32
  178.7 1.0 copy-done.28
  179.7 8.8 %output_and_input_grad_terms.6 = (bf16[2,128,2048]{2,1,0:T(8,128)(2,1)}, bf16[2,4,128,1024]{3,2,1,0:T(8,128)(2,1)}) custom-call(s32[129]{0:T(256)} %get-tuple-element.69.up_list.refs_0_, s32[129]{0:T(256)} %get-tuple-element.70.down_list.refs_1_, bf16[2,128,1024]{2,1,0:T(8,128)(2,1)} %spiking_and_surrogate.6.refs_2_, bf16[2,128,1024]{2,1,0:T(8,128)(2,1)} %copy-done.23, ...), custom_call_target="tpu_custom_call" | custom-call | flops 536870912 | bytes 16777216 | tf_op jit(solution)/shard_map/output_and_input_grad_terms/pallas_call | solution.py:373
  188.5 4.8 %collective-permute-start.36 = (bf16[2,128,2048]{2,1,0:T(8,128)(2,1)}, bf16[2,128,2048]{2,1,0:T(8,128)(2,1)}, u32[]{:S(2)}, u32[]{:S(2)}) collective-permute-start(bf16[2,128,2048]{2,1,0:T(8,128)(2,1)} %get-tuple-element.123), channel_id=1, source_target_pairs={{0,8},{8,12},{12,4},{4,0},{1,9},{9,13},{13,5},{5,1},{2,10},{10,14}... | collective-permute-start | bytes 3145736 | tf_op jit(solution)/shard_map/ppermute | solution.py:552
  194.4 8.3 %collective-permute-done.34.refs_5_ = bf16[2,64,1024]{2,1,0:T(8,128)(2,1)S(1)} collective-permute-done((bf16[2,64,1024]{2,1,0:T(8,128)(2,1)S(1)}, bf16[2,64,1024]{2,1,0:T(8,128)(2,1)S(1)}, u32[]{:S(2)}, u32[]{:S(2)}) %collective-permute-start.34) | collective-permute-done | bytes 262176 | tf_op jit(solution)/shard_map/ppermute | solution.py:542
  202.7 1.0 collective-permute-start.35
  203.7 11.8 %zero_weight_grads.1 = (bf16[2048,4096]{1,0:T(8,128)(2,1)}, bf16[4096,2048]{1,0:T(8,128)(2,1)}) custom-call(s32[2]{0:T(128)} %pad_add_fusion.place), custom_call_target="tpu_custom_call" | custom-call | bytes 33554432 | tf_op jit(solution)/shard_map/zero_weight_grads/pallas_call | solution.py:410
  216.3 8.7 %output_and_input_grad_terms.7 = (bf16[2,128,2048]{2,1,0:T(8,128)(2,1)}, bf16[2,4,128,1024]{3,2,1,0:T(8,128)(2,1)}) custom-call(s32[129]{0:T(256)} %get-tuple-element.69.up_list.refs_0_, s32[129]{0:T(256)} %get-tuple-element.70.down_list.refs_1_, bf16[2,128,1024]{2,1,0:T(8,128)(2,1)} %spiking_and_surrogate.7.refs_2_, bf16[2,128,1024]{2,1,0:T(8,128)(2,1)} %copy-done.20, ...), custom_call_target="tpu_custom_call" | custom-call | flops 536870912 | bytes 16777216 | tf_op jit(solution)/shard_map/output_and_input_grad_terms/pallas_call | solution.py:373
  225.7 1.6 collective-permute-start.45
  227.3 6.6 %collective-permute-done.44.refs_17_ = bf16[2,2048,128]{2,1,0:T(8,128)(2,1)S(1)} collective-permute-done((bf16[2,2048,128]{2,1,0:T(8,128)(2,1)}, bf16[2,2048,128]{2,1,0:T(8,128)(2,1)S(1)}, u32[]{:S(2)}, u32[]{:S(2)}) %collective-permute-start.44) | collective-permute-done | bytes 1048608 | tf_op jit(solution)/shard_map/ppermute | solution.py:546
  233.9 1.4 copy-done.5
  235.3 1.3 copy-done.6
  236.6 16.3 %weight_grads.1 = (bf16[2048,4096]{1,0:T(8,128)(2,1)}, bf16[4096,2048]{1,0:T(8,128)(2,1)}) custom-call(s32[129]{0:T(256)} %get-tuple-element.69.up_list.refs_0_, s32[129]{0:T(256)} %get-tuple-element.70.down_list.refs_1_, bf16[2,4,128,1024]{3,2,1,0:T(8,128)(2,1)} %get-tuple-element.95.refs_2_, ...), custom_call_target="tpu_custom_call", output_to_operand_aliasing={{0}: (18, {}), {1}: (19, {})} | custom-call | flops 4294967296 | bytes 33554432 | tf_op jit(solution)/shard_map/weight_grads/pallas_call | solution.py:512
  253.3 1.0 slice_bitcast_fusion
  (155 shorter events, 18.9 us)
Async XLA Ops:
  2.0 26.5 %collective-permute-start = (bf16[2,128,2048]{2,1,0:T(8,128)(2,1)S(1)}, bf16[2,128,2048]{2,1,0:T(8,128)(2,1)S(1)}, u32[]{:S(2)}, u32[]{:S(2)}) collective-permute-start(bf16[2,128,2048]{2,1,0:T(8,128)(2,1)S(1)} %pad_maximum_fusion.left), channel_id=1, source_target_pairs={{0,8},{8,12},{12,4},{4,0},{1,9},{9,13},{13,5},{5,1},{2,10},{10,14}... | collective-permute-start | bytes 3145736 | tf_op jit(solution)/shard_map/ppermute | solution.py:552
  18.8 13.7 %collective-permute-start.1 = (s16[2,2,64,1024]{3,2,1,0:T(8,128)(2,1)}, s16[2,2,64,1024]{3,2,1,0:T(8,128)(2,1)S(1)}, u32[]{:S(2)}, u32[]{:S(2)}) collective-permute-start(s16[2,2,64,1024]{3,2,1,0:T(8,128)(2,1)} %get-tuple-element.75), channel_id=1, source_target_pairs={{0,2},{1,3},{2,0},{3,1},{4,6},{5,7},{6,4},{7,5},{8,10},{9,11},{10,... | collective-permute-start | bytes 1572872 | tf_op jit(solution)/shard_map/ppermute | solution.py:542
  20.1 13.5 %collective-permute-start.2 = (s16[2,2,64,1024]{3,2,1,0:T(8,128)(2,1)}, s16[2,2,64,1024]{3,2,1,0:T(8,128)(2,1)S(1)}, u32[]{:S(2)}, u32[]{:S(2)}) collective-permute-start(s16[2,2,64,1024]{3,2,1,0:T(8,128)(2,1)} %get-tuple-element.76), channel_id=1, source_target_pairs={{0,1},{1,0},{2,3},{3,2},{4,5},{5,4},{6,7},{7,6},{8,9},{9,8},{10,11... | collective-permute-start | bytes 1572872 | tf_op jit(solution)/shard_map/ppermute | solution.py:542
  28.5 11.2 %copy-start.27 = (bf16[2,128,2048]{2,1,0:T(8,128)(2,1)}, bf16[2,128,2048]{2,1,0:T(8,128)(2,1)S(1)}, u32[]{:S(2)}) copy-start(bf16[2,128,2048]{2,1,0:T(8,128)(2,1)S(1)} %collective-permute-done.left) | copy-start | bytes 3145732
  28.5 29.5 %collective-permute-start.5 = (bf16[2,128,2048]{2,1,0:T(8,128)(2,1)S(1)}, bf16[2,128,2048]{2,1,0:T(8,128)(2,1)S(1)}, u32[]{:S(2)}, u32[]{:S(2)}) collective-permute-start(bf16[2,128,2048]{2,1,0:T(8,128)(2,1)S(1)} %collective-permute-done.left), channel_id=1, source_target_pairs={{0,8},{8,12},{12,4},{4,0},{1,9},{9,13},{13,5},{5,1},{2,10},{10,14}... | collective-permute-start | bytes 3145736 | tf_op jit(solution)/shard_map/ppermute | solution.py:552
  37.5 14.0 %collective-permute-start.4 = (s16[2,64,1024]{2,1,0:T(8,128)(2,1)}, s16[2,64,1024]{2,1,0:T(8,128)(2,1)S(1)}, u32[]{:S(2)}, u32[]{:S(2)}) collective-permute-start(s16[2,64,1024]{2,1,0:T(8,128)(2,1)} %get-tuple-element.81), channel_id=1, source_target_pairs={{0,2},{1,3},{2,0},{3,1},{4,6},{5,7},{6,4},{7,5},{8,10},{9,11},{10,... | collective-permute-start | bytes 786440 | tf_op jit(solution)/shard_map/ppermute | solution.py:542
  38.1 13.4 %collective-permute-start.3 = (s16[2,64,1024]{2,1,0:T(8,128)(2,1)}, s16[2,64,1024]{2,1,0:T(8,128)(2,1)}, u32[]{:S(2)}, u32[]{:S(2)}) collective-permute-start(s16[2,64,1024]{2,1,0:T(8,128)(2,1)} %get-tuple-element.77), channel_id=1, source_target_pairs={{0,1},{1,0},{2,3},{3,2},{4,5},{5,4},{6,7},{7,6},{8,9},{9,8},{10,11... | collective-permute-start | bytes 786440 | tf_op jit(solution)/shard_map/ppermute | solution.py:542
  48.1 15.1 %collective-permute-start.6 = (s16[2,2,64,1024]{3,2,1,0:T(8,128)(2,1)}, s16[2,2,64,1024]{3,2,1,0:T(8,128)(2,1)S(1)}, u32[]{:S(2)}, u32[]{:S(2)}) collective-permute-start(s16[2,2,64,1024]{3,2,1,0:T(8,128)(2,1)} %get-tuple-element.86), channel_id=1, source_target_pairs={{0,2},{1,3},{2,0},{3,1},{4,6},{5,7},{6,4},{7,5},{8,10},{9,11},{10,... | collective-permute-start | bytes 1572872 | tf_op jit(solution)/shard_map/ppermute | solution.py:542
  49.5 15.1 %collective-permute-start.7 = (s16[2,2,64,1024]{3,2,1,0:T(8,128)(2,1)}, s16[2,2,64,1024]{3,2,1,0:T(8,128)(2,1)S(1)}, u32[]{:S(2)}, u32[]{:S(2)}) collective-permute-start(s16[2,2,64,1024]{3,2,1,0:T(8,128)(2,1)} %get-tuple-element.87), channel_id=1, source_target_pairs={{0,1},{1,0},{2,3},{3,2},{4,5},{5,4},{6,7},{7,6},{8,9},{9,8},{10,11... | collective-permute-start | bytes 1572872 | tf_op jit(solution)/shard_map/ppermute | solution.py:542
  55.9 18.6 %collective-permute-start.11 = (bf16[2,128,1024]{2,1,0:T(8,128)(2,1)}, bf16[2,128,1024]{2,1,0:T(8,128)(2,1)S(1)}, u32[]{:S(2)}, u32[]{:S(2)}) collective-permute-start(bf16[2,128,1024]{2,1,0:T(8,128)(2,1)} %spiking_and_surrogate.4.refs_2_), channel_id=1, source_target_pairs={{0,2},{1,3},{2,0},{3,1},{4,6},{5,7},{6,4},{7,5},{8,10},{9,11},{10,... | collective-permute-start | bytes 1572872 | tf_op jit(solution)/shard_map/ppermute | solution.py:542
  56.1 19.7 %collective-permute-start.10 = (bf16[2,128,1024]{2,1,0:T(8,128)(2,1)}, bf16[2,128,1024]{2,1,0:T(8,128)(2,1)S(1)}, u32[]{:S(2)}, u32[]{:S(2)}) collective-permute-start(bf16[2,128,1024]{2,1,0:T(8,128)(2,1)} %spiking_and_surrogate.4.refs_2_), channel_id=1, source_target_pairs={{0,1},{1,0},{2,3},{3,2},{4,5},{5,4},{6,7},{7,6},{8,9},{9,8},{10,11... | collective-permute-start | bytes 1572872 | tf_op jit(solution)/shard_map/ppermute | solution.py:542
  58.0 18.7 %copy-start.25 = (bf16[2,128,2048]{2,1,0:T(8,128)(2,1)}, bf16[2,128,2048]{2,1,0:T(8,128)(2,1)S(1)}, u32[]{:S(2)}) copy-start(bf16[2,128,2048]{2,1,0:T(8,128)(2,1)S(1)} %collective-permute-done.5.left) | copy-start | bytes 3145732
  58.0 53.2 %collective-permute-start.14 = (bf16[2,128,2048]{2,1,0:T(8,128)(2,1)S(1)}, bf16[2,128,2048]{2,1,0:T(8,128)(2,1)S(1)}, u32[]{:S(2)}, u32[]{:S(2)}) collective-permute-start(bf16[2,128,2048]{2,1,0:T(8,128)(2,1)S(1)} %collective-permute-done.5.left), channel_id=1, source_target_pairs={{0,8},{8,12},{12,4},{4,0},{1,9},{9,13},{13,5},{5,1},{2,10},{10,14}... | collective-permute-start | bytes 3145736 | tf_op jit(solution)/shard_map/ppermute | solution.py:552
  68.5 16.9 %collective-permute-start.9 = (s16[2,64,1024]{2,1,0:T(8,128)(2,1)}, s16[2,64,1024]{2,1,0:T(8,128)(2,1)S(1)}, u32[]{:S(2)}, u32[]{:S(2)}) collective-permute-start(s16[2,64,1024]{2,1,0:T(8,128)(2,1)} %get-tuple-element.92), channel_id=1, source_target_pairs={{0,2},{1,3},{2,0},{3,1},{4,6},{5,7},{6,4},{7,5},{8,10},{9,11},{10,... | collective-permute-start | bytes 786440 | tf_op jit(solution)/shard_map/ppermute | solution.py:542
  69.2 17.3 %collective-permute-start.8 = (s16[2,64,1024]{2,1,0:T(8,128)(2,1)}, s16[2,64,1024]{2,1,0:T(8,128)(2,1)S(1)}, u32[]{:S(2)}, u32[]{:S(2)}) collective-permute-start(s16[2,64,1024]{2,1,0:T(8,128)(2,1)} %get-tuple-element.88), channel_id=1, source_target_pairs={{0,1},{1,0},{2,3},{3,2},{4,5},{5,4},{6,7},{7,6},{8,9},{9,8},{10,11... | collective-permute-start | bytes 786440 | tf_op jit(solution)/shard_map/ppermute | solution.py:542
  74.5 10.9 %copy-start.16 = (bf16[2,128,1024]{2,1,0:T(8,128)(2,1)}, bf16[2,128,1024]{2,1,0:T(8,128)(2,1)S(1)}, u32[]{:S(2)}) copy-start(bf16[2,128,1024]{2,1,0:T(8,128)(2,1)S(1)} %collective-permute-done.11.refs_4_) | copy-start | bytes 1572868
  74.5 16.9 %collective-permute-start.12 = (bf16[2,64,1024]{2,1,0:T(8,128)(2,1)S(1)}, bf16[2,64,1024]{2,1,0:T(8,128)(2,1)S(1)}, u32[]{:S(2)}, u32[]{:S(2)}) collective-permute-start(bf16[2,64,1024]{2,1,0:T(8,128)(2,1)S(1)} %slice.42), channel_id=1, source_target_pairs={{0,1},{1,0},{2,3},{3,2},{4,5},{5,4},{6,7},{7,6},{8,9},{9,8},{10,11... | collective-permute-start | bytes 786440 | tf_op jit(solution)/shard_map/ppermute | solution.py:542
  75.8 9.6 %copy-start.17 = (bf16[2,128,1024]{2,1,0:T(8,128)(2,1)}, bf16[2,128,1024]{2,1,0:T(8,128)(2,1)S(1)}, u32[]{:S(2)}) copy-start(bf16[2,128,1024]{2,1,0:T(8,128)(2,1)S(1)} %collective-permute-done.10.refs_3_) | copy-start | bytes 1572868
  75.9 16.5 %collective-permute-start.13 = (bf16[2,64,1024]{2,1,0:T(8,128)(2,1)S(1)}, bf16[2,64,1024]{2,1,0:T(8,128)(2,1)S(1)}, u32[]{:S(2)}, u32[]{:S(2)}) collective-permute-start(bf16[2,64,1024]{2,1,0:T(8,128)(2,1)S(1)} %slice.43), channel_id=1, source_target_pairs={{0,2},{1,3},{2,0},{3,1},{4,6},{5,7},{6,4},{7,5},{8,10},{9,11},{10,... | collective-permute-start | bytes 786440 | tf_op jit(solution)/shard_map/ppermute | solution.py:542
  85.4 16.6 %collective-permute-start.15 = (s16[2,2,64,1024]{3,2,1,0:T(8,128)(2,1)}, s16[2,2,64,1024]{3,2,1,0:T(8,128)(2,1)S(1)}, u32[]{:S(2)}, u32[]{:S(2)}) collective-permute-start(s16[2,2,64,1024]{3,2,1,0:T(8,128)(2,1)} %get-tuple-element.100), channel_id=1, source_target_pairs={{0,2},{1,3},{2,0},{3,1},{4,6},{5,7},{6,4},{7,5},{8,10},{9,11},{10,... | collective-permute-start | bytes 1572872 | tf_op jit(solution)/shard_map/ppermute | solution.py:542
  86.5 15.6 %collective-permute-start.16 = (s16[2,2,64,1024]{3,2,1,0:T(8,128)(2,1)}, s16[2,2,64,1024]{3,2,1,0:T(8,128)(2,1)S(1)}, u32[]{:S(2)}, u32[]{:S(2)}) collective-permute-start(s16[2,2,64,1024]{3,2,1,0:T(8,128)(2,1)} %get-tuple-element.101), channel_id=1, source_target_pairs={{0,1},{1,0},{2,3},{3,2},{4,5},{5,4},{6,7},{7,6},{8,9},{9,8},{10,11... | collective-permute-start | bytes 1572872 | tf_op jit(solution)/shard_map/ppermute | solution.py:542
  91.5 17.9 %collective-permute-start.20 = (bf16[2,128,1024]{2,1,0:T(8,128)(2,1)}, bf16[2,128,1024]{2,1,0:T(8,128)(2,1)S(1)}, u32[]{:S(2)}, u32[]{:S(2)}) collective-permute-start(bf16[2,128,1024]{2,1,0:T(8,128)(2,1)} %spiking_and_surrogate.5.refs_2_), channel_id=1, source_target_pairs={{0,2},{1,3},{2,0},{3,1},{4,6},{5,7},{6,4},{7,5},{8,10},{9,11},{10,... | collective-permute-start | bytes 1572872 | tf_op jit(solution)/shard_map/ppermute | solution.py:542
  92.3 17.6 %collective-permute-start.19 = (bf16[2,128,1024]{2,1,0:T(8,128)(2,1)}, bf16[2,128,1024]{2,1,0:T(8,128)(2,1)S(1)}, u32[]{:S(2)}, u32[]{:S(2)}) collective-permute-start(bf16[2,128,1024]{2,1,0:T(8,128)(2,1)} %spiking_and_surrogate.5.refs_2_), channel_id=1, source_target_pairs={{0,1},{1,0},{2,3},{3,2},{4,5},{5,4},{6,7},{7,6},{8,9},{9,8},{10,11... | collective-permute-start | bytes 1572872 | tf_op jit(solution)/shard_map/ppermute | solution.py:542
  106.0 14.7 %collective-permute-start.18 = (s16[2,64,1024]{2,1,0:T(8,128)(2,1)}, s16[2,64,1024]{2,1,0:T(8,128)(2,1)S(1)}, u32[]{:S(2)}, u32[]{:S(2)}) collective-permute-start(s16[2,64,1024]{2,1,0:T(8,128)(2,1)} %get-tuple-element.106), channel_id=1, source_target_pairs={{0,2},{1,3},{2,0},{3,1},{4,6},{5,7},{6,4},{7,5},{8,10},{9,11},{10,... | collective-permute-start | bytes 786440 | tf_op jit(solution)/shard_map/ppermute | solution.py:542
  106.8 14.0 %collective-permute-start.17 = (s16[2,64,1024]{2,1,0:T(8,128)(2,1)}, s16[2,64,1024]{2,1,0:T(8,128)(2,1)S(1)}, u32[]{:S(2)}, u32[]{:S(2)}) collective-permute-start(s16[2,64,1024]{2,1,0:T(8,128)(2,1)} %get-tuple-element.102), channel_id=1, source_target_pairs={{0,1},{1,0},{2,3},{3,2},{4,5},{5,4},{6,7},{7,6},{8,9},{9,8},{10,11... | collective-permute-start | bytes 786440 | tf_op jit(solution)/shard_map/ppermute | solution.py:542
  109.4 11.3 %copy-start.18 = (bf16[2,128,1024]{2,1,0:T(8,128)(2,1)}, bf16[2,128,1024]{2,1,0:T(8,128)(2,1)S(1)}, u32[]{:S(2)}) copy-start(bf16[2,128,1024]{2,1,0:T(8,128)(2,1)S(1)} %collective-permute-done.20.refs_4_) | copy-start | bytes 1572868
  109.4 16.6 %collective-permute-start.21 = (bf16[2,64,1024]{2,1,0:T(8,128)(2,1)S(1)}, bf16[2,64,1024]{2,1,0:T(8,128)(2,1)S(1)}, u32[]{:S(2)}, u32[]{:S(2)}) collective-permute-start(bf16[2,64,1024]{2,1,0:T(8,128)(2,1)S(1)} %slice.44), channel_id=1, source_target_pairs={{0,1},{1,0},{2,3},{3,2},{4,5},{5,4},{6,7},{7,6},{8,9},{9,8},{10,11... | collective-permute-start | bytes 786440 | tf_op jit(solution)/shard_map/ppermute | solution.py:542
  110.0 10.8 %copy-start.21 = (bf16[2,128,1024]{2,1,0:T(8,128)(2,1)}, bf16[2,128,1024]{2,1,0:T(8,128)(2,1)S(1)}, u32[]{:S(2)}) copy-start(bf16[2,128,1024]{2,1,0:T(8,128)(2,1)S(1)} %collective-permute-done.19.refs_3_) | copy-start | bytes 1572868
  110.0 16.0 %collective-permute-start.22 = (bf16[2,64,1024]{2,1,0:T(8,128)(2,1)S(1)}, bf16[2,64,1024]{2,1,0:T(8,128)(2,1)S(1)}, u32[]{:S(2)}, u32[]{:S(2)}) collective-permute-start(bf16[2,64,1024]{2,1,0:T(8,128)(2,1)S(1)} %slice.45), channel_id=1, source_target_pairs={{0,2},{1,3},{2,0},{3,1},{4,6},{5,7},{6,4},{7,5},{8,10},{9,11},{10,... | collective-permute-start | bytes 786440 | tf_op jit(solution)/shard_map/ppermute | solution.py:542
  126.0 14.6 %copy-start.46 = (s16[2,2,64,1024]{3,2,1,0:T(8,128)(2,1)S(1)}, s16[2,2,64,1024]{3,2,1,0:T(8,128)(2,1)}, u32[]{:S(2)}) copy-start(s16[2,2,64,1024]{3,2,1,0:T(8,128)(2,1)} %get-tuple-element.112) | copy-start | bytes 1572868
  126.0 14.9 %copy-start.45 = (s16[2,2,64,1024]{3,2,1,0:T(8,128)(2,1)S(1)}, s16[2,2,64,1024]{3,2,1,0:T(8,128)(2,1)}, u32[]{:S(2)}) copy-start(s16[2,2,64,1024]{3,2,1,0:T(8,128)(2,1)} %get-tuple-element.113) | copy-start | bytes 1572868
  126.0 17.7 %copy-start.1 = (bf16[2,128,1024]{2,1,0:T(8,128)(2,1)S(1)}, bf16[2,128,1024]{2,1,0:T(8,128)(2,1)}, u32[]{:S(2)}) copy-start(bf16[2,128,1024]{2,1,0:T(8,128)(2,1)} %spiking_and_surrogate.6.refs_2_) | copy-start | bytes 1572868
  135.7 42.2 %collective-permute-start.31 = (bf16[2,128,2048]{2,1,0:T(8,128)(2,1)}, bf16[2,128,2048]{2,1,0:T(8,128)(2,1)S(1)}, u32[]{:S(2)}, u32[]{:S(2)}) collective-permute-start(bf16[2,128,2048]{2,1,0:T(8,128)(2,1)} %get-tuple-element.118), channel_id=1, source_target_pairs={{0,8},{8,12},{12,4},{4,0},{1,9},{9,13},{13,5},{5,1},{2,10},{10,14}... | collective-permute-start | bytes 3145736 | tf_op jit(solution)/shard_map/ppermute | solution.py:552
  140.5 13.8 %collective-permute-start.23 = (s16[2,2,64,1024]{3,2,1,0:T(8,128)(2,1)S(1)}, s16[2,2,64,1024]{3,2,1,0:T(8,128)(2,1)S(1)}, u32[]{:S(2)}, u32[]{:S(2)}) collective-permute-start(s16[2,2,64,1024]{3,2,1,0:T(8,128)(2,1)S(1)} %copy-done.46), channel_id=1, source_target_pairs={{0,2},{1,3},{2,0},{3,1},{4,6},{5,7},{6,4},{7,5},{8,10},{9,11},{10,... | collective-permute-start | bytes 1572872 | tf_op jit(solution)/shard_map/ppermute | solution.py:542
  140.8 15.3 %collective-permute-start.24 = (s16[2,2,64,1024]{3,2,1,0:T(8,128)(2,1)S(1)}, s16[2,2,64,1024]{3,2,1,0:T(8,128)(2,1)S(1)}, u32[]{:S(2)}, u32[]{:S(2)}) collective-permute-start(s16[2,2,64,1024]{3,2,1,0:T(8,128)(2,1)S(1)} %copy-done.45), channel_id=1, source_target_pairs={{0,1},{1,0},{2,3},{3,2},{4,5},{5,4},{6,7},{7,6},{8,9},{9,8},{10,11... | collective-permute-start | bytes 1572872 | tf_op jit(solution)/shard_map/ppermute | solution.py:542
  143.7 19.3 %collective-permute-start.28 = (bf16[2,128,1024]{2,1,0:T(8,128)(2,1)S(1)}, bf16[2,128,1024]{2,1,0:T(8,128)(2,1)S(1)}, u32[]{:S(2)}, u32[]{:S(2)}) collective-permute-start(bf16[2,128,1024]{2,1,0:T(8,128)(2,1)S(1)} %copy-done.1), channel_id=1, source_target_pairs={{0,2},{1,3},{2,0},{3,1},{4,6},{5,7},{6,4},{7,5},{8,10},{9,11},{10,... | collective-permute-start | bytes 1572872 | tf_op jit(solution)/shard_map/ppermute | solution.py:542
  143.8 20.6 %collective-permute-start.27 = (bf16[2,128,1024]{2,1,0:T(8,128)(2,1)S(1)}, bf16[2,128,1024]{2,1,0:T(8,128)(2,1)S(1)}, u32[]{:S(2)}, u32[]{:S(2)}) collective-permute-start(bf16[2,128,1024]{2,1,0:T(8,128)(2,1)S(1)} %copy-done.1), channel_id=1, source_target_pairs={{0,1},{1,0},{2,3},{3,2},{4,5},{5,4},{6,7},{7,6},{8,9},{9,8},{10,11... | collective-permute-start | bytes 1572872 | tf_op jit(solution)/shard_map/ppermute | solution.py:542
  160.1 9.5 %collective-permute-start.26 = (s16[2,64,1024]{2,1,0:T(8,128)(2,1)}, s16[2,64,1024]{2,1,0:T(8,128)(2,1)S(1)}, u32[]{:S(2)}, u32[]{:S(2)}) collective-permute-start(s16[2,64,1024]{2,1,0:T(8,128)(2,1)} %get-tuple-element.116), channel_id=1, source_target_pairs={{0,2},{1,3},{2,0},{3,1},{4,6},{5,7},{6,4},{7,5},{8,10},{9,11},{10,... | collective-permute-start | bytes 786440 | tf_op jit(solution)/shard_map/ppermute | solution.py:542
  160.1 9.9 %collective-permute-start.25 = (s16[2,64,1024]{2,1,0:T(8,128)(2,1)}, s16[2,64,1024]{2,1,0:T(8,128)(2,1)S(1)}, u32[]{:S(2)}, u32[]{:S(2)}) collective-permute-start(s16[2,64,1024]{2,1,0:T(8,128)(2,1)} %get-tuple-element.114), channel_id=1, source_target_pairs={{0,1},{1,0},{2,3},{3,2},{4,5},{5,4},{6,7},{7,6},{8,9},{9,8},{10,11... | collective-permute-start | bytes 786440 | tf_op jit(solution)/shard_map/ppermute | solution.py:542
  163.0 11.7 %copy-start.22 = (bf16[2,128,1024]{2,1,0:T(8,128)(2,1)}, bf16[2,128,1024]{2,1,0:T(8,128)(2,1)S(1)}, u32[]{:S(2)}) copy-start(bf16[2,128,1024]{2,1,0:T(8,128)(2,1)S(1)} %collective-permute-done.28.refs_4_) | copy-start | bytes 1572868
  163.0 15.0 %collective-permute-start.29 = (bf16[2,64,1024]{2,1,0:T(8,128)(2,1)S(1)}, bf16[2,64,1024]{2,1,0:T(8,128)(2,1)S(1)}, u32[]{:S(2)}, u32[]{:S(2)}) collective-permute-start(bf16[2,64,1024]{2,1,0:T(8,128)(2,1)S(1)} %slice.46), channel_id=1, source_target_pairs={{0,1},{1,0},{2,3},{3,2},{4,5},{5,4},{6,7},{7,6},{8,9},{9,8},{10,11... | collective-permute-start | bytes 786440 | tf_op jit(solution)/shard_map/ppermute | solution.py:542
  164.4 13.6 %copy-start.23 = (bf16[2,128,1024]{2,1,0:T(8,128)(2,1)}, bf16[2,128,1024]{2,1,0:T(8,128)(2,1)S(1)}, u32[]{:S(2)}) copy-start(bf16[2,128,1024]{2,1,0:T(8,128)(2,1)S(1)} %collective-permute-done.27.refs_3_) | copy-start | bytes 1572868
  164.4 13.5 %collective-permute-start.30 = (bf16[2,64,1024]{2,1,0:T(8,128)(2,1)S(1)}, bf16[2,64,1024]{2,1,0:T(8,128)(2,1)S(1)}, u32[]{:S(2)}, u32[]{:S(2)}) collective-permute-start(bf16[2,64,1024]{2,1,0:T(8,128)(2,1)S(1)} %slice.47), channel_id=1, source_target_pairs={{0,2},{1,3},{2,0},{3,1},{4,6},{5,7},{6,4},{7,5},{8,10},{9,11},{10,... | collective-permute-start | bytes 786440 | tf_op jit(solution)/shard_map/ppermute | solution.py:542
  174.7 19.1 %copy-start.2 = (bf16[2,4,128,1024]{3,2,1,0:T(8,128)(2,1)S(1)}, bf16[2,4,128,1024]{3,2,1,0:T(8,128)(2,1)}, u32[]{:S(2)}) copy-start(bf16[2,4,128,1024]{3,2,1,0:T(8,128)(2,1)} %get-tuple-element.95.refs_2_) | copy-start | bytes 6291460
  174.7 41.0 %copy-start.3 = (bf16[2,4,128,1024]{3,2,1,0:T(8,128)(2,1)S(1)}, bf16[2,4,128,1024]{3,2,1,0:T(8,128)(2,1)}, u32[]{:S(2)}) copy-start(bf16[2,4,128,1024]{3,2,1,0:T(8,128)(2,1)} %get-tuple-element.108.refs_3_) | copy-start | bytes 6291460
  174.7 19.1 %collective-permute-start.33 = (bf16[2,128,1024]{2,1,0:T(8,128)(2,1)}, bf16[2,128,1024]{2,1,0:T(8,128)(2,1)S(1)}, u32[]{:S(2)}, u32[]{:S(2)}) collective-permute-start(bf16[2,128,1024]{2,1,0:T(8,128)(2,1)} %spiking_and_surrogate.7.refs_2_), channel_id=1, source_target_pairs={{0,2},{1,3},{2,0},{3,1},{4,6},{5,7},{6,4},{7,5},{8,10},{9,11},{10,... | collective-permute-start | bytes 1572872 | tf_op jit(solution)/shard_map/ppermute | solution.py:542
  176.1 17.8 %collective-permute-start.32 = (bf16[2,128,1024]{2,1,0:T(8,128)(2,1)}, bf16[2,128,1024]{2,1,0:T(8,128)(2,1)S(1)}, u32[]{:S(2)}, u32[]{:S(2)}) collective-permute-start(bf16[2,128,1024]{2,1,0:T(8,128)(2,1)} %spiking_and_surrogate.7.refs_2_), channel_id=1, source_target_pairs={{0,1},{1,0},{2,3},{3,2},{4,5},{5,4},{6,7},{7,6},{8,9},{9,8},{10,11... | collective-permute-start | bytes 1572872 | tf_op jit(solution)/shard_map/ppermute | solution.py:542
  188.5 27.2 %collective-permute-start.36 = (bf16[2,128,2048]{2,1,0:T(8,128)(2,1)}, bf16[2,128,2048]{2,1,0:T(8,128)(2,1)}, u32[]{:S(2)}, u32[]{:S(2)}) collective-permute-start(bf16[2,128,2048]{2,1,0:T(8,128)(2,1)} %get-tuple-element.123), channel_id=1, source_target_pairs={{0,8},{8,12},{12,4},{4,0},{1,9},{9,13},{13,5},{5,1},{2,10},{10,14}... | collective-permute-start | bytes 3145736 | tf_op jit(solution)/shard_map/ppermute | solution.py:552
  193.3 31.7 %collective-permute-start.41 = (bf16[2,2048,128]{2,1,0:T(8,128)(2,1)}, bf16[2,2048,128]{2,1,0:T(8,128)(2,1)}, u32[]{:S(2)}, u32[]{:S(2)}) collective-permute-start(bf16[2,2048,128]{2,1,0:T(8,128)(2,1)} %get-tuple-element.125.refs_10_), channel_id=1, source_target_pairs={{0,16},{16,0},{1,17},{17,1},{2,18},{18,2},{3,19},{19,3},{4,20},{20... | collective-permute-start | bytes 3145736 | tf_op jit(solution)/shard_map/ppermute | solution.py:546
  193.3 31.8 %collective-permute-start.42 = (bf16[2,2048,128]{2,1,0:T(8,128)(2,1)}, bf16[2,2048,128]{2,1,0:T(8,128)(2,1)}, u32[]{:S(2)}, u32[]{:S(2)}) collective-permute-start(bf16[2,2048,128]{2,1,0:T(8,128)(2,1)} %get-tuple-element.126.refs_11_), channel_id=1, source_target_pairs={{0,16},{16,0},{1,17},{17,1},{2,18},{18,2},{3,19},{19,3},{4,20},{20... | collective-permute-start | bytes 3145736 | tf_op jit(solution)/shard_map/ppermute | solution.py:546
  193.8 22.4 %copy-start.19 = (bf16[2,128,1024]{2,1,0:T(8,128)(2,1)}, bf16[2,128,1024]{2,1,0:T(8,128)(2,1)S(1)}, u32[]{:S(2)}) copy-start(bf16[2,128,1024]{2,1,0:T(8,128)(2,1)S(1)} %collective-permute-done.33.refs_4_) | copy-start | bytes 1572868
  193.8 31.8 %collective-permute-start.37 = (bf16[2,4,128,1024]{3,2,1,0:T(8,128)(2,1)S(1)}, bf16[2,4,128,1024]{3,2,1,0:T(8,128)(2,1)}, u32[]{:S(2)}, u32[]{:S(2)}) collective-permute-start(bf16[2,4,128,1024]{3,2,1,0:T(8,128)(2,1)S(1)} %copy-done.2), channel_id=1, source_target_pairs={{0,16},{16,0},{1,17},{17,1},{2,18},{18,2},{3,19},{19,3},{4,20},{20... | collective-permute-start | bytes 6291464 | tf_op jit(solution)/shard_map/ppermute | solution.py:546
  193.9 22.3 %copy-start.20 = (bf16[2,128,1024]{2,1,0:T(8,128)(2,1)}, bf16[2,128,1024]{2,1,0:T(8,128)(2,1)S(1)}, u32[]{:S(2)}) copy-start(bf16[2,128,1024]{2,1,0:T(8,128)(2,1)S(1)} %collective-permute-done.32.refs_3_) | copy-start | bytes 1572868
  193.9 8.8 %collective-permute-start.34 = (bf16[2,64,1024]{2,1,0:T(8,128)(2,1)S(1)}, bf16[2,64,1024]{2,1,0:T(8,128)(2,1)S(1)}, u32[]{:S(2)}, u32[]{:S(2)}) collective-permute-start(bf16[2,64,1024]{2,1,0:T(8,128)(2,1)S(1)} %slice.48), channel_id=1, source_target_pairs={{0,1},{1,0},{2,3},{3,2},{4,5},{5,4},{6,7},{7,6},{8,9},{9,8},{10,11... | collective-permute-start | bytes 786440 | tf_op jit(solution)/shard_map/ppermute | solution.py:542
  202.7 13.5 %copy-start.35 = (bf16[2,64,1024]{2,1,0:T(8,128)(2,1)}, bf16[2,64,1024]{2,1,0:T(8,128)(2,1)S(1)}, u32[]{:S(2)}) copy-start(bf16[2,64,1024]{2,1,0:T(8,128)(2,1)S(1)} %collective-permute-done.34.refs_5_) | copy-start | bytes 786436
  202.7 12.9 %collective-permute-start.35 = (bf16[2,64,1024]{2,1,0:T(8,128)(2,1)S(1)}, bf16[2,64,1024]{2,1,0:T(8,128)(2,1)S(1)}, u32[]{:S(2)}, u32[]{:S(2)}) collective-permute-start(bf16[2,64,1024]{2,1,0:T(8,128)(2,1)S(1)} %slice.49), channel_id=1, source_target_pairs={{0,2},{1,3},{2,0},{3,1},{4,6},{5,7},{6,4},{7,5},{8,10},{9,11},{10,... | collective-permute-start | bytes 786440 | tf_op jit(solution)/shard_map/ppermute | solution.py:542
  215.6 9.4 %copy-start.4 = (bf16[2,4,128,1024]{3,2,1,0:T(8,128)(2,1)S(1)}, bf16[2,4,128,1024]{3,2,1,0:T(8,128)(2,1)}, u32[]{:S(2)}) copy-start(bf16[2,4,128,1024]{3,2,1,0:T(8,128)(2,1)} %get-tuple-element.119.refs_4_) | copy-start | bytes 6291460
  215.6 10.0 %collective-permute-start.43 = (bf16[2,2048,128]{2,1,0:T(8,128)(2,1)}, bf16[2,2048,128]{2,1,0:T(8,128)(2,1)}, u32[]{:S(2)}, u32[]{:S(2)}) collective-permute-start(bf16[2,2048,128]{2,1,0:T(8,128)(2,1)} %get-tuple-element.127.refs_12_), channel_id=1, source_target_pairs={{0,16},{16,0},{1,17},{17,1},{2,18},{18,2},{3,19},{19,3},{4,20},{20... | collective-permute-start | bytes 3145736 | tf_op jit(solution)/shard_map/ppermute | solution.py:546
  215.7 18.2 %collective-permute-start.38 = (bf16[2,4,128,1024]{3,2,1,0:T(8,128)(2,1)S(1)}, bf16[2,4,128,1024]{3,2,1,0:T(8,128)(2,1)}, u32[]{:S(2)}, u32[]{:S(2)}) collective-permute-start(bf16[2,4,128,1024]{3,2,1,0:T(8,128)(2,1)S(1)} %copy-done.3), channel_id=1, source_target_pairs={{0,16},{16,0},{1,17},{17,1},{2,18},{18,2},{3,19},{19,3},{4,20},{20... | collective-permute-start | bytes 6291464 | tf_op jit(solution)/shard_map/ppermute | solution.py:546
  225.0 8.9 %collective-permute-start.39 = (bf16[2,4,128,1024]{3,2,1,0:T(8,128)(2,1)S(1)}, bf16[2,4,128,1024]{3,2,1,0:T(8,128)(2,1)S(1)}, u32[]{:S(2)}, u32[]{:S(2)}) collective-permute-start(bf16[2,4,128,1024]{3,2,1,0:T(8,128)(2,1)S(1)} %copy-done.4), channel_id=1, source_target_pairs={{0,16},{16,0},{1,17},{17,1},{2,18},{18,2},{3,19},{19,3},{4,20},{20... | collective-permute-start | bytes 6291464 | tf_op jit(solution)/shard_map/ppermute | solution.py:546
  225.1 10.2 %collective-permute-start.40 = (bf16[2,4,128,1024]{3,2,1,0:T(8,128)(2,1)}, bf16[2,4,128,1024]{3,2,1,0:T(8,128)(2,1)S(1)}, u32[]{:S(2)}, u32[]{:S(2)}) collective-permute-start(bf16[2,4,128,1024]{3,2,1,0:T(8,128)(2,1)} %get-tuple-element.124.refs_5_), channel_id=1, source_target_pairs={{0,16},{16,0},{1,17},{17,1},{2,18},{18,2},{3,19},{19,3},{4,20},{20... | collective-permute-start | bytes 6291464 | tf_op jit(solution)/shard_map/ppermute | solution.py:546
  225.6 8.4 %collective-permute-start.44 = (bf16[2,2048,128]{2,1,0:T(8,128)(2,1)}, bf16[2,2048,128]{2,1,0:T(8,128)(2,1)S(1)}, u32[]{:S(2)}, u32[]{:S(2)}) collective-permute-start(bf16[2,2048,128]{2,1,0:T(8,128)(2,1)} %get-tuple-element.128.refs_13_), channel_id=1, source_target_pairs={{0,16},{16,0},{1,17},{17,1},{2,18},{18,2},{3,19},{19,3},{4,20},{20... | collective-permute-start | bytes 3145736 | tf_op jit(solution)/shard_map/ppermute | solution.py:546
  225.7 27.3 %collective-permute-start.45 = (bf16[2,128,2048]{2,1,0:T(8,128)(2,1)}, bf16[2,128,2048]{2,1,0:T(8,128)(2,1)S(1)}, u32[]{:S(2)}, u32[]{:S(2)}) collective-permute-start(bf16[2,128,2048]{2,1,0:T(8,128)(2,1)} %get-tuple-element.132), channel_id=1, source_target_pairs={{0,8},{8,12},{12,4},{4,0},{1,9},{9,13},{13,5},{5,1},{2,10},{10,14}... | collective-permute-start | bytes 3145736 | tf_op jit(solution)/shard_map/ppermute | solution.py:552
  236.6 16.4 %copy-start.7 = (f32[2,128,2048]{2,1,0:T(8,128)S(1)}, f32[2,128,2048]{2,1,0:T(8,128)}, u32[]{:S(2)}) copy-start(f32[2,128,2048]{2,1,0:T(8,128)} %get-tuple-element.131) | copy-start | bytes 6291460
  (29 other events, 43.2 us)

commit v2 on v1

--- a/solution.py
+++ b/solution.py
@@ -13,12 +13,13 @@
 QUARTERS = 4
 LANES = 128
 SLOTS = 32
+RELAYS = {}
 STAGES = 4
 PIECES = 8
 CODE_UNIT = 2.0**-13
 LARGEST_INPUT = 6.0
 LARGEST_WEIGHT = 0.1875
-VMEM_LIMIT = 56 * 1024 * 1024
+VMEM_LIMIT = 63 * 1024 * 1024 + 768 * 1024
 
 
 spike_width = 1.0
@@ -26,6 +27,12 @@
 VMEM = pl.BlockSpec(memory_space=pltpu.VMEM)
 SMEM = pl.BlockSpec(memory_space=pltpu.SMEM)
 ANY = pl.BlockSpec(memory_space=pl.ANY)
+
+
+def cost(microseconds):
+    return pl.CostEstimate(
+        flops=0, bytes_accessed=int(microseconds * 3.69e6), transcendentals=0
+    )
 
 
 def params():
@@ -80,7 +87,7 @@
             up_list[up] = entry
             down_list[down] = entry
             up = up + mask_up[feature, unit]
-            down = down + mask_down[unit, feature]
+            down = down + mask_down[feature, unit]
         return up, down
 
     up, down = lax.fori_loop(0, groups, walk, (jnp.int32(0), jnp.int32(0)))
@@ -98,12 +105,15 @@
         out_specs=[SMEM] * 2,
         out_shape=[shape((size,), jnp.int32)] * 2,
         compiler_params=params(),
+        cost_estimate=cost(3),
         name="kept_blocks",
     )(place, mask_up, mask_down)
 
 
 def each_kept(lists, weights, held, sems, width, hidden_first, use, meanwhile):
+    kinds = range(len(lists))
     counts = [entries[entries.shape[0] - 1] for entries in lists]
+    longest = functools.reduce(jnp.maximum, counts)
 
     def copy(which, entry, slot):
         units = pl.ds(pl.multiple_of((entry >> 16) * width, width), width)
@@ -113,13 +123,16 @@
         return pltpu.make_async_copy(source, held[which].at[slot], sems.at[which, slot])
 
     def fetch(base):
-        for which in range(2):
-
-            def start(i, _, which=which):
-                copy(which, lists[which][base + i], i).start()
-                return 0
-
-            lax.fori_loop(0, jnp.clip(counts[which] - base, 0, SLOTS), start, 0)
+        def start(i, _):
+            for which in kinds:
+
+                @pl.when(base + i < counts[which])
+                def _():
+                    copy(which, lists[which][base + i], i).start()
+
+            return 0
+
+        lax.fori_loop(0, jnp.clip(longest - base, 0, SLOTS), start, 0)
 
     fetch(0)
     for slots in held:
@@ -134,37 +147,61 @@
         def _():
             fetch(base)
 
-        for which in range(2):
-
-            def finish(i, _, which=which):
-                copy(which, lists[which][base + i], i).wait()
-                return 0
-
-            lax.fori_loop(0, live[which], finish, 0)
-
         def work(i, _):
+            todo = []
             for t in range(2):
                 spot = i * 2 + t
-                for which in range(2):
+                for which in kinds:
                     real = spot < live[which]
                     entry = lists[which][jnp.where(real, base + spot, 0)]
                     slot = jnp.where(real, spot, SLOTS)
-                    use(which, (entry >> 8) & 255, entry & 255, held[which].at[slot])
+
+                    @pl.when(real)
+                    def _():
+                        copy(which, entry, spot).wait()
+
+                    todo.append((which, (entry >> 8) & 255, entry & 255, held[which].at[slot]))
+            for item in todo:
+                use(*item)
             return 0
 
-        lax.fori_loop(0, (jnp.maximum(live[0], live[1]) + 1) // 2, work, 0)
+        lax.fori_loop(0, (jnp.clip(longest - base, 0, SLOTS) + 1) // 2, work, 0)
         return 0
 
-    turns = (jnp.maximum(counts[0], counts[1]) + SLOTS - 1) // SLOTS
-    lax.fori_loop(0, turns, turn, 0)
+    lax.fori_loop(0, (longest + SLOTS - 1) // SLOTS, turn, 0)
+
+
+class Copies:
+    def __init__(self, sems):
+        self.sems = sems
+        self.started = []
+
+    def start(self, source, target):
+        copy = pltpu.make_async_copy(source, target, self.sems.at[len(self.started)])
+        copy.start()
+        self.started.append(copy)
+        return copy
+
+    def finish(self):
+        for copy in self.started:
+            copy.wait()
 
 
 def scatter_kernel(
     up_list,
     down_list,
-    left,
+    left_x,
+    left_c,
     w_up,
     w_down,
+    earlier,
+    own_out,
+    keep_a_out,
+    keep_b_out,
+    send_y_out,
+    send_x_out,
+    turned_out,
+    left,
     own,
     keep_a,
     keep_b,
@@ -175,19 +212,30 @@
     held_down,
     acc,
     sems,
+    in_sems,
+    out_sems,
+    *,
+    stacked,
+    first,
 ):
     _, groups, rows, width = acc.shape
     depth = left.shape[2]
     parts = groups // QUARTERS
     half = rows // 2
     rate = code_rate(depth)
+    out = Copies(out_sems)
+    moves = Copies(in_sems)
+    for which, source in enumerate((left_x, left_c)):
+        moves.start(source.at[which] if stacked else source, left.at[which])
 
     def meanwhile():
         acc[...] = jnp.zeros_like(acc)
+        moves.finish()
         for which in range(2):
             for k in range(depth // BLOCK):
                 columns = slice(k * BLOCK, (k + 1) * BLOCK)
                 turned[which, columns, :] = left[which, :, columns].T
+        out.start(turned, turned_out.at[:, :, pl.ds(first, rows)])
 
     def use(which, g, k, block):
         columns = pl.ds(pl.multiple_of(k * BLOCK, BLOCK), BLOCK)
@@ -207,44 +255,63 @@
         for part in range(parts):
             columns = slice(part * width, (part + 1) * width)
             near_x, near_y, far = (acc.at[which, r * parts + part] for r in (1, 2, 3))
+            keep_a[which, :, columns] = near_x[:half]
+            keep_b[which, :, columns] = near_y[half:]
+            own[which, :, columns] = acc[which, part]
             send_y[which, 0, :, columns] = encode(near_y[:half], rate)
             send_y[which, 1, :, columns] = encode(far[:half], rate)
             send_x[which, 0, :, columns] = encode(near_x[half:], rate)
             send_x[which, 1, :, columns] = encode(far[half:], rate)
-            keep_a[which, :, columns] = near_x[:half]
-            keep_b[which, :, columns] = near_y[half:]
-            own[which, :, columns] = acc[which, part]
-
-
-def scatter_terms(lists, left, w_up, w_down):
-    _, rows, depth = left.shape
+        for source, target in (
+            (keep_a, keep_a_out),
+            (keep_b, keep_b_out),
+            (own, own_out),
+            (send_y, send_y_out),
+            (send_x, send_x_out),
+        ):
+            out.start(source.at[which], target.at[which])
+    out.finish()
+
+
+def scatter_terms(lists, left, w_up, w_down, earlier, first, all_rows):
+    stacked = not isinstance(left, tuple)
+    kind = left.dtype if stacked else left[0].dtype
+    rows, depth = left.shape[1:] if stacked else left[0].shape
     units = w_up.shape[1]
     quarter, width, parts = split_units(units)
     half = rows // 2
+    if earlier is None:
+        earlier, aliases = w_up, {}
+    else:
+        aliases = {6: 5}
+    outs = [
+        ((2, rows, quarter), jnp.float32),
+        ((2, half, quarter), jnp.float32),
+        ((2, half, quarter), jnp.float32),
+        ((2, 2, half, quarter), jnp.int16),
+        ((2, 2, half, quarter), jnp.int16),
+        ((2, depth, rows), kind),
+    ]
     return pl.pallas_call(
-        scatter_kernel,
-        in_specs=[SMEM, SMEM, VMEM, ANY, ANY],
-        out_specs=[VMEM] * 6,
+        functools.partial(scatter_kernel, stacked=stacked, first=first),
+        in_specs=[SMEM, SMEM, ANY, ANY, ANY, ANY, ANY],
+        out_specs=[ANY] * 6,
         scratch_shapes=[
+            pltpu.VMEM((2, rows, depth), kind),
+            *(pltpu.VMEM(*out) for out in outs),
             pltpu.VMEM((SLOTS + 1, BLOCK, width), w_up.dtype),
             pltpu.VMEM((SLOTS + 1, width, BLOCK), w_down.dtype),
             pltpu.VMEM((2, QUARTERS * parts, rows, width), jnp.float32),
             pltpu.SemaphoreType.DMA((2, SLOTS)),
+            pltpu.SemaphoreType.DMA((2,)),
+            pltpu.SemaphoreType.DMA((11,)),
         ],
-        out_shape=[
-            shape((2, rows, quarter), jnp.float32),
-            shape((2, half, quarter), jnp.float32),
-            shape((2, half, quarter), jnp.float32),
-            shape((2, 2, half, quarter), jnp.int16),
-            shape((2, 2, half, quarter), jnp.int16),
-            shape((2, depth, rows), left.dtype),
-        ],
+        out_shape=[shape(*out) for out in outs[:5]] + [shape((2, depth, all_rows), kind)],
+        input_output_aliases=aliases,
         compiler_params=params(),
-        cost_estimate=pl.CostEstimate(
-            flops=rows * depth * units // 2, bytes_accessed=16 * 2**20, transcendentals=0
-        ),
+        cost_estimate=cost(7),
         name="current_and_hidden_grad_terms",
-    )(*lists, left, w_up, w_down)
+    )(*lists, *((left, left) if stacked else left), w_up, w_down, earlier)
 
 
 def relay_kernel(keep_a, keep_b, near_y, near_x, late_a, late_b, *, rate):
@@ -260,6 +327,7 @@
         out_specs=[VMEM] * 2,
         out_shape=[shape(keep_a.shape, jnp.int16)] * 2,
         compiler_params=params(),
+        cost_estimate=cost(3),
         name="relayed_terms",
     )(keep_a, keep_b, near_y, near_x)
 
@@ -313,83 +381,103 @@
         scratch_shapes=[pltpu.VMEM((quarter // LANES, rows, LANES), jnp.float32)] * 4,
         out_shape=shape((2, rows, quarter), jnp.bfloat16),
         compiler_params=params(),
+        cost_estimate=cost(4),
         name="spiking_and_surrogate",
     )(own, near_y, near_x, late_a, late_b, theta)
 
 
-def collect_kernel(*refs, carried):
-    up_list, down_list, mine, over_x, over_y, far_a, far_b = refs[:7]
-    at = 8 if carried else 7
-    w_up, w_down, out, whole, held_up, held_down, acc, sems = refs[at:]
-    _, rows, quarter = mine.shape
+def collect_kernel(*refs, count, carried, first_row):
+    refs = list(refs)
+
+    def take(count):
+        taken, refs[:count] = refs[:count], []
+        return taken
+
+    lists = take(2)
+    pieces = take(count)
+    came_in = take(1)[0] if carried else None
+    weights = take(2)
+    _, out, whole_out = take(3)
+    held = take(2)
+    whole, came, part, acc, sems, in_sems, out_sems = refs
+    _, rows, quarter = pieces[0].shape
     wide = acc.shape[1]
-    width = held_up.shape[2]
+    width = min(BLOCK, quarter)
     parts = quarter // width
-    half = rows // 2
+    moves = Copies(in_sems)
+    leave = Copies(out_sems)
+    if carried:
+        moves.start(came_in, came)
+    for r, source in enumerate(pieces[:3]):
+        moves.start(source, whole.at[:, r])
+    first = 0
+    for source in pieces[3:]:
+        moves.start(source, whole.at[:, 3, pl.ds(first, source.shape[1])])
+        first += source.shape[1]
 
     def meanwhile():
-        whole[:, 0] = mine[...]
-        whole[:, 1] = over_x[...]
-        whole[:, 2] = over_y[...]
-        whole[:, 3, :half] = far_a[...]
-        whole[:, 3, half:] = far_b[...]
-        if carried:
-            came = refs[7]
-            first = came.shape[1]
-            for which in range(2):
-                for j in range(wide):
-                    columns = slice(j * BLOCK, (j + 1) * BLOCK)
-                    acc[which, j, :first] = came[which, :, columns].astype(jnp.float32)
-            if first < rows:
-                acc[:, :, first:] = jnp.zeros((2, wide, rows - first, BLOCK), jnp.float32)
-        else:
-            acc[...] = jnp.zeros_like(acc)
-
-    def use(which, g, k, block):
-        r, part = g // parts, g % parts
-        columns = pl.ds(pl.multiple_of(part * width, width), width)
-        acc[which, k] += product(whole[which, r, :, columns], block[...], 1, which)
-
-    each_kept(
-        (down_list, up_list),
-        (w_down, w_up),
-        (held_down, held_up),
-        sems,
-        width,
-        (True, False),
-        use,
-        meanwhile,
-    )
-    for which in range(2):
+        moves.finish()
+        leave.start(whole, whole_out.at[:, :, pl.ds(first_row, rows), :])
+        first = came.shape[1] if carried else 0
+        for i in range(2):
+            for j in range(wide):
+                columns = slice(j * BLOCK, (j + 1) * BLOCK)
+                if carried:
+                    acc[i, j, :first] = came[i, :, columns].astype(jnp.float32)
+                if first < rows:
+                    acc[i, j, first:] = jnp.zeros((rows - first, BLOCK), jnp.float32)
+
+    def use(i, g, k, block):
+        r, piece = g // parts, g % parts
+        columns = pl.ds(pl.multiple_of(piece * width, width), width)
+        acc[i, k] += product(whole[i, r, :, columns], block[...], 1, i)
+
+    each_kept(lists, weights, held, sems, width, (True, False), use, meanwhile)
+    for i in range(2):
         for j in range(wide):
-            out[which, :, j * BLOCK : (j + 1) * BLOCK] = acc[which, j].astype(out.dtype)
-
-
-def collect_terms(lists, pieces, came, w_up, w_down, out_type):
+            part[i, :, j * BLOCK : (j + 1) * BLOCK] = acc[i, j].astype(part.dtype)
+        leave.start(part.at[i], out.at[i])
+    leave.finish()
+
+
+def collect_terms(lists, pieces, came, w_up, w_down, out_type, earlier, first, all_rows):
     _, rows, quarter = pieces[0].shape
     features, units = w_up.shape
     _, width, _ = split_units(units)
     extra = [] if came is None else [came]
+    came_dims = (2, 16, BLOCK) if came is None else came.shape
+    whole_dims = (2, QUARTERS, rows, quarter)
+    outs = [
+        shape((2, rows, features), out_type),
+        shape((2, QUARTERS, all_rows, quarter), pieces[0].dtype),
+    ]
+    if earlier is None:
+        earlier, aliases = w_up, {}
+    else:
+        aliases = {4 + len(pieces) + len(extra): 1}
     return pl.pallas_call(
-        functools.partial(collect_kernel, carried=came is not None),
-        in_specs=[SMEM, SMEM] + [VMEM] * (5 + len(extra)) + [ANY, ANY],
-        out_specs=[VMEM, VMEM],
+        functools.partial(
+            collect_kernel, count=len(pieces), carried=came is not None, first_row=first
+        ),
+        in_specs=[SMEM] * 2 + [ANY] * (3 + len(pieces) + len(extra)),
+        out_specs=[ANY] * len(outs),
         scratch_shapes=[
+            pltpu.VMEM((SLOTS + 1, width, BLOCK), w_up.dtype),
             pltpu.VMEM((SLOTS + 1, BLOCK, width), w_up.dtype),
-            pltpu.VMEM((SLOTS + 1, width, BLOCK), w_down.dtype),
+            pltpu.VMEM(whole_dims, pieces[0].dtype),
+            pltpu.VMEM(came_dims, jnp.bfloat16),
+            pltpu.VMEM((2, rows, features), out_type),
             pltpu.VMEM((2, features // BLOCK, rows, BLOCK), jnp.float32),
             pltpu.SemaphoreType.DMA((2, SLOTS)),
+            pltpu.SemaphoreType.DMA((6,)),
+            pltpu.SemaphoreType.DMA((3,)),
         ],
-        out_shape=[
-            shape((2, rows, features), out_type),
-            shape((2, QUARTERS, rows, quarter), pieces[0].dtype),
-        ],
+        out_shape=outs,
+        input_output_aliases=aliases,
         compiler_params=params(),
-        cost_estimate=pl.CostEstimate(
-            flops=rows * features * units // 2, bytes_accessed=16 * 2**20, transcendentals=0
-        ),
+        cost_estimate=cost(7),
         name="output_and_input_grad_terms",
-    )(*lists, *pieces, *extra, w_up, w_down)
+    )(lists[1], lists[0], *pieces, *extra, w_down, w_up, earlier)
 
 
 def clear_kernel(place, up, down, rows_up, rows_down, sems):
@@ -418,43 +506,36 @@
         ],
         out_shape=[shape((features, units), kind), shape((units, features), kind)],
         compiler_params=params(),
-        cost_estimate=pl.CostEstimate(
-            flops=0, bytes_accessed=4 * features * units, transcendentals=0
-        ),
+        cost_estimate=cost(12),
         name="zero_weight_grads",
     )(place)
 
 
-def weight_grads_kernel(*refs, count):
+def weight_grads_kernel(*refs, places, count):
     lists = refs[:2]
-    units = refs[2 : 2 + count]
-    turned = refs[2 + count : 2 + 2 * count]
-    outs = refs[4 + 2 * count : 6 + 2 * count]
-    held_u, held_f, stage_up, stage_down, load_sems, out_sems = refs[6 + 2 * count :]
+    many = len(places)
+    units = refs[2 : 2 + many]
+    turned = refs[2 + many : 2 + many + count]
+    outs = refs[4 + many + count : 6 + many + count]
+    held_u, held_f, stage_up, stage_down, load_sems, out_sems = refs[6 + many + count :]
     width = stage_up.shape[2]
     parts = held_u.shape[3] // width
     stages = (stage_up, stage_down)
 
     def loads(which):
-        copies = []
+        pairs = []
+        for source, first in zip(units, places):
+            span = pl.ds(first, source.shape[2])
+            pairs.append((source.at[1 - which], held_u.at[1 - which, :, span, :]))
         first = 0
-        for i in range(count):
-            rows = units[i].shape[2]
-            span = pl.ds(first, rows)
-            first += rows
-            copies.append(
-                pltpu.make_async_copy(
-                    units[i].at[1 - which],
-                    held_u.at[1 - which, :, span, :],
-                    load_sems.at[which, 0, i],
-                )
-            )
-            copies.append(
-                pltpu.make_async_copy(
-                    turned[i].at[which], held_f.at[which, :, span], load_sems.at[which, 1, i]
-                )
-            )
-        return copies
+        for source in turned:
+            span = pl.ds(first, source.shape[2])
+            first += source.shape[2]
+            pairs.append((source.at[which], held_f.at[which, :, span]))
+        return [
+            pltpu.make_async_copy(source, target, load_sems.at[which, i])
+            for i, (source, target) in enumerate(pairs)
+        ]
 
     def store(which, n):
         entry = lists[which][n]
@@ -502,33 +583,29 @@
         lax.fori_loop(jnp.maximum(totals[which] - STAGES, 0), totals[which], drain, 0)
 
 
-def weight_grads(lists, units, turned, zeros):
-    count = len(units)
-    quarter = units[0].shape[3]
-    rows = sum(piece.shape[2] for piece in units)
+def weight_grads(lists, units, places, turned, zeros):
+    count, many = len(turned), len(units)
+    quarter = units[0].shape[-1]
+    rows = sum(piece.shape[2] for piece in turned)
     features = turned[0].shape[1]
     width = min(BLOCK, quarter)
     kind = units[0].dtype
     return pl.pallas_call(
-        functools.partial(weight_grads_kernel, count=count),
-        in_specs=[SMEM] * 2 + [ANY] * (2 * count + 2),
+        functools.partial(weight_grads_kernel, places=places, count=count),
+        in_specs=[SMEM] * 2 + [ANY] * (many + count + 2),
         out_specs=[ANY, ANY],
         scratch_shapes=[
             pltpu.VMEM((2, QUARTERS, rows, quarter), kind),
             pltpu.VMEM((2, features, rows), kind),
             pltpu.VMEM((STAGES, BLOCK, width), kind),
             pltpu.VMEM((STAGES, width, BLOCK), kind),
-            pltpu.SemaphoreType.DMA((2, 2, count)),
+            pltpu.SemaphoreType.DMA((2, many + count)),
             pltpu.SemaphoreType.DMA((2, STAGES)),
         ],
         out_shape=[shape(zero.shape, kind) for zero in zeros],
-        input_output_aliases={2 + 2 * count: 0, 3 + 2 * count: 1},
+        input_output_aliases={2 + many + count: 0, 3 + many + count: 1},
         compiler_params=params(),
-        cost_estimate=pl.CostEstimate(
-            flops=rows * QUARTERS * quarter * features // 2,
-            bytes_accessed=32 * 2**20,
-            transcendentals=0,
-        ),
+        cost_estimate=cost(16),
         name="weight_grads",
     )(*lists, *units, *turned, *zeros)
 
@@ -560,29 +637,31 @@
     quarter = units // QUARTERS
     rate = code_rate(features)
     theta = lax.dynamic_slice(threshold, (col_place * quarter,), (quarter,)).reshape(1, quarter)
-    lists = kept_lists(place, mask_up, mask_down, features, units)
+    lists = kept_lists(place, mask_up, mask_down.T, features, units)
     rows = inputs.shape[0]
 
     ringed = lax.axis_size("row") == 4
-    both = jnp.stack([inputs, cotangent])
     if ringed:
-        rings = [both, around(both)]
-        groups = ((0,), (1,), (2,), (3,))
+        rings = [(inputs, cotangent), around(jnp.stack([inputs, cotangent]))]
+        count = 4
     else:
+        both = jnp.stack([inputs, cotangent])
         rings = [lax.all_gather(both, "row", axis=1, tiled=True)]
-        groups = ((0,),)
-
-    count = len(groups)
-    terms, relays, pairs, gathered, wholes = ([None] * count for _ in range(5))
-    carry = {"mine": None, "came": None, "last": None, "zeros": None}
+        count = 1
+        rows = rings[0].shape[1]
+
+    terms, relays, gathered = ([None] * count for _ in range(3))
+    lead = max(count - 1, 1)
+    carry = dict.fromkeys(("mine", "came", "last", "zeros", "turned", "whole", "end"))
 
     def scatter(i):
-        chunk = [rings[j] for j in groups[i]]
-        chunk = chunk[0] if len(chunk) == 1 else jnp.concatenate(chunk, axis=1)
+        chunk = rings[i]
         if carry["last"] is not None:
             chunk = after(chunk, carry["last"])
-        own, keep_a, keep_b, send_y, send_x, turned = scatter_terms(lists, chunk, w_up, w_down)
-        terms[i] = (own, keep_a, keep_b, across(send_y, 2), across(send_x, 1), turned)
+        own, keep_a, keep_b, send_y, send_x, carry["turned"] = scatter_terms(
+            lists, chunk, w_up, w_down, carry["turned"], i * rows, count * rows
+        )
+        terms[i] = (own, keep_a, keep_b, across(send_y, 2), across(send_x, 1))
         carry["last"] = own
 
     def hop():
@@ -594,57 +673,72 @@
         carry["last"] = zeros[0]
 
     def pass_on(i):
-        _, keep_a, keep_b, near_y, near_x, _ = terms[i]
-        late_a, late_b = relay(after(keep_a, carry["last"]), keep_b, near_y, near_x, rate)
+        _, keep_a, keep_b, near_y, near_x = terms[i]
+        keep_a = after(keep_a, carry["last"])
+        late_a, late_b = relay(keep_a, keep_b, near_y, near_x, rate)
         relays[i] = (across(late_a, 1), across(late_b, 2))
         carry["last"] = late_a
 
     def fire(i):
-        own, _, _, near_y, near_x, _ = terms[i]
+        own, _, _, near_y, near_x = terms[i]
         pair = neurons(after(own, carry["last"]), near_y, near_x, *relays[i], theta, rate)
-        half = pair.shape[1] // 2
-        over_x = across(pair, 1)
-        over_y = across(pair, 2)
-        far_a = across(over_y[:, :half], 1)
-        far_b = across(over_x[:, half:], 2)
-        gathered[i] = (pair, over_x, over_y, far_a, far_b)
+        over_x, over_y = across(pair, 1), across(pair, 2)
+        if i in RELAYS:
+            far = [across(over_y, 1) if RELAYS[i] == 1 else across(over_x, 2)]
+        else:
+            half = pair.shape[1] // 2
+            far = [across(over_y[:, :half], 1), across(over_x[:, half:], 2)]
+        gathered[i] = (pair, over_x, over_y, *far)
         carry["last"] = pair
 
     def collect(i):
         first = carry["mine"] is None
         kind = jnp.float32 if first else jnp.bfloat16
         pair, *others = gathered[i]
+        end = i == lead
         part, whole = collect_terms(
-            lists, (after(pair, carry["last"]), *others), carry["came"], w_up, w_down, kind
+            lists,
+            (after(pair, carry["last"]), *others),
+            carry["came"],
+            w_up,
+            w_down,
+            kind,
+            None if end else carry["whole"],
+            0 if end else i * rows,
+            rows if end else lead * rows,
         )
         if first:
             carry["mine"] = part
         else:
-            came = around(part[:, :rows])
-            for j in range(1, len(groups[i])):
-                came = around(part[:, j * rows : (j + 1) * rows] + came)
-            carry["came"] = came
-        wholes[i] = whole
-        carry["last"] = whole
+            carry["came"] = around(part)
+        carry["end" if end else "whole"] = whole
+        carry["last"] = part
 
     if ringed:
-        order = "S0 H R0 S1 H F0 R1 S2 F1 C0 R2 S3 F2 C1 R3 F3 C2 Z C3"
+        order = ("S0", "H", "R0", "S1", "H", "F0", "S2", "R1", "F1", "C0", "R2", "S3", "F2", "C1")
+        order += ("R3", "C2", "F3", "Z", "C3")
     else:
-        order = "S0 R0 F0 Z C0"
-    for word in order.split():
+        order = ("S0", "R0", "F0", "Z", "C0")
+    actions = {"S": scatter, "R": pass_on, "F": fire, "C": collect}
+    for word in order:
         if word == "Z":
             clear()
         elif word == "H":
             hop()
         else:
-            {"S": scatter, "R": pass_on, "F": fire, "C": collect}[word[0]](int(word[1]))
-
-    unit_parts = wholes + [other_core(whole) for whole in wholes]
-    feature_parts = [term[5] for term in terms] + [other_core(term[5]) for term in terms]
-    up_grad, down_grad = weight_grads(lists, unit_parts, feature_parts, carry["zeros"])
+            actions[word[0]](int(word[1]))
+
+    units = [carry["whole"]] + ([carry["end"]] if count > 1 else [])
+    units += [other_core(value) for value in units]
+    turned = [carry["turned"], other_core(carry["turned"])]
+    places, first = [], 0
+    for value in units:
+        places.append(first)
+        first += value.shape[2]
+    up_grad, down_grad = weight_grads(lists, units, places, turned, carry["zeros"])
     mine, came = after(carry["mine"], up_grad), carry["came"]
     if ringed:
-        ends = mine + came.astype(jnp.float32)
+        ends = [mine[kind] + came[kind].astype(jnp.float32) for kind in range(2)]
     else:
         ends = lax.psum_scatter(mine, "row", scatter_dimension=1, tiled=True)
     output, input_grad = ends[0].astype(jnp.bfloat16), ends[1].astype(jnp.bfloat16)

time: 259 us -> 248 us (0.958); the launches traced: 254 us -> 248 us
  starting transfers between devices: 57.1 us -> 45.3 us
  other arithmetic: 2.14 us -> 5.96 us
  waiting for transfers between devices: 50.4 us -> 53.7 us
    ppermute x6, starting transfers between devices: 21.7 us -> 9.87 us  [around(): lax.ppermute(value, 'row', [(ring[i], ring[(i + 1) % size]) for i in rang...]
    unnamed x95 -> x8, local copies, waits for them, and re-layouts: 14.1 us -> 3.28 us
    slice x8, local copies, waits for them, and re-layouts: 0.14 us -> 9.65 us  [fire(): far = [across(over_y[:, :half], 1), across(over_x[:, half:], 2)]]
    convert_element_type x0 -> x1, other arithmetic: none -> 3.09 us  [per_device(): ends[1].astype(jnp.bfloat16)]
    ppermute x32, waiting for transfers between devices: 37.3 us -> 40.2 us  [across(): return lax.ppermute(value, 'col', [(i, i ^ flip) for i in range(size)])]
    ppermute x6, waiting for transfers between devices: 6.48 us -> 9.26 us  [around(): lax.ppermute(value, 'row', [(ring[i], ring[(i + 1) % size]) for i in rang...]
    ppermute x8 -> x3, waiting for transfers between devices: 6.65 us -> 4.31 us  [other_core(): return lax.ppermute(value, 'dp', [(0, 1), (1, 0)])]
  transfers between devices with their start and end apart: 46 -> 41, of which waited for: 17 -> 17; matrix products, arithmetic and copies ran while one was open for 1% -> 5% of each run, Pallas kernels for 47% -> 45%
where the time goes in v2:
time: 248 us
  Pallas kernels  128 us (52%)
  waiting for transfers between devices  53.7 us (22%)
  starting transfers between devices  45.3 us (18%)
  local copies, waits for them, and re-layouts  14.2 us (6%)
  other arithmetic  5.96 us (2%)
    ppermute x32, waiting for transfers between devices, across(): return lax.ppermute(value, 'col', [(i, i ^ flip) for i in range(size)])  40.2 us
    ppermute x32, starting transfers between devices, across(): return lax.ppermute(value, 'col', [(i, i ^ flip) for i in range(size)])  34.7 us
    pallas_call x4, Pallas kernels, scatter_terms(): pl.pallas_call(functools.partial(scatter_kernel, stacked=stacked, first=f...  33.9 us
    pallas_call x4, Pallas kernels, collect_terms(): pl.pallas_call(functools.partial(collect_kernel, count=len(pieces), carri...  32.5 us
    pallas_call x1, Pallas kernels, weight_grads(): pl.pallas_call(functools.partial(weight_grads_kernel, places=places, coun...  19.9 us
    pallas_call x4, Pallas kernels, neurons(): pl.pallas_call(functools.partial(neuron_kernel, rate=rate), in_specs=[VME...  15 us
    pallas_call x4, Pallas kernels, relay(): pl.pallas_call(functools.partial(relay_kernel, rate=rate), in_specs=[VMEM...  12.3 us
    pallas_call x1, Pallas kernels, cleared(): pl.pallas_call(clear_kernel, in_specs=[SMEM], out_specs=[ANY, ANY], scrat...  11.8 us
  transfers between devices with their start and end apart: 41, of which 17 were waited for; matrix products, arithmetic and copies ran while one was open for 5% of the time, Pallas kernels for 45%

profile of v2, /device:TPU:0, one launch (start us, length us, event | category | flops | bytes accessed | tf_op | source)
XLA Modules:
  0.0 247.8 jit_solution(14334940306662353117)
XLA Ops:
  0.6 2.3 pad_maximum_fusion
  2.9 4.0 %collective-permute-start = (bf16[2,128,2048]{2,1,0:T(8,128)(2,1)}, bf16[2,128,2048]{2,1,0:T(8,128)(2,1)}, u32[]{:S(2)}, u32[]{:S(2)}) collective-permute-start(bf16[2,128,2048]{2,1,0:T(8,128)(2,1)} %pad_maximum_fusion), channel_id=1, source_target_pairs={{0,8},{8,12},{12,4},{4,0},{1,9},{9,13},{13,5},{5,1},{2,10},{10,14}... | collective-permute-start | bytes 3145736 | tf_op jit(solution)/shard_map/ppermute | solution.py:629
  7.5 2.5 %kept_blocks.1 = (s32[129]{0:T(256)}, s32[129]{0:T(256)}) custom-call(s32[2]{0:T(128)} %pad_add_fusion.place, s32[32,64]{1,0:T(8,128)} %mask_up.1, s32[32,64]{1,0:T(8,128)} %bitcast.16), custom_call_target="tpu_custom_call" | custom-call | bytes 11070000 | tf_op jit(solution)/shard_map/kept_blocks/pallas_call | solution.py:102
  10.0 8.5 %current_and_hidden_grad_terms.4 = (f32[2,128,1024]{2,1,0:T(8,128)}, f32[2,64,1024]{2,1,0:T(8,128)}, f32[2,64,1024]{2,1,0:T(8,128)}, s16[2,2,64,1024]{3,2,1,0:T(...) custom-call(s32[129]{0:T(256)} %get-tuple-element.70.up_list.refs_1_.refs_0_, ...), custom_call_target="tpu_custom_call" | custom-call | bytes 25830000 | tf_op jit(solution)/shard_map/current_and_hidden_grad_terms/pallas_call | solution.py:295
  18.5 1.3 collective-permute-start.1
  19.8 2.1 collective-permute-start.2
  21.9 7.7 %collective-permute-done.left_x.left_c = bf16[2,128,2048]{2,1,0:T(8,128)(2,1)} collective-permute-done((bf16[2,128,2048]{2,1,0:T(8,128)(2,1)}, bf16[2,128,2048]{2,1,0:T(8,128)(2,1)}, u32[]{:S(2)}, u32[]{:S(2)}) %collective-permute-start) | collective-permute-done | bytes 1048608 | tf_op jit(solution)/shard_map/ppermute | solution.py:629
  29.7 3.4 %collective-permute-start.5 = (bf16[2,128,2048]{2,1,0:T(8,128)(2,1)}, bf16[2,128,2048]{2,1,0:T(8,128)(2,1)}, u32[]{:S(2)}, u32[]{:S(2)}) collective-permute-start(bf16[2,128,2048]{2,1,0:T(8,128)(2,1)} %collective-permute-done.left_x.left_c), channel_id=1, source_target_pairs={{0,8},{8,12},{12,4},{4,0},{1,9},{9,13},{13,5},{5,1},{2,10},{10,14}... | collective-permute-start | bytes 3145736 | tf_op jit(solution)/shard_map/ppermute | solution.py:629
  33.6 3.1 %relayed_terms.4 = (s16[2,64,1024]{2,1,0:T(8,128)(2,1)}, s16[2,64,1024]{2,1,0:T(8,128)(2,1)}) custom-call(f32[2,64,1024]{2,1,0:T(8,128)} %get-tuple-element.73.keep_a, f32[2,64,1024]{2,1,0:T(8,128)} %get-tuple-element.74.keep_b, s16[2,2,64,1024]{3,2,1,0:T(8,128)(2,1)} %collective-permute-done.1.near_y, s16[2,2,64,1024]{3,2,1,0:T(8,128)(2,1)} %collective-permute-done.2.near_x), custom_call_target="tpu_custom_call" | custom-call | bytes 11070000 | tf_op jit(solution)/shard_map/relayed_terms/pallas_call | solution.py:324
  36.7 1.0 collective-permute-start.4
  37.6 1.5 collective-permute-start.3
  39.1 8.5 %current_and_hidden_grad_terms.5 = (f32[2,128,1024]{2,1,0:T(8,128)}, f32[2,64,1024]{2,1,0:T(8,128)}, f32[2,64,1024]{2,1,0:T(8,128)}, s16[2,2,64,1024]{3,2,1,0:T(...) custom-call(s32[129]{0:T(256)} %get-tuple-element.70.up_list.refs_1_., ...), custom_call_target="tpu_custom_call", output_to_operand_aliasing={{5}: (6, {})} | custom-call | bytes 25830000 | tf_op jit(solution)/shard_map/current_and_hidden_grad_terms/pallas_call | solution.py:295
  47.6 1.1 collective-permute-start.6
  48.7 0.9 collective-permute-start.7
  49.6 1.3 dynamic_slice.3
  50.9 3.7 %spiking_and_surrogate.4.refs_2_ = bf16[2,128,1024]{2,1,0:T(8,128)(2,1)} custom-call(f32[2,128,1024]{2,1,0:T(8,128)} %get-tuple-element.81.own, s16[2,2,64,1024]{3,2,1,0:T(8,128)(2,1)} %collective-permute-done.1.near_y, s16[2,2,64,1024]{3,2,1,0:T(8,128)(2,1)} %collective-permute-done.2.near_x, s16[2,64,1024]{2,1,0:T(8,128)(2,1)} %collective-permute-done.3.late_a, ...), custom_call_target="tpu_custom_call" | custom-call | bytes 14760000 | tf_op jit(solution)/shard_map/spiking_and_surrogate/pallas_call | solution.py:377
  54.7 2.0 collective-permute-start.10
  56.7 8.4 %current_and_hidden_grad_terms.6 = (f32[2,128,1024]{2,1,0:T(8,128)}, f32[2,64,1024]{2,1,0:T(8,128)}, f32[2,64,1024]{2,1,0:T(8,128)}, s16[2,2,64,1024]{3,2,1,0:T(...) custom-call(s32[129]{0:T(256)} %get-tuple-element.70.up_list.refs_1_., ...), custom_call_target="tpu_custom_call", output_to_operand_aliasing={{5}: (6, {})} | custom-call | bytes 25830000 | tf_op jit(solution)/shard_map/current_and_hidden_grad_terms/pallas_call | solution.py:295
  65.2 3.1 %relayed_terms.5 = (s16[2,64,1024]{2,1,0:T(8,128)(2,1)}, s16[2,64,1024]{2,1,0:T(8,128)(2,1)}) custom-call(f32[2,64,1024]{2,1,0:T(8,128)} %get-tuple-element.88.keep_a, f32[2,64,1024]{2,1,0:T(8,128)} %get-tuple-element.89.keep_b, s16[2,2,64,1024]{3,2,1,0:T(8,128)(2,1)} %collective-permute-done.6.near_y, s16[2,2,64,1024]{3,2,1,0:T(8,128)(2,1)} %collective-permute-done.7.near_x), custom_call_target="tpu_custom_call" | custom-call | bytes 11070000 | tf_op jit(solution)/shard_map/relayed_terms/pallas_call | solution.py:324
  69.0 1.8 collective-permute-start.14
  70.7 1.8 collective-permute-start.8
  72.6 1.4 collective-permute-done.11.refs_4_
  74.0 1.7 slice.48
  75.7 1.7 slice.49
  77.3 1.3 collective-permute-start.13
  79.4 0.9 collective-permute-done.8.late_a
  80.3 1.8 collective-permute-start.16
  82.1 3.7 %spiking_and_surrogate.5.refs_2_ = bf16[2,128,1024]{2,1,0:T(8,128)(2,1)} custom-call(f32[2,128,1024]{2,1,0:T(8,128)} %get-tuple-element.93.own, s16[2,2,64,1024]{3,2,1,0:T(8,128)(2,1)} %collective-permute-done.6.near_y, s16[2,2,64,1024]{3,2,1,0:T(8,128)(2,1)} %collective-permute-done.7.near_x, s16[2,64,1024]{2,1,0:T(8,128)(2,1)} %collective-permute-done.8.late_a, ...), custom_call_target="tpu_custom_call" | custom-call | bytes 14760000 | tf_op jit(solution)/shard_map/spiking_and_surrogate/pallas_call | solution.py:377
  85.9 0.8 collective-permute-start.20
  86.9 2.0 collective-permute-start.19
  88.9 8.3 %output_and_input_grad_terms.4 = (f32[2,128,2048]{2,1,0:T(8,128)}, bf16[2,4,384,1024]{3,2,1,0:T(8,128)(2,1)}) custom-call(s32[129]{0:T(256)} %get-tuple-element.69.down_list.refs_0_.refs_1_, s32[129]{0:T(256)} %get-tuple-element.70.up_list.refs_1_.refs_0_, bf16[2,128,1024]{2,1,0:T(8,128)(2,1)} %spiking_and_surrogate.4.refs_2_, ...), custom_call_target="tpu_custom_call" | custom-call | bytes 25830000 | tf_op jit(solution)/shard_map/output_and_input_grad_terms/pallas_call | solution.py:458
  97.2 0.9 collective-permute-done.15.near_y
  98.1 3.1 %relayed_terms.6 = (s16[2,64,1024]{2,1,0:T(8,128)(2,1)}, s16[2,64,1024]{2,1,0:T(8,128)(2,1)}) custom-call(f32[2,64,1024]{2,1,0:T(8,128)} %get-tuple-element.99.keep_a, f32[2,64,1024]{2,1,0:T(8,128)} %get-tuple-element.100.keep_b, s16[2,2,64,1024]{3,2,1,0:T(8,128)(2,1)} %collective-permute-done.15.near_y, s16[2,2,64,1024]{3,2,1,0:T(8,128)(2,1)} %collective-permute-done.16.near_x), custom_call_target="tpu_custom_call" | custom-call | bytes 11070000 | tf_op jit(solution)/shard_map/relayed_terms/pallas_call | solution.py:324
  101.2 1.3 collective-permute-start.18
  102.5 1.4 collective-permute-start.17
  103.9 4.4 %collective-permute-done.20.refs_4_ = bf16[2,128,1024]{2,1,0:T(8,128)(2,1)} collective-permute-done((bf16[2,128,1024]{2,1,0:T(8,128)(2,1)}, bf16[2,128,1024]{2,1,0:T(8,128)(2,1)}, u32[]{:S(2)}, u32[]{:S(2)}) %collective-permute-start.20) | collective-permute-done | bytes 524320 | tf_op jit(solution)/shard_map/ppermute | solution.py:619
  108.3 1.7 slice.50
  110.4 1.7 slice.51
  112.1 1.5 collective-permute-start.22
  113.7 8.5 %current_and_hidden_grad_terms.7 = (f32[2,128,1024]{2,1,0:T(8,128)}, f32[2,64,1024]{2,1,0:T(8,128)}, f32[2,64,1024]{2,1,0:T(8,128)}, s16[2,2,64,1024]{3,2,1,0:T(...) custom-call(s32[129]{0:T(256)} %get-tuple-element.70.up_list.refs_1_., ...), custom_call_target="tpu_custom_call", output_to_operand_aliasing={{5}: (6, {})} | custom-call | bytes 25830000 | tf_op jit(solution)/shard_map/current_and_hidden_grad_terms/pallas_call | solution.py:295
  122.1 3.8 %spiking_and_surrogate.6.refs_2_ = bf16[2,128,1024]{2,1,0:T(8,128)(2,1)} custom-call(f32[2,128,1024]{2,1,0:T(8,128)} %get-tuple-element.107.own, s16[2,2,64,1024]{3,2,1,0:T(8,128)(2,1)} %collective-permute-done.15.near_y, s16[2,2,64,1024]{3,2,1,0:T(8,128)(2,1)} %collective-permute-done.16.near_x, s16[2,64,1024]{2,1,0:T(8,128)(2,1)} %collective-permute-done.17.late_a, ...), custom_call_target="tpu_custom_call" | custom-call | bytes 14760000 | tf_op jit(solution)/shard_map/spiking_and_surrogate/pallas_call | solution.py:377
  126.0 7.9 %output_and_input_grad_terms.5 = (bf16[2,128,2048]{2,1,0:T(8,128)(2,1)}, bf16[2,4,384,1024]{3,2,1,0:T(8,128)(2,1)}) custom-call(s32[129]{0:T(256)} %get-tuple-element.69.down_list.refs_0_.refs_1_, s32[129]{0:T(256)} %get-tuple-element.70.up_list.refs_1_.refs_0_, bf16[2,128,1024]{2,1,0:T(8,128)(2,1)} %spiking_and_surrogate.5.refs_2_, ...), custom_call_target="tpu_custom_call", output_to_operand_aliasing={{1}: (9, {})} | custom-call | bytes 25830000 | tf_op jit(solution)/shard_map/output_and_input_grad_terms/pallas_call | solution.py:458
  134.0 2.7 %collective-permute-start.25 = (bf16[2,128,1024]{2,1,0:T(8,128)(2,1)}, bf16[2,128,1024]{2,1,0:T(8,128)(2,1)S(1)}, u32[]{:S(2)}, u32[]{:S(2)}) collective-permute-start(bf16[2,128,1024]{2,1,0:T(8,128)(2,1)} %spiking_and_surrogate.6.refs_2_), channel_id=1, source_target_pairs={{0,1},{1,0},{2,3},{3,2},{4,5},{5,4},{6,7},{7,6},{8,9},{9,8},{10,11... | collective-permute-start | bytes 1572872 | tf_op jit(solution)/shard_map/ppermute | solution.py:619
  136.7 1.3 collective-permute-start.24
  138.0 10.7 %collective-permute-done.26.refs_4_ = bf16[2,128,1024]{2,1,0:T(8,128)(2,1)S(1)} collective-permute-done((bf16[2,128,1024]{2,1,0:T(8,128)(2,1)}, bf16[2,128,1024]{2,1,0:T(8,128)(2,1)S(1)}, u32[]{:S(2)}, u32[]{:S(2)}) %collective-permute-start.26) | collective-permute-done | bytes 524320 | tf_op jit(solution)/shard_map/ppermute | solution.py:619
  148.7 0.9 copy-done
  150.9 0.8 copy-done.1
  152.4 1.7 collective-permute-start.28
  154.7 3.1 %relayed_terms.7 = (s16[2,64,1024]{2,1,0:T(8,128)(2,1)}, s16[2,64,1024]{2,1,0:T(8,128)(2,1)}) custom-call(f32[2,64,1024]{2,1,0:T(8,128)} %get-tuple-element.113.keep_a, f32[2,64,1024]{2,1,0:T(8,128)} %get-tuple-element.114.keep_b, s16[2,2,64,1024]{3,2,1,0:T(8,128)(2,1)} %collective-permute-done.23.near_y, s16[2,2,64,1024]{3,2,1,0:T(8,128)(2,1)} %collective-permute-done.24.near_x), custom_call_target="tpu_custom_call" | custom-call | bytes 11070000 | tf_op jit(solution)/shard_map/relayed_terms/pallas_call | solution.py:324
  157.8 1.3 collective-permute-done.28.refs_6_
  159.1 8.2 %output_and_input_grad_terms.6 = (bf16[2,128,2048]{2,1,0:T(8,128)(2,1)}, bf16[2,4,384,1024]{3,2,1,0:T(8,128)(2,1)}) custom-call(s32[129]{0:T(256)} %get-tuple-element.69.down_list.refs_0_.refs_1_, s32[129]{0:T(256)} %get-tuple-element.70.up_list.refs_1_.refs_0_, ...), custom_call_target="tpu_custom_call", output_to_operand_aliasing={{1}: (10, {})} | custom-call | bytes 25830000 | tf_op jit(solution)/shard_map/output_and_input_grad_terms/pallas_call | solution.py:458
  167.9 1.4 collective-permute-start.31
  170.4 6.1 %collective-permute-done.31.late_b = s16[2,64,1024]{2,1,0:T(8,128)(2,1)} collective-permute-done((s16[2,64,1024]{2,1,0:T(8,128)(2,1)}, s16[2,64,1024]{2,1,0:T(8,128)(2,1)}, u32[]{:S(2)}, u32[]{:S(2)}) %collective-permute-start.31) | collective-permute-done | bytes 262176 | tf_op jit(solution)/shard_map/ppermute | solution.py:619
  176.5 1.1 collective-permute-done.30.late_a
  177.6 3.7 %spiking_and_surrogate.7.refs_2_ = bf16[2,128,1024]{2,1,0:T(8,128)(2,1)} custom-call(f32[2,128,1024]{2,1,0:T(8,128)} %get-tuple-element.122.own, s16[2,2,64,1024]{3,2,1,0:T(8,128)(2,1)} %collective-permute-done.23.near_y, s16[2,2,64,1024]{3,2,1,0:T(8,128)(2,1)} %collective-permute-done.24.near_x, s16[2,64,1024]{2,1,0:T(8,128)(2,1)} %collective-permute-done.30.late_a, ...), custom_call_target="tpu_custom_call" | custom-call | bytes 14760000 | tf_op jit(solution)/shard_map/spiking_and_surrogate/pallas_call | solution.py:377
  182.5 11.8 %collective-permute-done.33.refs_4_ = bf16[2,128,1024]{2,1,0:T(8,128)(2,1)S(1)} collective-permute-done((bf16[2,128,1024]{2,1,0:T(8,128)(2,1)}, bf16[2,128,1024]{2,1,0:T(8,128)(2,1)S(1)}, u32[]{:S(2)}, u32[]{:S(2)}) %collective-permute-start.33) | collective-permute-done | bytes 524320 | tf_op jit(solution)/shard_map/ppermute | solution.py:619
  194.3 0.8 copy-done.2
  196.6 0.8 copy-done.3
  198.7 11.8 %zero_weight_grads.1 = (bf16[2048,4096]{1,0:T(8,128)(2,1)}, bf16[4096,2048]{1,0:T(8,128)(2,1)}) custom-call(s32[2]{0:T(128)} %pad_add_fusion.place), custom_call_target="tpu_custom_call" | custom-call | bytes 44280000 | tf_op jit(solution)/shard_map/zero_weight_grads/pallas_call | solution.py:498
  210.6 8.2 %output_and_input_grad_terms.7 = (bf16[2,128,2048]{2,1,0:T(8,128)(2,1)}, bf16[2,4,128,1024]{3,2,1,0:T(8,128)(2,1)}) custom-call(s32[129]{0:T(256)} %get-tuple-element.69.down_list.refs_0_.refs_1_, s32[129]{0:T(256)} %get-tuple-element.70.up_list.refs_1_.refs_0_, bf16[2,128,1024]{2,1,0:T(8,128)(2,1)} %spiking_and_surrogate.7.refs_2_, ...), custom_call_target="tpu_custom_call" | custom-call | bytes 25830000 | tf_op jit(solution)/shard_map/output_and_input_grad_terms/pallas_call | solution.py:458
  219.0 4.3 %collective-permute-done.38.refs_5_ = bf16[2,4,128,1024]{3,2,1,0:T(8,128)(2,1)} collective-permute-done((bf16[2,4,128,1024]{3,2,1,0:T(8,128)(2,1)}, bf16[2,4,128,1024]{3,2,1,0:T(8,128)(2,1)}, u32[]{:S(2)}, u32[]{:S(2)}) %collective-permute-start.38) | collective-permute-done | bytes 2097184 | tf_op jit(solution)/shard_map/ppermute | solution.py:623
  223.3 19.9 %weight_grads.1 = (bf16[2048,4096]{1,0:T(8,128)(2,1)}, bf16[4096,2048]{1,0:T(8,128)(2,1)}) custom-call(s32[129]{0:T(256)} %get-tuple-element.70.up_list.refs_1_.refs_0_, s32[129]{0:T(256)} %get-tuple-element.69.down_list.refs_0_.refs_1_, bf16[2,4,384,1024]{3,2,1,0:T(8,128)(2,1)} %get-tuple-element.120.refs_2_, ...), custom_call_target="tpu_custom_call", output_to_operand_aliasing={{0}: (8, {}), {1}: (9, {})} | custom-call | bytes 59040000 | tf_op jit(solution)/shard_map/weight_grads/pallas_call | solution.py:593
  243.2 1.5 collective-permute-done.40
  244.7 3.1 %fusion.1 = (bf16[128,2048]{1,0:T(8,128)(2,1)}, bf16[128,2048]{1,0:T(8,128)(2,1)}) fusion(f32[2,128,2048]{2,1,0:T(8,128)} %get-tuple-element.131, bf16[2,128,2048]{2,1,0:T(8,128)(2,1)} %collective-permute-done.40), kind=kLoop, calls=%fused_computation.4 | loop fusion | flops 1572864 | bytes 4194304 | tf_op jit(solution)/shard_map/convert_element_type | solution.py:744
  (57 shorter events, 12.1 us)
Async XLA Ops:
  2.9 26.8 %collective-permute-start = (bf16[2,128,2048]{2,1,0:T(8,128)(2,1)}, bf16[2,128,2048]{2,1,0:T(8,128)(2,1)}, u32[]{:S(2)}, u32[]{:S(2)}) collective-permute-start(bf16[2,128,2048]{2,1,0:T(8,128)(2,1)} %pad_maximum_fusion), channel_id=1, source_target_pairs={{0,8},{8,12},{12,4},{4,0},{1,9},{9,13},{13,5},{5,1},{2,10},{10,14}... | collective-permute-start | bytes 3145736 | tf_op jit(solution)/shard_map/ppermute | solution.py:629
  18.5 14.5 %collective-permute-start.1 = (s16[2,2,64,1024]{3,2,1,0:T(8,128)(2,1)}, s16[2,2,64,1024]{3,2,1,0:T(8,128)(2,1)}, u32[]{:S(2)}, u32[]{:S(2)}) collective-permute-start(s16[2,2,64,1024]{3,2,1,0:T(8,128)(2,1)} %get-tuple-element.75), channel_id=1, source_target_pairs={{0,2},{1,3},{2,0},{3,1},{4,6},{5,7},{6,4},{7,5},{8,10},{9,11},{10,... | collective-permute-start | bytes 1572872 | tf_op jit(solution)/shard_map/ppermute | solution.py:619
  19.8 13.8 %collective-permute-start.2 = (s16[2,2,64,1024]{3,2,1,0:T(8,128)(2,1)}, s16[2,2,64,1024]{3,2,1,0:T(8,128)(2,1)}, u32[]{:S(2)}, u32[]{:S(2)}) collective-permute-start(s16[2,2,64,1024]{3,2,1,0:T(8,128)(2,1)} %get-tuple-element.76), channel_id=1, source_target_pairs={{0,1},{1,0},{2,3},{3,2},{4,5},{5,4},{6,7},{7,6},{8,9},{9,8},{10,11... | collective-permute-start | bytes 1572872 | tf_op jit(solution)/shard_map/ppermute | solution.py:619
  29.7 27.1 %collective-permute-start.5 = (bf16[2,128,2048]{2,1,0:T(8,128)(2,1)}, bf16[2,128,2048]{2,1,0:T(8,128)(2,1)}, u32[]{:S(2)}, u32[]{:S(2)}) collective-permute-start(bf16[2,128,2048]{2,1,0:T(8,128)(2,1)} %collective-permute-done.left_x.left_c), channel_id=1, source_target_pairs={{0,8},{8,12},{12,4},{4,0},{1,9},{9,13},{13,5},{5,1},{2,10},{10,14}... | collective-permute-start | bytes 3145736 | tf_op jit(solution)/shard_map/ppermute | solution.py:629
  36.7 14.2 %collective-permute-start.4 = (s16[2,64,1024]{2,1,0:T(8,128)(2,1)}, s16[2,64,1024]{2,1,0:T(8,128)(2,1)}, u32[]{:S(2)}, u32[]{:S(2)}) collective-permute-start(s16[2,64,1024]{2,1,0:T(8,128)(2,1)} %get-tuple-element.82), channel_id=1, source_target_pairs={{0,2},{1,3},{2,0},{3,1},{4,6},{5,7},{6,4},{7,5},{8,10},{9,11},{10,... | collective-permute-start | bytes 786440 | tf_op jit(solution)/shard_map/ppermute | solution.py:619
  37.6 13.2 %collective-permute-start.3 = (s16[2,64,1024]{2,1,0:T(8,128)(2,1)}, s16[2,64,1024]{2,1,0:T(8,128)(2,1)}, u32[]{:S(2)}, u32[]{:S(2)}) collective-permute-start(s16[2,64,1024]{2,1,0:T(8,128)(2,1)} %get-tuple-element.77), channel_id=1, source_target_pairs={{0,1},{1,0},{2,3},{3,2},{4,5},{5,4},{6,7},{7,6},{8,9},{9,8},{10,11... | collective-permute-start | bytes 786440 | tf_op jit(solution)/shard_map/ppermute | solution.py:619
  47.6 17.6 %collective-permute-start.6 = (s16[2,2,64,1024]{3,2,1,0:T(8,128)(2,1)}, s16[2,2,64,1024]{3,2,1,0:T(8,128)(2,1)}, u32[]{:S(2)}, u32[]{:S(2)}) collective-permute-start(s16[2,2,64,1024]{3,2,1,0:T(8,128)(2,1)} %get-tuple-element.90), channel_id=1, source_target_pairs={{0,2},{1,3},{2,0},{3,1},{4,6},{5,7},{6,4},{7,5},{8,10},{9,11},{10,... | collective-permute-start | bytes 1572872 | tf_op jit(solution)/shard_map/ppermute | solution.py:619
  48.7 16.5 %collective-permute-start.7 = (s16[2,2,64,1024]{3,2,1,0:T(8,128)(2,1)}, s16[2,2,64,1024]{3,2,1,0:T(8,128)(2,1)}, u32[]{:S(2)}, u32[]{:S(2)}) collective-permute-start(s16[2,2,64,1024]{3,2,1,0:T(8,128)(2,1)} %get-tuple-element.91), channel_id=1, source_target_pairs={{0,1},{1,0},{2,3},{3,2},{4,5},{5,4},{6,7},{7,6},{8,9},{9,8},{10,11... | collective-permute-start | bytes 1572872 | tf_op jit(solution)/shard_map/ppermute | solution.py:619
  54.6 19.4 %collective-permute-start.11 = (bf16[2,128,1024]{2,1,0:T(8,128)(2,1)}, bf16[2,128,1024]{2,1,0:T(8,128)(2,1)}, u32[]{:S(2)}, u32[]{:S(2)}) collective-permute-start(bf16[2,128,1024]{2,1,0:T(8,128)(2,1)} %spiking_and_surrogate.4.refs_2_), channel_id=1, source_target_pairs={{0,2},{1,3},{2,0},{3,1},{4,6},{5,7},{6,4},{7,5},{8,10},{9,11},{10,... | collective-permute-start | bytes 1572872 | tf_op jit(solution)/shard_map/ppermute | solution.py:619
  54.7 20.9 %collective-permute-start.10 = (bf16[2,128,1024]{2,1,0:T(8,128)(2,1)}, bf16[2,128,1024]{2,1,0:T(8,128)(2,1)}, u32[]{:S(2)}, u32[]{:S(2)}) collective-permute-start(bf16[2,128,1024]{2,1,0:T(8,128)(2,1)} %spiking_and_surrogate.4.refs_2_), channel_id=1, source_target_pairs={{0,1},{1,0},{2,3},{3,2},{4,5},{5,4},{6,7},{7,6},{8,9},{9,8},{10,11... | collective-permute-start | bytes 1572872 | tf_op jit(solution)/shard_map/ppermute | solution.py:619
  68.3 10.4 %collective-permute-start.9 = (s16[2,64,1024]{2,1,0:T(8,128)(2,1)}, s16[2,64,1024]{2,1,0:T(8,128)(2,1)}, u32[]{:S(2)}, u32[]{:S(2)}) collective-permute-start(s16[2,64,1024]{2,1,0:T(8,128)(2,1)} %get-tuple-element.94), channel_id=1, source_target_pairs={{0,2},{1,3},{2,0},{3,1},{4,6},{5,7},{6,4},{7,5},{8,10},{9,11},{10,... | collective-permute-start | bytes 786440 | tf_op jit(solution)/shard_map/ppermute | solution.py:619
  69.0 44.7 %collective-permute-start.14 = (bf16[2,128,2048]{2,1,0:T(8,128)(2,1)}, bf16[2,128,2048]{2,1,0:T(8,128)(2,1)}, u32[]{:S(2)}, u32[]{:S(2)}) collective-permute-start(bf16[2,128,2048]{2,1,0:T(8,128)(2,1)} %collective-permute-done.5.left_x.left_c), channel_id=1, source_target_pairs={{0,8},{8,12},{12,4},{4,0},{1,9},{9,13},{13,5},{5,1},{2,10},{10,14}... | collective-permute-start | bytes 3145736 | tf_op jit(solution)/shard_map/ppermute | solution.py:629
  70.7 9.6 %collective-permute-start.8 = (s16[2,64,1024]{2,1,0:T(8,128)(2,1)}, s16[2,64,1024]{2,1,0:T(8,128)(2,1)}, u32[]{:S(2)}, u32[]{:S(2)}) collective-permute-start(s16[2,64,1024]{2,1,0:T(8,128)(2,1)} %get-tuple-element.92), channel_id=1, source_target_pairs={{0,1},{1,0},{2,3},{3,2},{4,5},{5,4},{6,7},{7,6},{8,9},{9,8},{10,11... | collective-permute-start | bytes 786440 | tf_op jit(solution)/shard_map/ppermute | solution.py:619
  75.7 10.3 %collective-permute-start.12 = (bf16[2,64,1024]{2,1,0:T(8,128)(2,1)}, bf16[2,64,1024]{2,1,0:T(8,128)(2,1)}, u32[]{:S(2)}, u32[]{:S(2)}) collective-permute-start(bf16[2,64,1024]{2,1,0:T(8,128)(2,1)} %slice.48), channel_id=1, source_target_pairs={{0,1},{1,0},{2,3},{3,2},{4,5},{5,4},{6,7},{7,6},{8,9},{9,8},{10,11... | collective-permute-start | bytes 786440 | tf_op jit(solution)/shard_map/ppermute | solution.py:619
  77.3 9.6 %collective-permute-start.13 = (bf16[2,64,1024]{2,1,0:T(8,128)(2,1)}, bf16[2,64,1024]{2,1,0:T(8,128)(2,1)}, u32[]{:S(2)}, u32[]{:S(2)}) collective-permute-start(bf16[2,64,1024]{2,1,0:T(8,128)(2,1)} %slice.49), channel_id=1, source_target_pairs={{0,2},{1,3},{2,0},{3,1},{4,6},{5,7},{6,4},{7,5},{8,10},{9,11},{10,... | collective-permute-start | bytes 786440 | tf_op jit(solution)/shard_map/ppermute | solution.py:619
  78.6 19.5 %collective-permute-start.15 = (s16[2,2,64,1024]{3,2,1,0:T(8,128)(2,1)}, s16[2,2,64,1024]{3,2,1,0:T(8,128)(2,1)}, u32[]{:S(2)}, u32[]{:S(2)}) collective-permute-start(s16[2,2,64,1024]{3,2,1,0:T(8,128)(2,1)} %get-tuple-element.101), channel_id=1, source_target_pairs={{0,2},{1,3},{2,0},{3,1},{4,6},{5,7},{6,4},{7,5},{8,10},{9,11},{10,... | collective-permute-start | bytes 1572872 | tf_op jit(solution)/shard_map/ppermute | solution.py:619
  80.3 17.8 %collective-permute-start.16 = (s16[2,2,64,1024]{3,2,1,0:T(8,128)(2,1)}, s16[2,2,64,1024]{3,2,1,0:T(8,128)(2,1)}, u32[]{:S(2)}, u32[]{:S(2)}) collective-permute-start(s16[2,2,64,1024]{3,2,1,0:T(8,128)(2,1)} %get-tuple-element.102), channel_id=1, source_target_pairs={{0,1},{1,0},{2,3},{3,2},{4,5},{5,4},{6,7},{7,6},{8,9},{9,8},{10,11... | collective-permute-start | bytes 1572872 | tf_op jit(solution)/shard_map/ppermute | solution.py:619
  85.9 22.4 %collective-permute-start.20 = (bf16[2,128,1024]{2,1,0:T(8,128)(2,1)}, bf16[2,128,1024]{2,1,0:T(8,128)(2,1)}, u32[]{:S(2)}, u32[]{:S(2)}) collective-permute-start(bf16[2,128,1024]{2,1,0:T(8,128)(2,1)} %spiking_and_surrogate.5.refs_2_), channel_id=1, source_target_pairs={{0,2},{1,3},{2,0},{3,1},{4,6},{5,7},{6,4},{7,5},{8,10},{9,11},{10,... | collective-permute-start | bytes 1572872 | tf_op jit(solution)/shard_map/ppermute | solution.py:619
  86.9 23.5 %collective-permute-start.19 = (bf16[2,128,1024]{2,1,0:T(8,128)(2,1)}, bf16[2,128,1024]{2,1,0:T(8,128)(2,1)}, u32[]{:S(2)}, u32[]{:S(2)}) collective-permute-start(bf16[2,128,1024]{2,1,0:T(8,128)(2,1)} %spiking_and_surrogate.5.refs_2_), channel_id=1, source_target_pairs={{0,1},{1,0},{2,3},{3,2},{4,5},{5,4},{6,7},{7,6},{8,9},{9,8},{10,11... | collective-permute-start | bytes 1572872 | tf_op jit(solution)/shard_map/ppermute | solution.py:619
  101.2 20.9 %collective-permute-start.18 = (s16[2,64,1024]{2,1,0:T(8,128)(2,1)}, s16[2,64,1024]{2,1,0:T(8,128)(2,1)}, u32[]{:S(2)}, u32[]{:S(2)}) collective-permute-start(s16[2,64,1024]{2,1,0:T(8,128)(2,1)} %get-tuple-element.108), channel_id=1, source_target_pairs={{0,2},{1,3},{2,0},{3,1},{4,6},{5,7},{6,4},{7,5},{8,10},{9,11},{10,... | collective-permute-start | bytes 786440 | tf_op jit(solution)/shard_map/ppermute | solution.py:619
  102.5 19.6 %collective-permute-start.17 = (s16[2,64,1024]{2,1,0:T(8,128)(2,1)}, s16[2,64,1024]{2,1,0:T(8,128)(2,1)}, u32[]{:S(2)}, u32[]{:S(2)}) collective-permute-start(s16[2,64,1024]{2,1,0:T(8,128)(2,1)} %get-tuple-element.103), channel_id=1, source_target_pairs={{0,1},{1,0},{2,3},{3,2},{4,5},{5,4},{6,7},{7,6},{8,9},{9,8},{10,11... | collective-permute-start | bytes 786440 | tf_op jit(solution)/shard_map/ppermute | solution.py:619
  110.0 16.0 %collective-permute-start.21 = (bf16[2,64,1024]{2,1,0:T(8,128)(2,1)}, bf16[2,64,1024]{2,1,0:T(8,128)(2,1)}, u32[]{:S(2)}, u32[]{:S(2)}) collective-permute-start(bf16[2,64,1024]{2,1,0:T(8,128)(2,1)} %slice.50), channel_id=1, source_target_pairs={{0,1},{1,0},{2,3},{3,2},{4,5},{5,4},{6,7},{7,6},{8,9},{9,8},{10,11... | collective-permute-start | bytes 786440 | tf_op jit(solution)/shard_map/ppermute | solution.py:619
  112.1 13.8 %collective-permute-start.22 = (bf16[2,64,1024]{2,1,0:T(8,128)(2,1)}, bf16[2,64,1024]{2,1,0:T(8,128)(2,1)}, u32[]{:S(2)}, u32[]{:S(2)}) collective-permute-start(bf16[2,64,1024]{2,1,0:T(8,128)(2,1)} %slice.51), channel_id=1, source_target_pairs={{0,2},{1,3},{2,0},{3,1},{4,6},{5,7},{6,4},{7,5},{8,10},{9,11},{10,... | collective-permute-start | bytes 786440 | tf_op jit(solution)/shard_map/ppermute | solution.py:619
  133.8 25.3 %collective-permute-start.29 = (bf16[2,128,2048]{2,1,0:T(8,128)(2,1)}, bf16[2,128,2048]{2,1,0:T(8,128)(2,1)}, u32[]{:S(2)}, u32[]{:S(2)}) collective-permute-start(bf16[2,128,2048]{2,1,0:T(8,128)(2,1)} %get-tuple-element.112), channel_id=1, source_target_pairs={{0,8},{8,12},{12,4},{4,0},{1,9},{9,13},{13,5},{5,1},{2,10},{10,14}... | collective-permute-start | bytes 3145736 | tf_op jit(solution)/shard_map/ppermute | solution.py:629
  133.9 14.8 %collective-permute-start.26 = (bf16[2,128,1024]{2,1,0:T(8,128)(2,1)}, bf16[2,128,1024]{2,1,0:T(8,128)(2,1)S(1)}, u32[]{:S(2)}, u32[]{:S(2)}) collective-permute-start(bf16[2,128,1024]{2,1,0:T(8,128)(2,1)} %spiking_and_surrogate.6.refs_2_), channel_id=1, source_target_pairs={{0,2},{1,3},{2,0},{3,1},{4,6},{5,7},{6,4},{7,5},{8,10},{9,11},{10,... | collective-permute-start | bytes 1572872 | tf_op jit(solution)/shard_map/ppermute | solution.py:619
  134.0 16.9 %collective-permute-start.25 = (bf16[2,128,1024]{2,1,0:T(8,128)(2,1)}, bf16[2,128,1024]{2,1,0:T(8,128)(2,1)S(1)}, u32[]{:S(2)}, u32[]{:S(2)}) collective-permute-start(bf16[2,128,1024]{2,1,0:T(8,128)(2,1)} %spiking_and_surrogate.6.refs_2_), channel_id=1, source_target_pairs={{0,1},{1,0},{2,3},{3,2},{4,5},{5,4},{6,7},{7,6},{8,9},{9,8},{10,11... | collective-permute-start | bytes 1572872 | tf_op jit(solution)/shard_map/ppermute | solution.py:619
  136.7 17.8 %collective-permute-start.23 = (s16[2,2,64,1024]{3,2,1,0:T(8,128)(2,1)}, s16[2,2,64,1024]{3,2,1,0:T(8,128)(2,1)}, u32[]{:S(2)}, u32[]{:S(2)}) collective-permute-start(s16[2,2,64,1024]{3,2,1,0:T(8,128)(2,1)} %get-tuple-element.115), channel_id=1, source_target_pairs={{0,2},{1,3},{2,0},{3,1},{4,6},{5,7},{6,4},{7,5},{8,10},{9,11},{10,... | collective-permute-start | bytes 1572872 | tf_op jit(solution)/shard_map/ppermute | solution.py:619
  136.7 18.0 %collective-permute-start.24 = (s16[2,2,64,1024]{3,2,1,0:T(8,128)(2,1)}, s16[2,2,64,1024]{3,2,1,0:T(8,128)(2,1)}, u32[]{:S(2)}, u32[]{:S(2)}) collective-permute-start(s16[2,2,64,1024]{3,2,1,0:T(8,128)(2,1)} %get-tuple-element.116), channel_id=1, source_target_pairs={{0,1},{1,0},{2,3},{3,2},{4,5},{5,4},{6,7},{7,6},{8,9},{9,8},{10,11... | collective-permute-start | bytes 1572872 | tf_op jit(solution)/shard_map/ppermute | solution.py:619
  148.7 0.9 copy-start
  150.3 7.5 %collective-permute-start.27 = (bf16[2,64,1024]{2,1,0:T(8,128)(2,1)}, bf16[2,64,1024]{2,1,0:T(8,128)(2,1)}, u32[]{:S(2)}, u32[]{:S(2)}) collective-permute-start(bf16[2,64,1024]{2,1,0:T(8,128)(2,1)} %slice.52), channel_id=1, source_target_pairs={{0,1},{1,0},{2,3},{3,2},{4,5},{5,4},{6,7},{7,6},{8,9},{9,8},{10,11... | collective-permute-start | bytes 786440 | tf_op jit(solution)/shard_map/ppermute | solution.py:619
  150.9 0.8 copy-start.1
  152.4 6.7 %collective-permute-start.28 = (bf16[2,64,1024]{2,1,0:T(8,128)(2,1)}, bf16[2,64,1024]{2,1,0:T(8,128)(2,1)}, u32[]{:S(2)}, u32[]{:S(2)}) collective-permute-start(bf16[2,64,1024]{2,1,0:T(8,128)(2,1)} %slice.53), channel_id=1, source_target_pairs={{0,2},{1,3},{2,0},{3,1},{4,6},{5,7},{6,4},{7,5},{8,10},{9,11},{10,... | collective-permute-start | bytes 786440 | tf_op jit(solution)/shard_map/ppermute | solution.py:619
  167.3 56.0 %collective-permute-start.37 = (bf16[2,4,384,1024]{3,2,1,0:T(8,128)(2,1)}, bf16[2,4,384,1024]{3,2,1,0:T(8,128)(2,1)}, u32[]{:S(2)}, u32[]{:S(2)}) collective-permute-start(bf16[2,4,384,1024]{3,2,1,0:T(8,128)(2,1)} %get-tuple-element.120.refs_2_), channel_id=1, source_target_pairs={{0,16},{16,0},{1,17},{17,1},{2,18},{18,2},{3,19},{19,3},{4,20},{20... | collective-permute-start | bytes 18874376 | tf_op jit(solution)/shard_map/ppermute | solution.py:623
  167.4 51.6 %collective-permute-start.39 = (bf16[2,2048,512]{2,1,0:T(8,128)(2,1)}, bf16[2,2048,512]{2,1,0:T(8,128)(2,1)}, u32[]{:S(2)}, u32[]{:S(2)}) collective-permute-start(bf16[2,2048,512]{2,1,0:T(8,128)(2,1)} %get-tuple-element.128.refs_6_), channel_id=1, source_target_pairs={{0,16},{16,0},{1,17},{17,1},{2,18},{18,2},{3,19},{19,3},{4,20},{20... | collective-permute-start | bytes 12582920 | tf_op jit(solution)/shard_map/ppermute | solution.py:623
  167.9 8.6 %collective-permute-start.31 = (s16[2,64,1024]{2,1,0:T(8,128)(2,1)}, s16[2,64,1024]{2,1,0:T(8,128)(2,1)}, u32[]{:S(2)}, u32[]{:S(2)}) collective-permute-start(s16[2,64,1024]{2,1,0:T(8,128)(2,1)} %get-tuple-element.123), channel_id=1, source_target_pairs={{0,2},{1,3},{2,0},{3,1},{4,6},{5,7},{6,4},{7,5},{8,10},{9,11},{10,... | collective-permute-start | bytes 786440 | tf_op jit(solution)/shard_map/ppermute | solution.py:619
  169.3 8.3 %collective-permute-start.30 = (s16[2,64,1024]{2,1,0:T(8,128)(2,1)}, s16[2,64,1024]{2,1,0:T(8,128)(2,1)}, u32[]{:S(2)}, u32[]{:S(2)}) collective-permute-start(s16[2,64,1024]{2,1,0:T(8,128)(2,1)} %get-tuple-element.117), channel_id=1, source_target_pairs={{0,1},{1,0},{2,3},{3,2},{4,5},{5,4},{6,7},{7,6},{8,9},{9,8},{10,11... | collective-permute-start | bytes 786440 | tf_op jit(solution)/shard_map/ppermute | solution.py:619
  170.0 40.6 %collective-permute-start.36 = (bf16[2,128,2048]{2,1,0:T(8,128)(2,1)}, bf16[2,128,2048]{2,1,0:T(8,128)(2,1)}, u32[]{:S(2)}, u32[]{:S(2)}) collective-permute-start(bf16[2,128,2048]{2,1,0:T(8,128)(2,1)} %get-tuple-element.121), channel_id=1, source_target_pairs={{0,8},{8,12},{12,4},{4,0},{1,9},{9,13},{13,5},{5,1},{2,10},{10,14}... | collective-permute-start | bytes 3145736 | tf_op jit(solution)/shard_map/ppermute | solution.py:629
  181.4 13.0 %collective-permute-start.33 = (bf16[2,128,1024]{2,1,0:T(8,128)(2,1)}, bf16[2,128,1024]{2,1,0:T(8,128)(2,1)S(1)}, u32[]{:S(2)}, u32[]{:S(2)}) collective-permute-start(bf16[2,128,1024]{2,1,0:T(8,128)(2,1)} %spiking_and_surrogate.7.refs_2_), channel_id=1, source_target_pairs={{0,2},{1,3},{2,0},{3,1},{4,6},{5,7},{6,4},{7,5},{8,10},{9,11},{10,... | collective-permute-start | bytes 1572872 | tf_op jit(solution)/shard_map/ppermute | solution.py:619
  182.0 14.6 %collective-permute-start.32 = (bf16[2,128,1024]{2,1,0:T(8,128)(2,1)}, bf16[2,128,1024]{2,1,0:T(8,128)(2,1)S(1)}, u32[]{:S(2)}, u32[]{:S(2)}) collective-permute-start(bf16[2,128,1024]{2,1,0:T(8,128)(2,1)} %spiking_and_surrogate.7.refs_2_), channel_id=1, source_target_pairs={{0,1},{1,0},{2,3},{3,2},{4,5},{5,4},{6,7},{7,6},{8,9},{9,8},{10,11... | collective-permute-start | bytes 1572872 | tf_op jit(solution)/shard_map/ppermute | solution.py:619
  194.3 0.8 copy-start.2
  195.9 14.7 %collective-permute-start.34 = (bf16[2,64,1024]{2,1,0:T(8,128)(2,1)}, bf16[2,64,1024]{2,1,0:T(8,128)(2,1)}, u32[]{:S(2)}, u32[]{:S(2)}) collective-permute-start(bf16[2,64,1024]{2,1,0:T(8,128)(2,1)} %slice.54), channel_id=1, source_target_pairs={{0,1},{1,0},{2,3},{3,2},{4,5},{5,4},{6,7},{7,6},{8,9},{9,8},{10,11... | collective-permute-start | bytes 786440 | tf_op jit(solution)/shard_map/ppermute | solution.py:619
  196.6 0.8 copy-start.3
  198.1 12.5 %collective-permute-start.35 = (bf16[2,64,1024]{2,1,0:T(8,128)(2,1)}, bf16[2,64,1024]{2,1,0:T(8,128)(2,1)}, u32[]{:S(2)}, u32[]{:S(2)}) collective-permute-start(bf16[2,64,1024]{2,1,0:T(8,128)(2,1)} %slice.55), channel_id=1, source_target_pairs={{0,2},{1,3},{2,0},{3,1},{4,6},{5,7},{6,4},{7,5},{8,10},{9,11},{10,... | collective-permute-start | bytes 786440 | tf_op jit(solution)/shard_map/ppermute | solution.py:619
  218.8 4.6 %collective-permute-start.38 = (bf16[2,4,128,1024]{3,2,1,0:T(8,128)(2,1)}, bf16[2,4,128,1024]{3,2,1,0:T(8,128)(2,1)}, u32[]{:S(2)}, u32[]{:S(2)}) collective-permute-start(bf16[2,4,128,1024]{3,2,1,0:T(8,128)(2,1)} %get-tuple-element.127.refs_3_), channel_id=1, source_target_pairs={{0,16},{16,0},{1,17},{17,1},{2,18},{18,2},{3,19},{19,3},{4,20},{20... | collective-permute-start | bytes 6291464 | tf_op jit(solution)/shard_map/ppermute | solution.py:623
  218.8 25.9 %collective-permute-start.40 = (bf16[2,128,2048]{2,1,0:T(8,128)(2,1)}, bf16[2,128,2048]{2,1,0:T(8,128)(2,1)}, u32[]{:S(2)}, u32[]{:S(2)}) collective-permute-start(bf16[2,128,2048]{2,1,0:T(8,128)(2,1)} %get-tuple-element.132), channel_id=1, source_target_pairs={{0,8},{8,12},{12,4},{4,0},{1,9},{9,13},{13,5},{5,1},{2,10},{10,14}... | collective-permute-start | bytes 3145736 | tf_op jit(solution)/shard_map/ppermute | solution.py:629

commit v3 on v2

--- a/solution.py
+++ b/solution.py
@@ -683,13 +683,18 @@
         own, _, _, near_y, near_x = terms[i]
         pair = neurons(after(own, carry["last"]), near_y, near_x, *relays[i], theta, rate)
         over_x, over_y = across(pair, 1), across(pair, 2)
+        if i == count - 1:
+            carry["last"] = pair
+            clear()
+            over_x, over_y = after((over_x, over_y), carry["zeros"][0])
         if i in RELAYS:
             far = [across(over_y, 1) if RELAYS[i] == 1 else across(over_x, 2)]
         else:
             half = pair.shape[1] // 2
             far = [across(over_y[:, :half], 1), across(over_x[:, half:], 2)]
         gathered[i] = (pair, over_x, over_y, *far)
-        carry["last"] = pair
+        if i < count - 1:
+            carry["last"] = pair
 
     def collect(i):
         first = carry["mine"] is None
@@ -716,14 +721,12 @@
 
     if ringed:
         order = ("S0", "H", "R0", "S1", "H", "F0", "S2", "R1", "F1", "C0", "R2", "S3", "F2", "C1")
-        order += ("R3", "C2", "F3", "Z", "C3")
+        order += ("R3", "C2", "F3", "C3")
     else:
-        order = ("S0", "R0", "F0", "Z", "C0")
+        order = ("S0", "R0", "F0", "C0")
     actions = {"S": scatter, "R": pass_on, "F": fire, "C": collect}
     for word in order:
-        if word == "Z":
-            clear()
-        elif word == "H":
+        if word == "H":
             hop()
         else:
             actions[word[0]](int(word[1]))

time: 248 us -> 241 us (0.972)
  Pallas kernels: 128 us -> 114 us
  starting transfers between devices: 45.3 us -> 54.9 us
  waiting for transfers between devices: 53.7 us -> 50.3 us
    ppermute x6, starting transfers between devices: 9.87 us -> 17.4 us  [around(): lax.ppermute(value, 'row', [(ring[i], ring[(i + 1) % size]) for i in rang...]
    pallas_call x4, Pallas kernels: 32.5 us -> 27.4 us  [collect_terms(): pl.pallas_call(functools.partial(collect_kernel, count=len(pieces), carri...]
    pallas_call x4, Pallas kernels: 33.9 us -> 28.8 us  [scatter_terms(): pl.pallas_call(functools.partial(scatter_kernel, stacked=stacked, first=f...]
    ppermute x32, waiting for transfers between devices: 40.2 us -> 35.4 us  [across(): return lax.ppermute(value, 'col', [(i, i ^ flip) for i in range(size)])]
    ppermute x6, waiting for transfers between devices: 9.26 us -> 13.6 us  [around(): lax.ppermute(value, 'row', [(ring[i], ring[(i + 1) % size]) for i in rang...]
    pallas_call x1, Pallas kernels: 19.9 us -> 16.5 us  [weight_grads(): pl.pallas_call(functools.partial(weight_grads_kernel, places=places, coun...]
    ppermute x3, waiting for transfers between devices: 4.31 us -> 1.26 us  [other_core(): return lax.ppermute(value, 'dp', [(0, 1), (1, 0)])]
  transfers between devices with their start and end apart: 41 -> 41, of which waited for: 17 -> 17; matrix products, arithmetic and copies ran while one was open for 5% -> 5% of each run, Pallas kernels for 45% -> 42%
where the time goes in v3:
time: 241 us; the launch traced here: 240 us
  Pallas kernels  114 us (47%)
  starting transfers between devices  54.9 us (23%)
  waiting for transfers between devices  50.3 us (21%)
  local copies, waits for them, and re-layouts  13.8 us (6%)
  other arithmetic  5.96 us (2%)
    ppermute x32, starting transfers between devices, across(): return lax.ppermute(value, 'col', [(i, i ^ flip) for i in range(size)])  36.9 us
    ppermute x32, waiting for transfers between devices, across(): return lax.ppermute(value, 'col', [(i, i ^ flip) for i in range(size)])  35.4 us
    pallas_call x4, Pallas kernels, scatter_terms(): pl.pallas_call(functools.partial(scatter_kernel, stacked=stacked, first=f...  28.8 us
    pallas_call x4, Pallas kernels, collect_terms(): pl.pallas_call(functools.partial(collect_kernel, count=len(pieces), carri...  27.4 us
    ppermute x6, starting transfers between devices, around(): lax.ppermute(value, 'row', [(ring[i], ring[(i + 1) % size]) for i in rang...  17.4 us
    pallas_call x1, Pallas kernels, weight_grads(): pl.pallas_call(functools.partial(weight_grads_kernel, places=places, coun...  16.5 us
    pallas_call x4, Pallas kernels, neurons(): pl.pallas_call(functools.partial(neuron_kernel, rate=rate), in_specs=[VME...  15 us
    ppermute x6, waiting for transfers between devices, around(): lax.ppermute(value, 'row', [(ring[i], ring[(i + 1) % size]) for i in rang...  13.6 us
  transfers between devices with their start and end apart: 41, of which 17 were waited for; matrix products, arithmetic and copies ran while one was open for 5% of the time, Pallas kernels for 42%

profile of v3, /device:TPU:0, one launch (start us, length us, event | category | flops | bytes accessed | tf_op | source)
XLA Modules:
  0.0 240.1 jit_solution(567717673723237694)
XLA Ops:
  0.6 2.3 pad_maximum_fusion
  2.9 4.0 %collective-permute-start = (bf16[2,128,2048]{2,1,0:T(8,128)(2,1)}, bf16[2,128,2048]{2,1,0:T(8,128)(2,1)}, u32[]{:S(2)}, u32[]{:S(2)}) collective-permute-start(bf16[2,128,2048]{2,1,0:T(8,128)(2,1)} %pad_maximum_fusion), channel_id=1, source_target_pairs={{0,8},{8,12},{12,4},{4,0},{1,9},{9,13},{13,5},{5,1},{2,10},{10,14}... | collective-permute-start | bytes 3145736 | tf_op jit(solution)/shard_map/ppermute | solution.py:629
  7.5 2.5 %kept_blocks.1 = (s32[129]{0:T(256)}, s32[129]{0:T(256)}) custom-call(s32[2]{0:T(128)} %pad_add_fusion.place, s32[32,64]{1,0:T(8,128)} %mask_up.1, s32[32,64]{1,0:T(8,128)} %bitcast.16), custom_call_target="tpu_custom_call" | custom-call | bytes 11070000 | tf_op jit(solution)/shard_map/kept_blocks/pallas_call | solution.py:102
  10.0 7.2 %current_and_hidden_grad_terms.4 = (f32[2,128,1024]{2,1,0:T(8,128)}, f32[2,64,1024]{2,1,0:T(8,128)}, f32[2,64,1024]{2,1,0:T(8,128)}, s16[2,2,64,1024]{3,2,1,0:T(...) custom-call(s32[129]{0:T(256)} %get-tuple-element.72.up_list.refs_1_.refs_0_, ...), custom_call_target="tpu_custom_call" | custom-call | bytes 25830000 | tf_op jit(solution)/shard_map/current_and_hidden_grad_terms/pallas_call | solution.py:295
  17.3 1.6 collective-permute-start.1
  18.9 2.7 %collective-permute-start.2 = (s16[2,2,64,1024]{3,2,1,0:T(8,128)(2,1)}, s16[2,2,64,1024]{3,2,1,0:T(8,128)(2,1)}, u32[]{:S(2)}, u32[]{:S(2)}) collective-permute-start(s16[2,2,64,1024]{3,2,1,0:T(8,128)(2,1)} %get-tuple-element.78), channel_id=1, source_target_pairs={{0,1},{1,0},{2,3},{3,2},{4,5},{5,4},{6,7},{7,6},{8,9},{9,8},{10,11... | collective-permute-start | bytes 1572872 | tf_op jit(solution)/shard_map/ppermute | solution.py:619
  21.6 8.1 %collective-permute-done.left_x.left_c = bf16[2,128,2048]{2,1,0:T(8,128)(2,1)} collective-permute-done((bf16[2,128,2048]{2,1,0:T(8,128)(2,1)}, bf16[2,128,2048]{2,1,0:T(8,128)(2,1)}, u32[]{:S(2)}, u32[]{:S(2)}) %collective-permute-start) | collective-permute-done | bytes 1048608 | tf_op jit(solution)/shard_map/ppermute | solution.py:629
  29.7 3.4 %collective-permute-start.5 = (bf16[2,128,2048]{2,1,0:T(8,128)(2,1)}, bf16[2,128,2048]{2,1,0:T(8,128)(2,1)}, u32[]{:S(2)}, u32[]{:S(2)}) collective-permute-start(bf16[2,128,2048]{2,1,0:T(8,128)(2,1)} %collective-permute-done.left_x.left_c), channel_id=1, source_target_pairs={{0,8},{8,12},{12,4},{4,0},{1,9},{9,13},{13,5},{5,1},{2,10},{10,14}... | collective-permute-start | bytes 3145736 | tf_op jit(solution)/shard_map/ppermute | solution.py:629
  33.3 3.1 %relayed_terms.4 = (s16[2,64,1024]{2,1,0:T(8,128)(2,1)}, s16[2,64,1024]{2,1,0:T(8,128)(2,1)}) custom-call(f32[2,64,1024]{2,1,0:T(8,128)} %get-tuple-element.75.keep_a, f32[2,64,1024]{2,1,0:T(8,128)} %get-tuple-element.76.keep_b, s16[2,2,64,1024]{3,2,1,0:T(8,128)(2,1)} %collective-permute-done.1.near_y, s16[2,2,64,1024]{3,2,1,0:T(8,128)(2,1)} %collective-permute-done.2.near_x), custom_call_target="tpu_custom_call" | custom-call | bytes 11070000 | tf_op jit(solution)/shard_map/relayed_terms/pallas_call | solution.py:324
  36.4 1.3 collective-permute-start.4
  37.6 1.5 collective-permute-start.3
  39.1 7.2 %current_and_hidden_grad_terms.5 = (f32[2,128,1024]{2,1,0:T(8,128)}, f32[2,64,1024]{2,1,0:T(8,128)}, f32[2,64,1024]{2,1,0:T(8,128)}, s16[2,2,64,1024]{3,2,1,0:T(...) custom-call(s32[129]{0:T(256)} %get-tuple-element.72.up_list.refs_1_., ...), custom_call_target="tpu_custom_call", output_to_operand_aliasing={{5}: (6, {})} | custom-call | bytes 25830000 | tf_op jit(solution)/shard_map/current_and_hidden_grad_terms/pallas_call | solution.py:295
  46.3 1.1 collective-permute-start.6
  47.4 1.5 collective-permute-start.7
  49.0 1.3 dynamic_slice.3
  50.2 3.7 %spiking_and_surrogate.4.refs_2_ = bf16[2,128,1024]{2,1,0:T(8,128)(2,1)} custom-call(f32[2,128,1024]{2,1,0:T(8,128)} %get-tuple-element.83.own, s16[2,2,64,1024]{3,2,1,0:T(8,128)(2,1)} %collective-permute-done.1.near_y, s16[2,2,64,1024]{3,2,1,0:T(8,128)(2,1)} %collective-permute-done.2.near_x, s16[2,64,1024]{2,1,0:T(8,128)(2,1)} %collective-permute-done.3.late_a, ...), custom_call_target="tpu_custom_call" | custom-call | bytes 14760000 | tf_op jit(solution)/shard_map/spiking_and_surrogate/pallas_call | solution.py:377
  55.5 7.2 %current_and_hidden_grad_terms.6 = (f32[2,128,1024]{2,1,0:T(8,128)}, f32[2,64,1024]{2,1,0:T(8,128)}, f32[2,64,1024]{2,1,0:T(8,128)}, s16[2,2,64,1024]{3,2,1,0:T(...) custom-call(s32[129]{0:T(256)} %get-tuple-element.72.up_list.refs_1_., ...), custom_call_target="tpu_custom_call", output_to_operand_aliasing={{5}: (6, {})} | custom-call | bytes 25830000 | tf_op jit(solution)/shard_map/current_and_hidden_grad_terms/pallas_call | solution.py:295
  62.7 3.1 %relayed_terms.5 = (s16[2,64,1024]{2,1,0:T(8,128)(2,1)}, s16[2,64,1024]{2,1,0:T(8,128)(2,1)}) custom-call(f32[2,64,1024]{2,1,0:T(8,128)} %get-tuple-element.90.keep_a, f32[2,64,1024]{2,1,0:T(8,128)} %get-tuple-element.91.keep_b, s16[2,2,64,1024]{3,2,1,0:T(8,128)(2,1)} %collective-permute-done.6.near_y, s16[2,2,64,1024]{3,2,1,0:T(8,128)(2,1)} %collective-permute-done.7.near_x), custom_call_target="tpu_custom_call" | custom-call | bytes 11070000 | tf_op jit(solution)/shard_map/relayed_terms/pallas_call | solution.py:324
  65.8 1.0 collective-permute-start.9
  66.8 4.0 %collective-permute-start.14 = (bf16[2,128,2048]{2,1,0:T(8,128)(2,1)}, bf16[2,128,2048]{2,1,0:T(8,128)(2,1)}, u32[]{:S(2)}, u32[]{:S(2)}) collective-permute-start(bf16[2,128,2048]{2,1,0:T(8,128)(2,1)} %collective-permute-done.5.left_x.left_c), channel_id=1, source_target_pairs={{0,8},{8,12},{12,4},{4,0},{1,9},{9,13},{13,5},{5,1},{2,10},{10,14}... | collective-permute-start | bytes 3145736 | tf_op jit(solution)/shard_map/ppermute | solution.py:629
  71.3 1.4 collective-permute-done.11.refs_4_
  72.7 1.7 slice.48
  75.1 1.7 slice.49
  77.7 1.1 collective-permute-start.15
  78.8 1.5 collective-permute-done.8.late_a
  80.9 3.7 %spiking_and_surrogate.5.refs_2_ = bf16[2,128,1024]{2,1,0:T(8,128)(2,1)} custom-call(f32[2,128,1024]{2,1,0:T(8,128)} %get-tuple-element.95.own, s16[2,2,64,1024]{3,2,1,0:T(8,128)(2,1)} %collective-permute-done.6.near_y, s16[2,2,64,1024]{3,2,1,0:T(8,128)(2,1)} %collective-permute-done.7.near_x, s16[2,64,1024]{2,1,0:T(8,128)(2,1)} %collective-permute-done.8.late_a, ...), custom_call_target="tpu_custom_call" | custom-call | bytes 14760000 | tf_op jit(solution)/shard_map/spiking_and_surrogate/pallas_call | solution.py:377
  84.6 1.4 collective-permute-done.12.refs_5_
  86.4 1.2 collective-permute-start.19
  87.7 7.0 %output_and_input_grad_terms.4 = (f32[2,128,2048]{2,1,0:T(8,128)}, bf16[2,4,384,1024]{3,2,1,0:T(8,128)(2,1)}) custom-call(s32[129]{0:T(256)} %get-tuple-element.71.down_list.refs_0_.refs_1_, s32[129]{0:T(256)} %get-tuple-element.72.up_list.refs_1_.refs_0_, bf16[2,128,1024]{2,1,0:T(8,128)(2,1)} %spiking_and_surrogate.4.refs_2_, ...), custom_call_target="tpu_custom_call" | custom-call | bytes 25830000 | tf_op jit(solution)/shard_map/output_and_input_grad_terms/pallas_call | solution.py:458
  94.6 2.9 %collective-permute-done.15.near_y = s16[2,2,64,1024]{3,2,1,0:T(8,128)(2,1)} collective-permute-done((s16[2,2,64,1024]{3,2,1,0:T(8,128)(2,1)}, s16[2,2,64,1024]{3,2,1,0:T(8,128)(2,1)}, u32[]{:S(2)}, u32[]{:S(2)}) %collective-permute-start.15) | collective-permute-done | bytes 524320 | tf_op jit(solution)/shard_map/ppermute | solution.py:619
  97.6 3.1 %relayed_terms.6 = (s16[2,64,1024]{2,1,0:T(8,128)(2,1)}, s16[2,64,1024]{2,1,0:T(8,128)(2,1)}) custom-call(f32[2,64,1024]{2,1,0:T(8,128)} %get-tuple-element.101.keep_a, f32[2,64,1024]{2,1,0:T(8,128)} %get-tuple-element.102.keep_b, s16[2,2,64,1024]{3,2,1,0:T(8,128)(2,1)} %collective-permute-done.15.near_y, s16[2,2,64,1024]{3,2,1,0:T(8,128)(2,1)} %collective-permute-done.16.near_x), custom_call_target="tpu_custom_call" | custom-call | bytes 11070000 | tf_op jit(solution)/shard_map/relayed_terms/pallas_call | solution.py:324
  101.5 1.1 collective-permute-start.17
  102.6 5.0 %collective-permute-done.20.refs_4_ = bf16[2,128,1024]{2,1,0:T(8,128)(2,1)} collective-permute-done((bf16[2,128,1024]{2,1,0:T(8,128)(2,1)}, bf16[2,128,1024]{2,1,0:T(8,128)(2,1)}, u32[]{:S(2)}, u32[]{:S(2)}) %collective-permute-start.20) | collective-permute-done | bytes 524320 | tf_op jit(solution)/shard_map/ppermute | solution.py:619
  107.7 1.7 slice.50
  109.4 1.7 slice.51
  111.0 1.8 collective-permute-start.22
  112.8 7.2 %current_and_hidden_grad_terms.7 = (f32[2,128,1024]{2,1,0:T(8,128)}, f32[2,64,1024]{2,1,0:T(8,128)}, f32[2,64,1024]{2,1,0:T(8,128)}, s16[2,2,64,1024]{3,2,1,0:T(...) custom-call(s32[129]{0:T(256)} %get-tuple-element.72.up_list.refs_1_., ...), custom_call_target="tpu_custom_call", output_to_operand_aliasing={{5}: (6, {})} | custom-call | bytes 25830000 | tf_op jit(solution)/shard_map/current_and_hidden_grad_terms/pallas_call | solution.py:295
  120.0 3.8 %spiking_and_surrogate.6.refs_2_ = bf16[2,128,1024]{2,1,0:T(8,128)(2,1)} custom-call(f32[2,128,1024]{2,1,0:T(8,128)} %get-tuple-element.109.own, s16[2,2,64,1024]{3,2,1,0:T(8,128)(2,1)} %collective-permute-done.15.near_y, s16[2,2,64,1024]{3,2,1,0:T(8,128)(2,1)} %collective-permute-done.16.near_x, s16[2,64,1024]{2,1,0:T(8,128)(2,1)} %collective-permute-done.17.late_a, ...), custom_call_target="tpu_custom_call" | custom-call | bytes 14760000 | tf_op jit(solution)/shard_map/spiking_and_surrogate/pallas_call | solution.py:377
  123.8 6.6 %output_and_input_grad_terms.5 = (bf16[2,128,2048]{2,1,0:T(8,128)(2,1)}, bf16[2,4,384,1024]{3,2,1,0:T(8,128)(2,1)}) custom-call(s32[129]{0:T(256)} %get-tuple-element.71.down_list.refs_0_.refs_1_, s32[129]{0:T(256)} %get-tuple-element.72.up_list.refs_1_.refs_0_, bf16[2,128,1024]{2,1,0:T(8,128)(2,1)} %spiking_and_surrogate.5.refs_2_, ...), custom_call_target="tpu_custom_call", output_to_operand_aliasing={{1}: (9, {})} | custom-call | bytes 25830000 | tf_op jit(solution)/shard_map/output_and_input_grad_terms/pallas_call | solution.py:458
  130.5 1.3 collective-permute-start.29
  131.7 1.7 collective-permute-start.26
  133.4 2.0 collective-permute-start.25
  135.8 11.0 %collective-permute-done.26.refs_4_ = bf16[2,128,1024]{2,1,0:T(8,128)(2,1)S(1)} collective-permute-done((bf16[2,128,1024]{2,1,0:T(8,128)(2,1)}, bf16[2,128,1024]{2,1,0:T(8,128)(2,1)S(1)}, u32[]{:S(2)}, u32[]{:S(2)}) %collective-permute-start.26) | collective-permute-done | bytes 524320 | tf_op jit(solution)/shard_map/ppermute | solution.py:619
  150.5 1.7 collective-permute-start.28
  152.5 1.1 collective-permute-done.24.near_x
  153.7 3.1 %relayed_terms.7 = (s16[2,64,1024]{2,1,0:T(8,128)(2,1)}, s16[2,64,1024]{2,1,0:T(8,128)(2,1)}) custom-call(f32[2,64,1024]{2,1,0:T(8,128)} %get-tuple-element.115.keep_a, f32[2,64,1024]{2,1,0:T(8,128)} %get-tuple-element.116.keep_b, s16[2,2,64,1024]{3,2,1,0:T(8,128)(2,1)} %collective-permute-done.23.near_y, s16[2,2,64,1024]{3,2,1,0:T(8,128)(2,1)} %collective-permute-done.24.near_x), custom_call_target="tpu_custom_call" | custom-call | bytes 11070000 | tf_op jit(solution)/shard_map/relayed_terms/pallas_call | solution.py:324
  157.2 6.9 %output_and_input_grad_terms.6 = (bf16[2,128,2048]{2,1,0:T(8,128)(2,1)}, bf16[2,4,384,1024]{3,2,1,0:T(8,128)(2,1)}) custom-call(s32[129]{0:T(256)} %get-tuple-element.71.down_list.refs_0_.refs_1_, s32[129]{0:T(256)} %get-tuple-element.72.up_list.refs_1_.refs_0_, ...), custom_call_target="tpu_custom_call", output_to_operand_aliasing={{1}: (10, {})} | custom-call | bytes 25830000 | tf_op jit(solution)/shard_map/output_and_input_grad_terms/pallas_call | solution.py:458
  164.7 1.8 collective-permute-start.31
  166.4 2.4 %collective-permute-start.30 = (s16[2,64,1024]{2,1,0:T(8,128)(2,1)}, s16[2,64,1024]{2,1,0:T(8,128)(2,1)}, u32[]{:S(2)}, u32[]{:S(2)}) collective-permute-start(s16[2,64,1024]{2,1,0:T(8,128)(2,1)} %get-tuple-element.119), channel_id=1, source_target_pairs={{0,1},{1,0},{2,3},{3,2},{4,5},{5,4},{6,7},{7,6},{8,9},{9,8},{10,11... | collective-permute-start | bytes 786440 | tf_op jit(solution)/shard_map/ppermute | solution.py:619
  168.9 1.5 collective-permute-start.36
  170.4 2.9 %collective-permute-done.31.late_b = s16[2,64,1024]{2,1,0:T(8,128)(2,1)} collective-permute-done((s16[2,64,1024]{2,1,0:T(8,128)(2,1)}, s16[2,64,1024]{2,1,0:T(8,128)(2,1)}, u32[]{:S(2)}, u32[]{:S(2)}) %collective-permute-start.31) | collective-permute-done | bytes 262176 | tf_op jit(solution)/shard_map/ppermute | solution.py:619
  173.3 2.2 collective-permute-done.30.late_a
  175.5 3.7 %spiking_and_surrogate.7.refs_2_ = bf16[2,128,1024]{2,1,0:T(8,128)(2,1)} custom-call(f32[2,128,1024]{2,1,0:T(8,128)} %get-tuple-element.124.own, s16[2,2,64,1024]{3,2,1,0:T(8,128)(2,1)} %collective-permute-done.23.near_y, s16[2,2,64,1024]{3,2,1,0:T(8,128)(2,1)} %collective-permute-done.24.near_x, s16[2,64,1024]{2,1,0:T(8,128)(2,1)} %collective-permute-done.30.late_a, ...), custom_call_target="tpu_custom_call" | custom-call | bytes 14760000 | tf_op jit(solution)/shard_map/spiking_and_surrogate/pallas_call | solution.py:377
  179.5 1.7 collective-permute-start.32
  181.2 11.8 %zero_weight_grads.1 = (bf16[2048,4096]{1,0:T(8,128)(2,1)}, bf16[4096,2048]{1,0:T(8,128)(2,1)}) custom-call(s32[2]{0:T(128)} %pad_add_fusion.place), custom_call_target="tpu_custom_call" | custom-call | bytes 44280000 | tf_op jit(solution)/shard_map/zero_weight_grads/pallas_call | solution.py:498
  195.0 1.3 collective-permute-start.34
  196.3 1.4 collective-permute-start.35
  197.8 4.2 %collective-permute-done.34.refs_5_ = bf16[2,64,1024]{2,1,0:T(8,128)(2,1)S(1)} collective-permute-done((bf16[2,64,1024]{2,1,0:T(8,128)(2,1)S(1)}, bf16[2,64,1024]{2,1,0:T(8,128)(2,1)S(1)}, u32[]{:S(2)}, u32[]{:S(2)}) %collective-permute-start.34) | collective-permute-done | bytes 262176 | tf_op jit(solution)/shard_map/ppermute | solution.py:619
  203.4 6.9 %output_and_input_grad_terms.7 = (bf16[2,128,2048]{2,1,0:T(8,128)(2,1)}, bf16[2,4,128,1024]{3,2,1,0:T(8,128)(2,1)}) custom-call(s32[129]{0:T(256)} %get-tuple-element.71.down_list.refs_0_.refs_1_, s32[129]{0:T(256)} %get-tuple-element.72.up_list.refs_1_.refs_0_, bf16[2,128,1024]{2,1,0:T(8,128)(2,1)} %spiking_and_surrogate.7.refs_2_, ...), custom_call_target="tpu_custom_call" | custom-call | bytes 25830000 | tf_op jit(solution)/shard_map/output_and_input_grad_terms/pallas_call | solution.py:458
  210.4 3.2 %collective-permute-start.40 = (bf16[2,128,2048]{2,1,0:T(8,128)(2,1)}, bf16[2,128,2048]{2,1,0:T(8,128)(2,1)}, u32[]{:S(2)}, u32[]{:S(2)}) collective-permute-start(bf16[2,128,2048]{2,1,0:T(8,128)(2,1)} %get-tuple-element.136), channel_id=1, source_target_pairs={{0,8},{8,12},{12,4},{4,0},{1,9},{9,13},{13,5},{5,1},{2,10},{10,14}... | collective-permute-start | bytes 3145736 | tf_op jit(solution)/shard_map/ppermute | solution.py:629
  213.6 1.3 collective-permute-done.38.refs_5_
  214.9 16.5 %weight_grads.1 = (bf16[2048,4096]{1,0:T(8,128)(2,1)}, bf16[4096,2048]{1,0:T(8,128)(2,1)}) custom-call(s32[129]{0:T(256)} %get-tuple-element.72.up_list.refs_1_.refs_0_, s32[129]{0:T(256)} %get-tuple-element.71.down_list.refs_0_.refs_1_, bf16[2,4,384,1024]{3,2,1,0:T(8,128)(2,1)} %get-tuple-element.122.refs_2_, ...), custom_call_target="tpu_custom_call", output_to_operand_aliasing={{0}: (8, {}), {1}: (9, {})} | custom-call | bytes 59040000 | tf_op jit(solution)/shard_map/weight_grads/pallas_call | solution.py:593
  231.4 5.6 %collective-permute-done.40 = bf16[2,128,2048]{2,1,0:T(8,128)(2,1)} collective-permute-done((bf16[2,128,2048]{2,1,0:T(8,128)(2,1)}, bf16[2,128,2048]{2,1,0:T(8,128)(2,1)}, u32[]{:S(2)}, u32[]{:S(2)}) %collective-permute-start.40) | collective-permute-done | bytes 1048608 | tf_op jit(solution)/shard_map/ppermute | solution.py:629
  237.0 3.1 %fusion.1 = (bf16[128,2048]{1,0:T(8,128)(2,1)}, bf16[128,2048]{1,0:T(8,128)(2,1)}) fusion(f32[2,128,2048]{2,1,0:T(8,128)} %get-tuple-element.135, bf16[2,128,2048]{2,1,0:T(8,128)(2,1)} %collective-permute-done.40), kind=kLoop, calls=%fused_computation.4 | loop fusion | flops 1572864 | bytes 4194304 | tf_op jit(solution)/shard_map/convert_element_type | solution.py:747
  (57 shorter events, 15.7 us)
Async XLA Ops:
  2.9 26.8 %collective-permute-start = (bf16[2,128,2048]{2,1,0:T(8,128)(2,1)}, bf16[2,128,2048]{2,1,0:T(8,128)(2,1)}, u32[]{:S(2)}, u32[]{:S(2)}) collective-permute-start(bf16[2,128,2048]{2,1,0:T(8,128)(2,1)} %pad_maximum_fusion), channel_id=1, source_target_pairs={{0,8},{8,12},{12,4},{4,0},{1,9},{9,13},{13,5},{5,1},{2,10},{10,14}... | collective-permute-start | bytes 3145736 | tf_op jit(solution)/shard_map/ppermute | solution.py:629
  17.3 15.8 %collective-permute-start.1 = (s16[2,2,64,1024]{3,2,1,0:T(8,128)(2,1)}, s16[2,2,64,1024]{3,2,1,0:T(8,128)(2,1)}, u32[]{:S(2)}, u32[]{:S(2)}) collective-permute-start(s16[2,2,64,1024]{3,2,1,0:T(8,128)(2,1)} %get-tuple-element.77), channel_id=1, source_target_pairs={{0,2},{1,3},{2,0},{3,1},{4,6},{5,7},{6,4},{7,5},{8,10},{9,11},{10,... | collective-permute-start | bytes 1572872 | tf_op jit(solution)/shard_map/ppermute | solution.py:619
  18.9 14.4 %collective-permute-start.2 = (s16[2,2,64,1024]{3,2,1,0:T(8,128)(2,1)}, s16[2,2,64,1024]{3,2,1,0:T(8,128)(2,1)}, u32[]{:S(2)}, u32[]{:S(2)}) collective-permute-start(s16[2,2,64,1024]{3,2,1,0:T(8,128)(2,1)} %get-tuple-element.78), channel_id=1, source_target_pairs={{0,1},{1,0},{2,3},{3,2},{4,5},{5,4},{6,7},{7,6},{8,9},{9,8},{10,11... | collective-permute-start | bytes 1572872 | tf_op jit(solution)/shard_map/ppermute | solution.py:619
  29.7 25.8 %collective-permute-start.5 = (bf16[2,128,2048]{2,1,0:T(8,128)(2,1)}, bf16[2,128,2048]{2,1,0:T(8,128)(2,1)}, u32[]{:S(2)}, u32[]{:S(2)}) collective-permute-start(bf16[2,128,2048]{2,1,0:T(8,128)(2,1)} %collective-permute-done.left_x.left_c), channel_id=1, source_target_pairs={{0,8},{8,12},{12,4},{4,0},{1,9},{9,13},{13,5},{5,1},{2,10},{10,14}... | collective-permute-start | bytes 3145736 | tf_op jit(solution)/shard_map/ppermute | solution.py:629
  36.4 13.9 %collective-permute-start.4 = (s16[2,64,1024]{2,1,0:T(8,128)(2,1)}, s16[2,64,1024]{2,1,0:T(8,128)(2,1)}, u32[]{:S(2)}, u32[]{:S(2)}) collective-permute-start(s16[2,64,1024]{2,1,0:T(8,128)(2,1)} %get-tuple-element.84), channel_id=1, source_target_pairs={{0,2},{1,3},{2,0},{3,1},{4,6},{5,7},{6,4},{7,5},{8,10},{9,11},{10,... | collective-permute-start | bytes 786440 | tf_op jit(solution)/shard_map/ppermute | solution.py:619
  37.6 12.6 %collective-permute-start.3 = (s16[2,64,1024]{2,1,0:T(8,128)(2,1)}, s16[2,64,1024]{2,1,0:T(8,128)(2,1)}, u32[]{:S(2)}, u32[]{:S(2)}) collective-permute-start(s16[2,64,1024]{2,1,0:T(8,128)(2,1)} %get-tuple-element.79), channel_id=1, source_target_pairs={{0,1},{1,0},{2,3},{3,2},{4,5},{5,4},{6,7},{7,6},{8,9},{9,8},{10,11... | collective-permute-start | bytes 786440 | tf_op jit(solution)/shard_map/ppermute | solution.py:619
  46.3 16.3 %collective-permute-start.6 = (s16[2,2,64,1024]{3,2,1,0:T(8,128)(2,1)}, s16[2,2,64,1024]{3,2,1,0:T(8,128)(2,1)}, u32[]{:S(2)}, u32[]{:S(2)}) collective-permute-start(s16[2,2,64,1024]{3,2,1,0:T(8,128)(2,1)} %get-tuple-element.92), channel_id=1, source_target_pairs={{0,2},{1,3},{2,0},{3,1},{4,6},{5,7},{6,4},{7,5},{8,10},{9,11},{10,... | collective-permute-start | bytes 1572872 | tf_op jit(solution)/shard_map/ppermute | solution.py:619
  47.4 15.3 %collective-permute-start.7 = (s16[2,2,64,1024]{3,2,1,0:T(8,128)(2,1)}, s16[2,2,64,1024]{3,2,1,0:T(8,128)(2,1)}, u32[]{:S(2)}, u32[]{:S(2)}) collective-permute-start(s16[2,2,64,1024]{3,2,1,0:T(8,128)(2,1)} %get-tuple-element.93), channel_id=1, source_target_pairs={{0,1},{1,0},{2,3},{3,2},{4,5},{5,4},{6,7},{7,6},{8,9},{9,8},{10,11... | collective-permute-start | bytes 1572872 | tf_op jit(solution)/shard_map/ppermute | solution.py:619
  54.0 18.8 %collective-permute-start.11 = (bf16[2,128,1024]{2,1,0:T(8,128)(2,1)}, bf16[2,128,1024]{2,1,0:T(8,128)(2,1)}, u32[]{:S(2)}, u32[]{:S(2)}) collective-permute-start(bf16[2,128,1024]{2,1,0:T(8,128)(2,1)} %spiking_and_surrogate.4.refs_2_), channel_id=1, source_target_pairs={{0,2},{1,3},{2,0},{3,1},{4,6},{5,7},{6,4},{7,5},{8,10},{9,11},{10,... | collective-permute-start | bytes 1572872 | tf_op jit(solution)/shard_map/ppermute | solution.py:619
  54.6 20.5 %collective-permute-start.10 = (bf16[2,128,1024]{2,1,0:T(8,128)(2,1)}, bf16[2,128,1024]{2,1,0:T(8,128)(2,1)}, u32[]{:S(2)}, u32[]{:S(2)}) collective-permute-start(bf16[2,128,1024]{2,1,0:T(8,128)(2,1)} %spiking_and_surrogate.4.refs_2_), channel_id=1, source_target_pairs={{0,1},{1,0},{2,3},{3,2},{4,5},{5,4},{6,7},{7,6},{8,9},{9,8},{10,11... | collective-permute-start | bytes 1572872 | tf_op jit(solution)/shard_map/ppermute | solution.py:619
  65.8 11.9 %collective-permute-start.9 = (s16[2,64,1024]{2,1,0:T(8,128)(2,1)}, s16[2,64,1024]{2,1,0:T(8,128)(2,1)}, u32[]{:S(2)}, u32[]{:S(2)}) collective-permute-start(s16[2,64,1024]{2,1,0:T(8,128)(2,1)} %get-tuple-element.96), channel_id=1, source_target_pairs={{0,2},{1,3},{2,0},{3,1},{4,6},{5,7},{6,4},{7,5},{8,10},{9,11},{10,... | collective-permute-start | bytes 786440 | tf_op jit(solution)/shard_map/ppermute | solution.py:619
  66.8 46.0 %collective-permute-start.14 = (bf16[2,128,2048]{2,1,0:T(8,128)(2,1)}, bf16[2,128,2048]{2,1,0:T(8,128)(2,1)}, u32[]{:S(2)}, u32[]{:S(2)}) collective-permute-start(bf16[2,128,2048]{2,1,0:T(8,128)(2,1)} %collective-permute-done.5.left_x.left_c), channel_id=1, source_target_pairs={{0,8},{8,12},{12,4},{4,0},{1,9},{9,13},{13,5},{5,1},{2,10},{10,14}... | collective-permute-start | bytes 3145736 | tf_op jit(solution)/shard_map/ppermute | solution.py:629
  70.7 9.6 %collective-permute-start.8 = (s16[2,64,1024]{2,1,0:T(8,128)(2,1)}, s16[2,64,1024]{2,1,0:T(8,128)(2,1)}, u32[]{:S(2)}, u32[]{:S(2)}) collective-permute-start(s16[2,64,1024]{2,1,0:T(8,128)(2,1)} %get-tuple-element.94), channel_id=1, source_target_pairs={{0,1},{1,0},{2,3},{3,2},{4,5},{5,4},{6,7},{7,6},{8,9},{9,8},{10,11... | collective-permute-start | bytes 786440 | tf_op jit(solution)/shard_map/ppermute | solution.py:619
  74.4 11.5 %collective-permute-start.12 = (bf16[2,64,1024]{2,1,0:T(8,128)(2,1)}, bf16[2,64,1024]{2,1,0:T(8,128)(2,1)}, u32[]{:S(2)}, u32[]{:S(2)}) collective-permute-start(bf16[2,64,1024]{2,1,0:T(8,128)(2,1)} %slice.48), channel_id=1, source_target_pairs={{0,1},{1,0},{2,3},{3,2},{4,5},{5,4},{6,7},{7,6},{8,9},{9,8},{10,11... | collective-permute-start | bytes 786440 | tf_op jit(solution)/shard_map/ppermute | solution.py:619
  76.8 9.7 %collective-permute-start.13 = (bf16[2,64,1024]{2,1,0:T(8,128)(2,1)}, bf16[2,64,1024]{2,1,0:T(8,128)(2,1)}, u32[]{:S(2)}, u32[]{:S(2)}) collective-permute-start(bf16[2,64,1024]{2,1,0:T(8,128)(2,1)} %slice.49), channel_id=1, source_target_pairs={{0,2},{1,3},{2,0},{3,1},{4,6},{5,7},{6,4},{7,5},{8,10},{9,11},{10,... | collective-permute-start | bytes 786440 | tf_op jit(solution)/shard_map/ppermute | solution.py:619
  77.7 19.9 %collective-permute-start.15 = (s16[2,2,64,1024]{3,2,1,0:T(8,128)(2,1)}, s16[2,2,64,1024]{3,2,1,0:T(8,128)(2,1)}, u32[]{:S(2)}, u32[]{:S(2)}) collective-permute-start(s16[2,2,64,1024]{3,2,1,0:T(8,128)(2,1)} %get-tuple-element.103), channel_id=1, source_target_pairs={{0,2},{1,3},{2,0},{3,1},{4,6},{5,7},{6,4},{7,5},{8,10},{9,11},{10,... | collective-permute-start | bytes 1572872 | tf_op jit(solution)/shard_map/ppermute | solution.py:619
  80.3 17.3 %collective-permute-start.16 = (s16[2,2,64,1024]{3,2,1,0:T(8,128)(2,1)}, s16[2,2,64,1024]{3,2,1,0:T(8,128)(2,1)}, u32[]{:S(2)}, u32[]{:S(2)}) collective-permute-start(s16[2,2,64,1024]{3,2,1,0:T(8,128)(2,1)} %get-tuple-element.104), channel_id=1, source_target_pairs={{0,1},{1,0},{2,3},{3,2},{4,5},{5,4},{6,7},{7,6},{8,9},{9,8},{10,11... | collective-permute-start | bytes 1572872 | tf_op jit(solution)/shard_map/ppermute | solution.py:619
  85.9 21.7 %collective-permute-start.20 = (bf16[2,128,1024]{2,1,0:T(8,128)(2,1)}, bf16[2,128,1024]{2,1,0:T(8,128)(2,1)}, u32[]{:S(2)}, u32[]{:S(2)}) collective-permute-start(bf16[2,128,1024]{2,1,0:T(8,128)(2,1)} %spiking_and_surrogate.5.refs_2_), channel_id=1, source_target_pairs={{0,2},{1,3},{2,0},{3,1},{4,6},{5,7},{6,4},{7,5},{8,10},{9,11},{10,... | collective-permute-start | bytes 1572872 | tf_op jit(solution)/shard_map/ppermute | solution.py:619
  86.4 22.9 %collective-permute-start.19 = (bf16[2,128,1024]{2,1,0:T(8,128)(2,1)}, bf16[2,128,1024]{2,1,0:T(8,128)(2,1)}, u32[]{:S(2)}, u32[]{:S(2)}) collective-permute-start(bf16[2,128,1024]{2,1,0:T(8,128)(2,1)} %spiking_and_surrogate.5.refs_2_), channel_id=1, source_target_pairs={{0,1},{1,0},{2,3},{3,2},{4,5},{5,4},{6,7},{7,6},{8,9},{9,8},{10,11... | collective-permute-start | bytes 1572872 | tf_op jit(solution)/shard_map/ppermute | solution.py:619
  100.6 19.4 %collective-permute-start.18 = (s16[2,64,1024]{2,1,0:T(8,128)(2,1)}, s16[2,64,1024]{2,1,0:T(8,128)(2,1)}, u32[]{:S(2)}, u32[]{:S(2)}) collective-permute-start(s16[2,64,1024]{2,1,0:T(8,128)(2,1)} %get-tuple-element.110), channel_id=1, source_target_pairs={{0,2},{1,3},{2,0},{3,1},{4,6},{5,7},{6,4},{7,5},{8,10},{9,11},{10,... | collective-permute-start | bytes 786440 | tf_op jit(solution)/shard_map/ppermute | solution.py:619
  101.5 18.5 %collective-permute-start.17 = (s16[2,64,1024]{2,1,0:T(8,128)(2,1)}, s16[2,64,1024]{2,1,0:T(8,128)(2,1)}, u32[]{:S(2)}, u32[]{:S(2)}) collective-permute-start(s16[2,64,1024]{2,1,0:T(8,128)(2,1)} %get-tuple-element.105), channel_id=1, source_target_pairs={{0,1},{1,0},{2,3},{3,2},{4,5},{5,4},{6,7},{7,6},{8,9},{9,8},{10,11... | collective-permute-start | bytes 786440 | tf_op jit(solution)/shard_map/ppermute | solution.py:619
  109.3 14.5 %collective-permute-start.21 = (bf16[2,64,1024]{2,1,0:T(8,128)(2,1)}, bf16[2,64,1024]{2,1,0:T(8,128)(2,1)}, u32[]{:S(2)}, u32[]{:S(2)}) collective-permute-start(bf16[2,64,1024]{2,1,0:T(8,128)(2,1)} %slice.50), channel_id=1, source_target_pairs={{0,1},{1,0},{2,3},{3,2},{4,5},{5,4},{6,7},{7,6},{8,9},{9,8},{10,11... | collective-permute-start | bytes 786440 | tf_op jit(solution)/shard_map/ppermute | solution.py:619
  111.0 12.8 %collective-permute-start.22 = (bf16[2,64,1024]{2,1,0:T(8,128)(2,1)}, bf16[2,64,1024]{2,1,0:T(8,128)(2,1)}, u32[]{:S(2)}, u32[]{:S(2)}) collective-permute-start(bf16[2,64,1024]{2,1,0:T(8,128)(2,1)} %slice.51), channel_id=1, source_target_pairs={{0,2},{1,3},{2,0},{3,1},{4,6},{5,7},{6,4},{7,5},{8,10},{9,11},{10,... | collective-permute-start | bytes 786440 | tf_op jit(solution)/shard_map/ppermute | solution.py:619
  130.5 26.7 %collective-permute-start.29 = (bf16[2,128,2048]{2,1,0:T(8,128)(2,1)}, bf16[2,128,2048]{2,1,0:T(8,128)(2,1)}, u32[]{:S(2)}, u32[]{:S(2)}) collective-permute-start(bf16[2,128,2048]{2,1,0:T(8,128)(2,1)} %get-tuple-element.114), channel_id=1, source_target_pairs={{0,8},{8,12},{12,4},{4,0},{1,9},{9,13},{13,5},{5,1},{2,10},{10,14}... | collective-permute-start | bytes 3145736 | tf_op jit(solution)/shard_map/ppermute | solution.py:629
  131.7 15.1 %collective-permute-start.26 = (bf16[2,128,1024]{2,1,0:T(8,128)(2,1)}, bf16[2,128,1024]{2,1,0:T(8,128)(2,1)S(1)}, u32[]{:S(2)}, u32[]{:S(2)}) collective-permute-start(bf16[2,128,1024]{2,1,0:T(8,128)(2,1)} %spiking_and_surrogate.6.refs_2_), channel_id=1, source_target_pairs={{0,2},{1,3},{2,0},{3,1},{4,6},{5,7},{6,4},{7,5},{8,10},{9,11},{10,... | collective-permute-start | bytes 1572872 | tf_op jit(solution)/shard_map/ppermute | solution.py:619
  133.4 15.5 %collective-permute-start.25 = (bf16[2,128,1024]{2,1,0:T(8,128)(2,1)}, bf16[2,128,1024]{2,1,0:T(8,128)(2,1)S(1)}, u32[]{:S(2)}, u32[]{:S(2)}) collective-permute-start(bf16[2,128,1024]{2,1,0:T(8,128)(2,1)} %spiking_and_surrogate.6.refs_2_), channel_id=1, source_target_pairs={{0,1},{1,0},{2,3},{3,2},{4,5},{5,4},{6,7},{7,6},{8,9},{9,8},{10,11... | collective-permute-start | bytes 1572872 | tf_op jit(solution)/shard_map/ppermute | solution.py:619
  135.4 17.1 %collective-permute-start.23 = (s16[2,2,64,1024]{3,2,1,0:T(8,128)(2,1)}, s16[2,2,64,1024]{3,2,1,0:T(8,128)(2,1)}, u32[]{:S(2)}, u32[]{:S(2)}) collective-permute-start(s16[2,2,64,1024]{3,2,1,0:T(8,128)(2,1)} %get-tuple-element.117), channel_id=1, source_target_pairs={{0,2},{1,3},{2,0},{3,1},{4,6},{5,7},{6,4},{7,5},{8,10},{9,11},{10,... | collective-permute-start | bytes 1572872 | tf_op jit(solution)/shard_map/ppermute | solution.py:619
  135.5 18.2 %collective-permute-start.24 = (s16[2,2,64,1024]{3,2,1,0:T(8,128)(2,1)}, s16[2,2,64,1024]{3,2,1,0:T(8,128)(2,1)}, u32[]{:S(2)}, u32[]{:S(2)}) collective-permute-start(s16[2,2,64,1024]{3,2,1,0:T(8,128)(2,1)} %get-tuple-element.118), channel_id=1, source_target_pairs={{0,1},{1,0},{2,3},{3,2},{4,5},{5,4},{6,7},{7,6},{8,9},{9,8},{10,11... | collective-permute-start | bytes 1572872 | tf_op jit(solution)/shard_map/ppermute | solution.py:619
  146.8 0.9 copy-start
  148.4 8.4 %collective-permute-start.27 = (bf16[2,64,1024]{2,1,0:T(8,128)(2,1)}, bf16[2,64,1024]{2,1,0:T(8,128)(2,1)}, u32[]{:S(2)}, u32[]{:S(2)}) collective-permute-start(bf16[2,64,1024]{2,1,0:T(8,128)(2,1)} %slice.52), channel_id=1, source_target_pairs={{0,1},{1,0},{2,3},{3,2},{4,5},{5,4},{6,7},{7,6},{8,9},{9,8},{10,11... | collective-permute-start | bytes 786440 | tf_op jit(solution)/shard_map/ppermute | solution.py:619
  148.9 0.8 copy-start.1
  150.5 6.7 %collective-permute-start.28 = (bf16[2,64,1024]{2,1,0:T(8,128)(2,1)}, bf16[2,64,1024]{2,1,0:T(8,128)(2,1)}, u32[]{:S(2)}, u32[]{:S(2)}) collective-permute-start(bf16[2,64,1024]{2,1,0:T(8,128)(2,1)} %slice.53), channel_id=1, source_target_pairs={{0,2},{1,3},{2,0},{3,1},{4,6},{5,7},{6,4},{7,5},{8,10},{9,11},{10,... | collective-permute-start | bytes 786440 | tf_op jit(solution)/shard_map/ppermute | solution.py:619
  164.1 50.8 %collective-permute-start.37 = (bf16[2,4,384,1024]{3,2,1,0:T(8,128)(2,1)}, bf16[2,4,384,1024]{3,2,1,0:T(8,128)(2,1)}, u32[]{:S(2)}, u32[]{:S(2)}) collective-permute-start(bf16[2,4,384,1024]{3,2,1,0:T(8,128)(2,1)} %get-tuple-element.122.refs_2_), channel_id=1, source_target_pairs={{0,16},{16,0},{1,17},{17,1},{2,18},{18,2},{3,19},{19,3},{4,20},{20... | collective-permute-start | bytes 18874376 | tf_op jit(solution)/shard_map/ppermute | solution.py:623
  164.2 49.5 %collective-permute-start.39 = (bf16[2,2048,512]{2,1,0:T(8,128)(2,1)}, bf16[2,2048,512]{2,1,0:T(8,128)(2,1)}, u32[]{:S(2)}, u32[]{:S(2)}) collective-permute-start(bf16[2,2048,512]{2,1,0:T(8,128)(2,1)} %get-tuple-element.132.refs_6_), channel_id=1, source_target_pairs={{0,16},{16,0},{1,17},{17,1},{2,18},{18,2},{3,19},{19,3},{4,20},{20... | collective-permute-start | bytes 12582920 | tf_op jit(solution)/shard_map/ppermute | solution.py:623
  164.7 8.6 %collective-permute-start.31 = (s16[2,64,1024]{2,1,0:T(8,128)(2,1)}, s16[2,64,1024]{2,1,0:T(8,128)(2,1)}, u32[]{:S(2)}, u32[]{:S(2)}) collective-permute-start(s16[2,64,1024]{2,1,0:T(8,128)(2,1)} %get-tuple-element.125), channel_id=1, source_target_pairs={{0,2},{1,3},{2,0},{3,1},{4,6},{5,7},{6,4},{7,5},{8,10},{9,11},{10,... | collective-permute-start | bytes 786440 | tf_op jit(solution)/shard_map/ppermute | solution.py:619
  166.4 9.0 %collective-permute-start.30 = (s16[2,64,1024]{2,1,0:T(8,128)(2,1)}, s16[2,64,1024]{2,1,0:T(8,128)(2,1)}, u32[]{:S(2)}, u32[]{:S(2)}) collective-permute-start(s16[2,64,1024]{2,1,0:T(8,128)(2,1)} %get-tuple-element.119), channel_id=1, source_target_pairs={{0,1},{1,0},{2,3},{3,2},{4,5},{5,4},{6,7},{7,6},{8,9},{9,8},{10,11... | collective-permute-start | bytes 786440 | tf_op jit(solution)/shard_map/ppermute | solution.py:619
  168.9 34.5 %collective-permute-start.36 = (bf16[2,128,2048]{2,1,0:T(8,128)(2,1)}, bf16[2,128,2048]{2,1,0:T(8,128)(2,1)}, u32[]{:S(2)}, u32[]{:S(2)}) collective-permute-start(bf16[2,128,2048]{2,1,0:T(8,128)(2,1)} %get-tuple-element.123), channel_id=1, source_target_pairs={{0,8},{8,12},{12,4},{4,0},{1,9},{9,13},{13,5},{5,1},{2,10},{10,14}... | collective-permute-start | bytes 3145736 | tf_op jit(solution)/shard_map/ppermute | solution.py:629
  179.2 13.9 %collective-permute-start.33 = (bf16[2,128,1024]{2,1,0:T(8,128)(2,1)}, bf16[2,128,1024]{2,1,0:T(8,128)(2,1)}, u32[]{:S(2)}, u32[]{:S(2)}) collective-permute-start(bf16[2,128,1024]{2,1,0:T(8,128)(2,1)} %spiking_and_surrogate.7.refs_2_), channel_id=1, source_target_pairs={{0,2},{1,3},{2,0},{3,1},{4,6},{5,7},{6,4},{7,5},{8,10},{9,11},{10,... | collective-permute-start | bytes 1572872 | tf_op jit(solution)/shard_map/ppermute | solution.py:619
  179.5 13.6 %collective-permute-start.32 = (bf16[2,128,1024]{2,1,0:T(8,128)(2,1)}, bf16[2,128,1024]{2,1,0:T(8,128)(2,1)}, u32[]{:S(2)}, u32[]{:S(2)}) collective-permute-start(bf16[2,128,1024]{2,1,0:T(8,128)(2,1)} %spiking_and_surrogate.7.refs_2_), channel_id=1, source_target_pairs={{0,1},{1,0},{2,3},{3,2},{4,5},{5,4},{6,7},{7,6},{8,9},{9,8},{10,11... | collective-permute-start | bytes 1572872 | tf_op jit(solution)/shard_map/ppermute | solution.py:619
  195.0 7.0 %collective-permute-start.34 = (bf16[2,64,1024]{2,1,0:T(8,128)(2,1)S(1)}, bf16[2,64,1024]{2,1,0:T(8,128)(2,1)S(1)}, u32[]{:S(2)}, u32[]{:S(2)}) collective-permute-start(bf16[2,64,1024]{2,1,0:T(8,128)(2,1)S(1)} %slice.42), channel_id=1, source_target_pairs={{0,1},{1,0},{2,3},{3,2},{4,5},{5,4},{6,7},{7,6},{8,9},{9,8},{10,11... | collective-permute-start | bytes 786440 | tf_op jit(solution)/shard_map/ppermute | solution.py:619
  196.3 6.4 %collective-permute-start.35 = (bf16[2,64,1024]{2,1,0:T(8,128)(2,1)S(1)}, bf16[2,64,1024]{2,1,0:T(8,128)(2,1)S(1)}, u32[]{:S(2)}, u32[]{:S(2)}) collective-permute-start(bf16[2,64,1024]{2,1,0:T(8,128)(2,1)S(1)} %slice.43), channel_id=1, source_target_pairs={{0,2},{1,3},{2,0},{3,1},{4,6},{5,7},{6,4},{7,5},{8,10},{9,11},{10,... | collective-permute-start | bytes 786440 | tf_op jit(solution)/shard_map/ppermute | solution.py:619
  202.0 0.7 copy-start.2
  202.7 0.7 copy-start.3
  210.3 4.6 %collective-permute-start.38 = (bf16[2,4,128,1024]{3,2,1,0:T(8,128)(2,1)}, bf16[2,4,128,1024]{3,2,1,0:T(8,128)(2,1)}, u32[]{:S(2)}, u32[]{:S(2)}) collective-permute-start(bf16[2,4,128,1024]{3,2,1,0:T(8,128)(2,1)} %get-tuple-element.131.refs_3_), channel_id=1, source_target_pairs={{0,16},{16,0},{1,17},{17,1},{2,18},{18,2},{3,19},{19,3},{4,20},{20... | collective-permute-start | bytes 6291464 | tf_op jit(solution)/shard_map/ppermute | solution.py:623
  210.4 26.6 %collective-permute-start.40 = (bf16[2,128,2048]{2,1,0:T(8,128)(2,1)}, bf16[2,128,2048]{2,1,0:T(8,128)(2,1)}, u32[]{:S(2)}, u32[]{:S(2)}) collective-permute-start(bf16[2,128,2048]{2,1,0:T(8,128)(2,1)} %get-tuple-element.136), channel_id=1, source_target_pairs={{0,8},{8,12},{12,4},{4,0},{1,9},{9,13},{13,5},{5,1},{2,10},{10,14}... | collective-permute-start | bytes 3145736 | tf_op jit(solution)/shard_map/ppermute | solution.py:629
